TPU v7x, 256 devices: a whole 4x4x8 slice. The times are simulated.
256 devices in a mesh: rows: 32 (over z, x), width: 8 (over y, core).
Axes of the slice: x: 4, y: 4, z: 8, core: 2. Of those that a mesh axis runs over, the one named last changes fastest.
Arguments:
- slab: bfloat16 [262144, 5120], P('rows', 'width'), may hold values from -200 to 200
- basis: bfloat16 [5120, 256], P('width'), may hold values from -3 to 3
Outputs:
- projected: float32 [5120, 256], P('width', 'rows')
- triangle: float32 [256, 256], replicated
All inputs are finite; a program needn't handle non-finite values.
Results may differ from a plain program's by a relative error of at most 0.00047.
Values may be sent and summed in bfloat16 or wider, within the bound.
No kernel may reach another device: no remote copies, remote signals or barrier semaphores. Data moves between devices by JAX's collectives and lax.ppermute only.
A program may use at most 128 MiB of HBM per device.

v0:
```python
import jax
import jax.numpy as jnp
from jax import lax
from jax.sharding import PartitionSpec as P


def gram_of(left):
    return jnp.einsum("rk,rj->kj", left, left, precision=lax.Precision.HIGHEST)


def factor_with(sketch, gram):
    lower = jnp.linalg.cholesky(gram)
    ortho = lax.linalg.triangular_solve(
        lower, sketch, left_side=False, lower=True, transpose_a=True
    )
    return (ortho, lower.T)


def shards(slab, basis):
    row_count = slab.shape[0]
    total_rows = row_count * lax.axis_size("rows")
    partial_sketch = jnp.dot(slab, basis, preferred_element_type=jnp.float32)
    sketch = lax.psum(partial_sketch, "width")
    gram = lax.psum(gram_of(sketch), "rows")
    ortho, factor = factor_with(sketch, gram)
    ortho_half = ortho.astype(jnp.bfloat16)
    partial_value = lax.dot_general(
        slab, ortho_half, (((0,), (0,)), ((), ())), preferred_element_type=jnp.float32
    )
    projected = lax.psum_scatter(partial_value, "rows", scatter_dimension=1, tiled=True)
    triangle = factor / jnp.sqrt(jnp.float32(total_rows))
    return (projected, triangle)


def solution(mesh):
    return jax.shard_map(
        shards,
        mesh=mesh,
        in_specs=(P("rows", "width"), P("width", None)),
        out_specs=(P("width", "rows"), P()),
        check_vma=False,
    )
```

profile of v0, /device:TPU:24, one launch (start us, length us, event | category | flops | bytes accessed | tf_op | source)
XLA Modules:
  0.0 531.0 jit_solution(16851322161751141027)
XLA Ops:
  7.2 0.9 copy-done
  8.1 10.6 %fusion.18 = f32[8192,256]{1,0:T(8,128)} fusion(bf16[8192,640]{1,0:T(8,128)(2,1)} %param.2, bf16[640,256]{1,0:T(8,128)(2,1)S(1)} %copy-done), kind=kOutput, calls=%fused_computation.38 | convolution fusion | flops 2684354560 | bytes 19202048 | tf_op jit(solution)/shard_map/dot_general | solution.py:22
  18.9 110.0 %all-reduce.6.cloned.1.call-done = f32[8192,256]{1,0:T(8,128)} async-done(((f32[8192,256]{1,0:T(8,128)}), f32[8192,256]{1,0:T(8,128)}) %all-reduce.6.cloned.1.call-update) | async-done | bytes 8388624 | tf_op jit(solution)/shard_map/psum | solution.py:23
  128.9 19.7 %fusion.19 = f32[256,256]{0,1:T(8,128)} fusion(f32[8192,256]{1,0:T(8,128)} %all-reduce.6.cloned.1.call-done), kind=kOutput, calls=%fused_computation.39 | convolution fusion | flops 6442450944 | bytes 8650752 | tf_op jit(solution)/shard_map/rk,rj->kj/dot_general | solution.py:8
  149.1 145.4 %all-reduce.8.cloned.1.call-done = f32[256,256]{0,1:T(8,128)} async-done(((f32[256,256]{0,1:T(8,128)}), f32[256,256]{0,1:T(8,128)}) %all-reduce.8.cloned.1.call-update) | async-done | bytes 262160 | tf_op jit(solution)/shard_map/psum | solution.py:24
  294.5 1.1 copy.8
  295.6 1.0 fusion.9
  296.6 11.7 %cholesky.50 = f32[128,128]{1,0:T(8,128)S(1)} custom-call(f32[128,128]{1,0:T(8,128)S(1)} %cholesky.118), custom_call_target="Cholesky" | custom-call | tf_op jit(solution)/shard_map/jit(cholesky)/cholesky | solution.py:12
  308.3 9.8 %custom-call.14 = f32[1,128,128]{1,2,0:T(8,128)S(1)} custom-call(f32[1,128,128]{2,1,0:T(8,128)S(1)} %get-tuple-element.29), custom_call_target="InvertDiagBlocksLowerTriangular" | custom-call | tf_op jit(solution)/shard_map/jit(cholesky)/cholesky | solution.py:12
  318.7 11.7 %cholesky.105 = f32[128,128]{1,0:T(8,128)S(1)} custom-call(f32[128,128]{1,0:T(8,128)S(1)} %convolution_subtract_fusion.1), custom_call_target="Cholesky" | custom-call | tf_op jit(solution)/shard_map/jit(cholesky)/cholesky | solution.py:12
  330.4 0.7 compare_reduce_fusion
  332.5 4.1 while.1
  332.7 0.6 fusion.30
  333.3 1.4 bitcast_dynamic-update-slice_fusion.2
  335.2 1.4 bitcast_dynamic-update-slice_fusion.2
  336.6 19.7 %custom-call.15 = f32[2,128,128]{1,2,0:T(8,128)S(1)} custom-call(f32[2,128,128]{2,1,0:T(8,128)S(1)} %get-tuple-element.9), custom_call_target="InvertDiagBlocksLowerTriangular" | custom-call | tf_op jit(solution)/shard_map/triangular_solve | solution.py:13
  356.3 5.8 %fusion.17 = (bf16[8192,128]{0,1:T(8,128)(2,1)S(1)}, f32[8192,128]{0,1:T(8,128)S(1)}) fusion(f32[2,128,128]{1,2,0:T(8,128)S(1)} %custom-call.15, f32[8192,256]{1,0:T(8,128)} %all-reduce.6.cloned.1.call-done), kind=kOutput, calls=%fused_computation.37 | convolution fusion | flops 1611661312 | bytes 10551296 | tf_op jit(solution)/shard_map/triangular_solve | solution.py:13
  362.1 6.7 %convolution_subtract_fusion = f32[8192,128]{1,0:T(8,128)S(1)} fusion(f32[8192,128]{0,1:T(8,128)S(1)} %get-tuple-element.33, f32[8192,256]{1,0:T(8,128)S(1)} %copy-done.1, f32[256,256]{1,0:T(8,128)S(1)} %get-tuple-element.86), kind=kOutput, calls=%fused_computation.2 | convolution fusion | flops 1611661312 | bytes 12648448 | tf_op jit(solution)/shard_map/triangular_solve | solution.py:13
  368.9 4.3 convolution_convert_fusion
  373.2 4.3 fusion.6
  377.5 0.6 dynamic-slice.3
  378.8 0.8 copy.9
  379.6 143.3 %all-reduce.10.cloned.1.call-done = f32[640,256]{0,1:T(8,128)} async-done(((f32[640,256]{0,1:T(8,128)}), f32[640,256]{0,1:T(8,128)}) %all-reduce.10.cloned.1.call-update) | async-done | bytes 655376
  522.9 1.3 constant_dynamic-slice_fusion.1
  (31 shorter events, 2.0 us)
Async XLA Ops:
  7.2 1.0 copy-start
  7.2 121.7 %all-reduce.6.cloned.1.call-start = ((), (), s32[]{:S(2)}) async-start(), calls=%async_computation | async-start | bytes 16777216 | tf_op jit(solution)/shard_map/psum | solution.py:23
  18.8 275.7 %all-reduce.8.cloned.1.call-start = ((), (), s32[]{:S(2)}) async-start(), calls=%async_computation.1 | async-start | bytes 524288 | tf_op jit(solution)/shard_map/psum | solution.py:24
  148.6 374.3 %all-reduce.10.cloned.1.call-start = ((), (), s32[]{:S(2)}) async-start(), calls=%async_computation.2 | async-start | bytes 1310720
  356.3 5.8 %copy-start.1 = (f32[8192,256]{1,0:T(8,128)S(1)}, f32[8192,256]{1,0:T(8,128)}, u32[]{:S(2)}) copy-start(f32[8192,256]{1,0:T(8,128)} %all-reduce.6.cloned.1.call-done) | copy-start | bytes 25165828
  356.3 16.9 %slice-start = ((s8[10485760]{0:T(1024)(128)(4,1)}), s8[4194304]{0:T(1024)(128)(4,1)S(1)}, s32[]{:S(2)}) async-start(s8[10485760]{0:T(1024)(128)(4,1)} %bitcast.43), calls=%async_computation.3 | async-start | bytes 8388608
  356.3 16.9 %slice-start.1 = ((s8[10485760]{0:T(1024)(128)(4,1)}), s8[4194304]{0:T(1024)(128)(4,1)S(1)}, s32[]{:S(2)}) async-start(s8[10485760]{0:T(1024)(128)(4,1)} %bitcast.43), calls=%async_computation.4 | async-start | bytes 8388608
  362.1 11.1 %slice-start.2 = ((s8[10485760]{0:T(1024)(128)(4,1)}), s8[2097152]{0:T(1024)(128)(4,1)S(1)}, s32[]{:S(2)}) async-start(s8[10485760]{0:T(1024)(128)(4,1)} %bitcast.43), calls=%async_computation.5 | async-start | bytes 4194304
  373.2 4.3 copy-start.2
Sparse Core Ops, SparseCore 0:
  18.9 109.9 all-reduce.5
  148.7 145.7 all-reduce.7
  377.6 145.2 all-reduce.9
where the time goes:
time: 539 us; the launch traced here: 531 us
  waiting for transfers between devices  399 us (74%)
  other arithmetic  54.7 us (10%)
  matrix products  51.9 us (10%)
  between operations  16.1 us (3%)
  local copies, waits for them, and re-layouts  8.79 us (2%)
    psum x1, waiting for transfers between devices, shards(): gram = lax.psum(gram_of(sketch), 'rows')  145 us
    unnamed x4, waiting for transfers between devices  143 us
    psum x1, waiting for transfers between devices, shards(): sketch = lax.psum(partial_sketch, 'width')  110 us
    another operation x6, other arithmetic, factor_with(): lower = jnp.linalg.cholesky(gram)  34 us
    dot_general x1, matrix products, gram_of(): return jnp.einsum('rk,rj->kj', left, left, precision=lax.Precision.HIGHEST)  19.7 us
    another operation x2, other arithmetic, factor_with(): lax.linalg.triangular_solve(lower, sketch, left_side=False, lower=True, t...  19.7 us
    another operation x3, matrix products, factor_with(): lax.linalg.triangular_solve(lower, sketch, left_side=False, lower=True, t...  16.8 us
  transfers between devices with their start and end apart: 3, of which 3 were waited for; matrix products, arithmetic and copies ran while one was open for 0% of the time, Pallas kernels for 0%

commit v1 on v0

v1 whole, which is shorter than its diff:
```python
import functools
import jax
import jax.numpy as jnp
from jax import lax
from jax.experimental import pallas as pl
from jax.experimental.pallas import tpu as pltpu
from jax.sharding import PartitionSpec as P

f32 = jnp.float32
HI = lax.Precision.HIGHEST


def factor_diagonal(block, b, g=8):
    lane = lax.broadcasted_iota(jnp.int32, (b, 128), 1)
    row = lax.broadcasted_iota(jnp.int32, (b, 128), 0)
    a = jnp.concatenate([block, jnp.zeros((b, 128 - b), f32)], axis=1)
    a = jnp.where(lane == row + b, 1.0, a)
    sub = lax.broadcasted_iota(jnp.int32, (8, 128), 0)
    done = []
    for s in range(0, b, g):
        top, rest = a[0:g, :], a[g:, :]
        tiles = (b - s - g) // 8
        rows = [jnp.broadcast_to(top[k : k + 1, :], (8, 128)) for k in range(g)]
        u = {
            (k, m): jnp.broadcast_to(top[k : k + 1, s + m : s + m + 1], (8, 128))
            for k in range(g)
            for m in range(k, g)
        }
        cols = [
            [
                jnp.broadcast_to(rest[8 * t : 8 * t + 8, s + k : s + k + 1], (8, 128))
                for t in range(tiles)
            ]
            for k in range(g)
        ]
        for k in range(g):
            scale = lax.rsqrt(u[k, k])
            rows[k] = rows[k] * scale
            cols[k] = [c * scale for c in cols[k]]
            for m in range(k + 1, g):
                u[k, m] = u[k, m] * scale
            for m in range(k + 1, g):
                for q in range(m, g):
                    u[m, q] = u[m, q] - u[k, m] * u[k, q]
                rows[m] = rows[m] - u[k, m] * rows[k]
                cols[m] = [c - u[k, m] * d for c, d in zip(cols[m], cols[k])]
        final = rows[0]
        for k in range(1, g):
            final = jnp.where(sub == k, rows[k], final)
        done.append(final)
        if tiles:
            out = []
            for t in range(tiles):
                v = rest[8 * t : 8 * t + 8, :]
                for k in range(g):
                    v = v - cols[k][t] * rows[k]
                out.append(v)
            a = jnp.concatenate(out, axis=0)
    return jnp.concatenate(done, axis=0)[:, b : 2 * b]


def factor_kernel(b, n, g_ref, r_ref, inv_ref, m_ref):
    m_ref[:, 0:n] = g_ref[...]
    ri = lax.broadcasted_iota(jnp.int32, (n, n), 0)
    ci = lax.broadcasted_iota(jnp.int32, (n, n), 1)
    m_ref[:, n : 2 * n] = jnp.where(ri == ci, 1.0, 0.0)
    for s in range(0, n, b):
        inverse = factor_diagonal(m_ref[s : s + b, s : s + b], b)
        rows = jnp.dot(
            inverse, m_ref[s : s + b, :], precision=HI, preferred_element_type=f32
        )
        rr = lax.broadcasted_iota(jnp.int32, (b, n), 0)
        cc = lax.broadcasted_iota(jnp.int32, (b, n), 1)
        left = jnp.where(cc >= rr + s, rows[:, 0:n], 0.0)
        right = rows[:, n : 2 * n]
        r_ref[s : s + b, :] = left
        inv_ref[s : s + b, :] = right
        if s + b < n:
            update = lax.dot_general(
                left,
                jnp.concatenate([left, right], axis=1),
                (((0,), (0,)), ((), ())),
                precision=HI,
                preferred_element_type=f32,
            )
            m_ref[s + b : n, :] = m_ref[s + b : n, :] - update[s + b : n, :]


def factor_and_inverse(gram, b=64):
    n = gram.shape[0]
    vmem = pl.BlockSpec(memory_space=pltpu.VMEM)
    return pl.pallas_call(
        functools.partial(factor_kernel, b, n),
        out_shape=(jax.ShapeDtypeStruct((n, n), f32),) * 2,
        in_specs=[vmem],
        out_specs=(vmem, vmem),
        scratch_shapes=[pltpu.VMEM((n, 2 * n), f32)],
        cost_estimate=pl.CostEstimate(
            flops=12 * n**3, bytes_accessed=12 * n * n, transcendentals=n
        ),
    )(gram)


def shift_core(x):
    return lax.ppermute(x, "width", [(i, i ^ 1) for i in range(8)])


def shift_y(x, k):
    return lax.ppermute(x, "width", [(i, (i + 2 * k) % 8) for i in range(8)])


def shift_x(x, k):
    return lax.ppermute(
        x, "rows", [(i, i // 4 * 4 + (i % 4 + k) % 4) for i in range(32)]
    )


def shift_z(x, k):
    return lax.ppermute(x, "rows", [(i, (i + 4 * k) % 32) for i in range(32)])


def sum_of_four(x, shift):
    return (x + shift(x, 2)) + (shift(x, 1) + shift(x, -1))


def sum_of_eight(x, shift):
    even = (x + shift(x, 4)) + (shift(x, 2) + shift(x, -2))
    odd = (shift(x, 1) + shift(x, -3)) + (shift(x, 3) + shift(x, -1))
    return even + odd


def sum_everywhere(x):
    core = lax.axis_index("width") % 2
    half = x.shape[0] // 2
    own = lax.dynamic_slice_in_dim(x, core * half, half, 0)
    other = lax.dynamic_slice_in_dim(x, (1 - core) * half, half, 0)
    own = own + shift_core(other)
    own = sum_of_four(own, shift_y)
    own = sum_of_four(own, shift_x)
    own = sum_of_eight(own, shift_z)
    other = shift_core(own)
    first = jnp.where(core == 0, own, other)
    second = jnp.where(core == 0, other, own)
    return jnp.concatenate([first, second], axis=0)


def shards(slab, basis):
    total_rows = slab.shape[0] * lax.axis_size("rows")
    partial_sketch = jnp.dot(slab, basis, preferred_element_type=f32)
    sketch = lax.psum_scatter(partial_sketch, "width", scatter_dimension=0, tiled=True)
    whole = lax.all_gather(sketch.astype(jnp.bfloat16), "width", axis=0, tiled=True)
    gram = lax.dot_general(
        sketch, sketch, (((0,), (0,)), ((), ())), precision=HI, preferred_element_type=f32
    )
    gram = sum_everywhere(gram)
    factor, inverse = factor_and_inverse(gram)
    value = lax.dot_general(
        whole, slab, (((0,), (0,)), ((), ())), preferred_element_type=f32
    )
    value = jnp.dot(inverse, value, precision=HI, preferred_element_type=f32)
    pieces = lax.all_to_all(value, "rows", 0, 0, tiled=True)
    projected = jnp.sum(pieces.reshape(32, 8, -1), axis=0).T
    triangle = factor / jnp.sqrt(f32(total_rows))
    return (projected, triangle)


def solution(mesh):
    return jax.shard_map(
        shards,
        mesh=mesh,
        in_specs=(P("rows", "width"), P("width", None)),
        out_specs=(P("width", "rows"), P()),
        check_vma=False,
    )
```

time: 539 us -> 193 us (0.36); the launches traced: 531 us -> 193 us
  waiting for transfers between devices: 399 us -> 99.3 us
  other arithmetic: 54.7 us -> 4.36 us
  starting transfers between devices: 0.59 us -> 37.4 us
  matrix products: 51.9 us -> 24.3 us
  Pallas kernels: 0 us -> 12.1 us
  local copies, waits for them, and re-layouts: 8.79 us -> 0.95 us
    psum x2 -> x0, waiting for transfers between devices: 255 us -> none  [the longest x1 145 us: shards(): gram = lax.psum(gram_of(sketch), 'rows')]
    unnamed x4 -> x2, waiting for transfers between devices: 143 us -> 0.03 us
    reduce_scatter x0 -> x1, waiting for transfers between devices: none -> 55.9 us  [shards(): lax.psum_scatter(partial_sketch, 'width', scatter_dimension=0, tiled=True)]
    another operation x8 -> x0, other arithmetic: 53.7 us -> none  [the longest x6 34 us: factor_with(): lower = jnp.linalg.cholesky(gram)]
    ppermute x0 -> x15, starting transfers between devices: none -> 27.7 us  [the longest x7 17.9 us: shift_z(): return lax.ppermute(x, 'rows', [(i, (i + 4 * k) % 32) for i in range(32)])]
    ppermute x0 -> x15, waiting for transfers between devices: none -> 23.6 us  [the longest x3 9.28 us: shift_y(): return lax.ppermute(x, 'width', [(i, (i + 2 * k) % 8) for i in range(8)])]
    all_to_all x0 -> x1, waiting for transfers between devices: none -> 19.8 us  [shards(): pieces = lax.all_to_all(value, 'rows', 0, 0, tiled=True)]
    another operation x5 -> x0, matrix products: 17.3 us -> none  [the longest x3 16.8 us: factor_with(): lax.linalg.triangular_solve(lower, sketch, left_side=False, lower=True, t...]
  transfers between devices with their start and end apart: 3 -> 18, of which waited for: 3 -> 13; matrix products, arithmetic and copies ran while one was open for 0% -> 3% of each run, Pallas kernels for 0% -> 6%
where the time goes in v1:
time: 193 us
  waiting for transfers between devices  99.3 us (51%)
  starting transfers between devices  37.4 us (19%)
  matrix products  24.3 us (13%)
  between operations  14.2 us (7%)
  Pallas kernels  12.1 us (6%)
  other arithmetic  4.36 us (2%)
    reduce_scatter x1, waiting for transfers between devices, shards(): lax.psum_scatter(partial_sketch, 'width', scatter_dimension=0, tiled=True)  55.9 us
    all_to_all x1, waiting for transfers between devices, shards(): pieces = lax.all_to_all(value, 'rows', 0, 0, tiled=True)  19.8 us
    ppermute x7, starting transfers between devices, shift_z(): return lax.ppermute(x, 'rows', [(i, (i + 4 * k) % 32) for i in range(32)])  17.9 us
    pallas_call x1, Pallas kernels, factor_and_inverse(): pl.pallas_call(functools.partial(factor_kernel, b, n), out_shape=(jax.Sha...  12.1 us
    dot_general x1, matrix products, shards(): partial_sketch = jnp.dot(slab, basis, preferred_element_type=f32)  10.7 us
    all_to_all x1, starting transfers between devices, shards(): pieces = lax.all_to_all(value, 'rows', 0, 0, tiled=True)  9.63 us
    ppermute x3, waiting for transfers between devices, shift_y(): return lax.ppermute(x, 'width', [(i, (i + 2 * k) % 8) for i in range(8)])  9.28 us
    dot_general x1, matrix products, shards(): lax.dot_general(whole, slab, (((0,), (0,)), ((), ())), preferred_element_...  8.4 us
  transfers between devices with their start and end apart: 18, of which 13 were waited for; matrix products, arithmetic and copies ran while one was open for 3% of the time, Pallas kernels for 6%

profile of v1, /device:TPU:24, one launch (start us, length us, event | category | flops | bytes accessed | tf_op | source)
XLA Modules:
  0.0 192.5 jit_solution(13017246999129928696)
XLA Ops:
  8.1 10.7 %fusion = f32[8192,256]{1,0:T(8,128)} fusion(bf16[8192,640]{1,0:T(8,128)(2,1)} %param.2, bf16[640,256]{1,0:T(8,128)(2,1)S(1)} %copy-done), kind=kOutput, calls=%fused_computation.10 | convolution fusion | flops 2684354560 | bytes 19202048 | tf_op jit(solution)/shard_map/dot_general | solution.py:149
  18.9 55.9 %reduce-scatter.2.cloned.1.call-done = f32[1024,256]{1,0:T(8,128)} async-done(((f32[8192,256]{1,0:T(8,128)}), f32[1024,256]{1,0:T(8,128)}) %reduce-scatter.2.cloned.1.call-update) | async-done | bytes 1048592 | tf_op jit(solution)/shard_map/reduce_scatter | solution.py:150
  74.8 2.1 %convert_element_type.3 = bf16[1024,256]{1,0:T(8,128)(2,1)} convert(f32[1024,256]{1,0:T(8,128)} %reduce-scatter.2.cloned.1.call-done) | non-fusion elementwise | flops 262144 | bytes 1572864 | tf_op jit(solution)/shard_map/convert_element_type | solution.py:151
  76.9 3.5 %fusion.1 = f32[256,256]{1,0:T(8,128)S(1)} fusion(f32[1024,256]{1,0:T(8,128)} %reduce-scatter.2.cloned.1.call-done), kind=kOutput, calls=%fused_computation.11 | convolution fusion | flops 805306368 | bytes 1310720 | tf_op jit(solution)/shard_map/dot_general | solution.py:152
  81.9 2.5 %collective-permute-start.2 = (f32[128,256]{1,0:T(8,128)S(1)}, f32[128,256]{1,0:T(8,128)S(1)}, u32[]{:S(2)}, u32[]{:S(2)}) collective-permute-start(f32[128,256]{1,0:T(8,128)S(1)} %dynamic-slice_add_fusion), channel_id=1, source_target_pairs={{0,2},{1,3},{2,4},{3,5},{4,6},{5,7},{6,0},{7,1},{8,10},{9,11},{10,... | collective-permute-start | bytes 393224 | tf_op jit(solution)/shard_map/ppermute | solution.py:109
  84.4 1.6 collective-permute-start.1
  86.0 1.6 collective-permute-done.2
  87.6 7.7 %collective-permute-done.3 = f32[128,256]{1,0:T(8,128)S(1)} collective-permute-done((f32[128,256]{1,0:T(8,128)S(1)}, f32[128,256]{1,0:T(8,128)S(1)}, u32[]{:S(2)}, u32[]{:S(2)}) %collective-permute-start.3) | collective-permute-done | bytes 131104 | tf_op jit(solution)/shard_map/ppermute | solution.py:109
  96.8 1.8 collective-permute-start.6
  98.6 1.8 collective-permute-start.4
  100.4 2.3 %collective-permute-done.5 = f32[128,256]{1,0:T(8,128)S(1)} collective-permute-done((f32[128,256]{1,0:T(8,128)S(1)}, f32[128,256]{1,0:T(8,128)S(1)}, u32[]{:S(2)}, u32[]{:S(2)}) %collective-permute-start.5) | collective-permute-done | bytes 131104 | tf_op jit(solution)/shard_map/ppermute | solution.py:113
  102.7 2.4 %collective-permute-done.4 = f32[128,256]{1,0:T(8,128)S(1)} collective-permute-done((f32[128,256]{1,0:T(8,128)S(1)}, f32[128,256]{1,0:T(8,128)S(1)}, u32[]{:S(2)}, u32[]{:S(2)}) %collective-permute-start.4) | collective-permute-done | bytes 131104 | tf_op jit(solution)/shard_map/ppermute | solution.py:113
  105.1 3.6 %collective-permute-start.12 = (f32[128,256]{1,0:T(8,128)S(1)}, f32[128,256]{1,0:T(8,128)S(1)}, u32[]{:S(2)}, u32[]{:S(2)}) collective-permute-start(f32[128,256]{1,0:T(8,128)S(1)} %add_add_fusion.1), channel_id=1, source_target_pairs={{0,96},{8,104},{16,112},{24,120},{32,128},{40,136},{48,144},{56,15... | collective-permute-start | bytes 393224 | tf_op jit(solution)/shard_map/ppermute | solution.py:119
  108.7 1.7 collective-permute-start.13
  112.3 3.7 %collective-permute-start.8 = (f32[128,256]{1,0:T(8,128)S(1)}, f32[128,256]{1,0:T(8,128)S(1)}, u32[]{:S(2)}, u32[]{:S(2)}) collective-permute-start(f32[128,256]{1,0:T(8,128)S(1)} %add_add_fusion.1), channel_id=1, source_target_pairs={{0,64},{8,72},{16,80},{24,88},{32,96},{40,104},{48,112},{56,120},{... | collective-permute-start | bytes 393224 | tf_op jit(solution)/shard_map/ppermute | solution.py:119
  116.8 3.1 %collective-permute-start.9 = (f32[128,256]{1,0:T(8,128)S(1)}, f32[128,256]{1,0:T(8,128)S(1)}, u32[]{:S(2)}, u32[]{:S(2)}) collective-permute-start(f32[128,256]{1,0:T(8,128)S(1)} %add_add_fusion.1), channel_id=1, source_target_pairs={{0,192},{8,200},{16,208},{24,216},{32,224},{40,232},{48,240},{56,2... | collective-permute-start | bytes 393224 | tf_op jit(solution)/shard_map/ppermute | solution.py:119
  120.0 3.9 %collective-permute-start.7 = (f32[128,256]{1,0:T(8,128)S(1)}, f32[128,256]{1,0:T(8,128)S(1)}, u32[]{:S(2)}, u32[]{:S(2)}) collective-permute-start(f32[128,256]{1,0:T(8,128)S(1)} %add_add_fusion.1), channel_id=1, source_target_pairs={{0,128},{8,136},{16,144},{24,152},{32,160},{40,168},{48,176},{56,1... | collective-permute-start | bytes 393224 | tf_op jit(solution)/shard_map/ppermute | solution.py:119
  123.8 2.6 %collective-permute-done.11 = f32[128,256]{1,0:T(8,128)S(1)} collective-permute-done((f32[128,256]{1,0:T(8,128)S(1)}, f32[128,256]{1,0:T(8,128)S(1)}, u32[]{:S(2)}, u32[]{:S(2)}) %collective-permute-start.11) | collective-permute-done | bytes 131104 | tf_op jit(solution)/shard_map/ppermute | solution.py:119
  126.7 2.2 %collective-permute-done.9 = f32[128,256]{1,0:T(8,128)S(1)} collective-permute-done((f32[128,256]{1,0:T(8,128)S(1)}, f32[128,256]{1,0:T(8,128)S(1)}, u32[]{:S(2)}, u32[]{:S(2)}) %collective-permute-start.9) | collective-permute-done | bytes 131104 | tf_op jit(solution)/shard_map/ppermute | solution.py:119
  132.6 12.1 %shard_map.41 = (f32[256,256]{1,0:T(8,128)}, f32[256,256]{1,0:T(8,128)}) custom-call(f32[256,256]{1,0:T(8,128)} %pad_maximum_fusion.g_ref), custom_call_target="tpu_custom_call" | custom-call | flops 201326592 | bytes 786432 | tf_op jit(solution)/shard_map/pallas_call | solution.py:92
  144.7 8.4 %fusion.2 = f32[256,640]{1,0:T(8,128)S(1)} fusion(bf16[8192,256]{1,0:T(8,128)(2,1)} %all-gather.2.cloned.1.call-done, bf16[8192,640]{1,0:T(8,128)(2,1)} %param.2), kind=kOutput, calls=%fused_computation.12 | convolution fusion | flops 2684354560 | bytes 15335424 | tf_op jit(solution)/shard_map/dot_general | solution.py:157
  153.2 1.7 convolution_bitcast_fusion
  154.8 9.6 %all-to-all-start = ((f32[32,8,640]{2,1,0:T(8,128)}), f32[32,8,640]{2,1,0:T(8,128)S(1)}, u32[]{:S(2)}, u32[]{:S(2)}) async-start(f32[32,8,640]{2,1,0:T(8,128)} %convolution_bitcast_fusion), calls=%async_computation.1 | async-start | bytes 1310720 | tf_op jit(solution)/shard_map/all_to_all | solution.py:161
  165.2 19.8 %all-to-all-done = f32[32,8,640]{2,1,0:T(8,128)S(1)} async-done(((f32[32,8,640]{2,1,0:T(8,128)}), f32[32,8,640]{2,1,0:T(8,128)S(1)}, u32[]{:S(2)}, u32[]{:S(2)}) %all-to-all-start) | async-done | bytes 655392 | tf_op jit(solution)/shard_map/all_to_all | solution.py:161
  (35 shorter events, 12.1 us)
Async XLA Ops:
  7.2 1.0 copy-start
  7.2 67.6 %reduce-scatter.2.cloned.1.call-start = ((), (), s32[]{:S(2)}) async-start(), calls=%async_computation.2 | async-start | bytes 9437184 | tf_op jit(solution)/shard_map/reduce_scatter | solution.py:150
  18.9 125.9 %all-gather.2.cloned.1.call-start = ((), (), s32[]{:S(2)}) async-start(), calls=%async_computation.3 | async-start | bytes 4718592 | tf_op jit(solution)/shard_map/all_gather | solution.py:151
  80.5 1.4 collective-permute-start
  81.9 5.6 %collective-permute-start.2 = (f32[128,256]{1,0:T(8,128)S(1)}, f32[128,256]{1,0:T(8,128)S(1)}, u32[]{:S(2)}, u32[]{:S(2)}) collective-permute-start(f32[128,256]{1,0:T(8,128)S(1)} %dynamic-slice_add_fusion), channel_id=1, source_target_pairs={{0,2},{1,3},{2,4},{3,5},{4,6},{5,7},{6,0},{7,1},{8,10},{9,11},{10,... | collective-permute-start | bytes 393224 | tf_op jit(solution)/shard_map/ppermute | solution.py:109
  84.4 10.8 %collective-permute-start.3 = (f32[128,256]{1,0:T(8,128)S(1)}, f32[128,256]{1,0:T(8,128)S(1)}, u32[]{:S(2)}, u32[]{:S(2)}) collective-permute-start(f32[128,256]{1,0:T(8,128)S(1)} %dynamic-slice_add_fusion), channel_id=1, source_target_pairs={{0,6},{1,7},{2,0},{3,1},{4,2},{5,3},{6,4},{7,5},{8,14},{9,15},{10,... | collective-permute-start | bytes 393224 | tf_op jit(solution)/shard_map/ppermute | solution.py:109
  84.4 10.8 %collective-permute-start.1 = (f32[128,256]{1,0:T(8,128)S(1)}, f32[128,256]{1,0:T(8,128)S(1)}, u32[]{:S(2)}, u32[]{:S(2)}) collective-permute-start(f32[128,256]{1,0:T(8,128)S(1)} %dynamic-slice_add_fusion), channel_id=1, source_target_pairs={{0,4},{1,5},{2,6},{3,7},{4,0},{5,1},{6,2},{7,3},{8,12},{9,13},{10,... | collective-permute-start | bytes 393224 | tf_op jit(solution)/shard_map/ppermute | solution.py:109
  95.3 7.4 %collective-permute-start.5 = (f32[128,256]{1,0:T(8,128)S(1)}, f32[128,256]{1,0:T(8,128)S(1)}, u32[]{:S(2)}, u32[]{:S(2)}) collective-permute-start(f32[128,256]{1,0:T(8,128)S(1)} %add_add_fusion.2), channel_id=1, source_target_pairs={{0,8},{8,16},{16,24},{24,0},{32,40},{40,48},{48,56},{56,32},{64,72... | collective-permute-start | bytes 393224 | tf_op jit(solution)/shard_map/ppermute | solution.py:113
  96.8 5.9 %collective-permute-start.6 = (f32[128,256]{1,0:T(8,128)S(1)}, f32[128,256]{1,0:T(8,128)S(1)}, u32[]{:S(2)}, u32[]{:S(2)}) collective-permute-start(f32[128,256]{1,0:T(8,128)S(1)} %add_add_fusion.2), channel_id=1, source_target_pairs={{0,24},{8,0},{16,8},{24,16},{32,56},{40,32},{48,40},{56,48},{64,88... | collective-permute-start | bytes 393224 | tf_op jit(solution)/shard_map/ppermute | solution.py:113
  98.6 6.5 %collective-permute-start.4 = (f32[128,256]{1,0:T(8,128)S(1)}, f32[128,256]{1,0:T(8,128)S(1)}, u32[]{:S(2)}, u32[]{:S(2)}) collective-permute-start(f32[128,256]{1,0:T(8,128)S(1)} %add_add_fusion.2), channel_id=1, source_target_pairs={{0,16},{8,24},{16,0},{24,8},{32,48},{40,56},{48,32},{56,40},{64,80... | collective-permute-start | bytes 393224 | tf_op jit(solution)/shard_map/ppermute | solution.py:113
  105.1 11.7 %collective-permute-start.12 = (f32[128,256]{1,0:T(8,128)S(1)}, f32[128,256]{1,0:T(8,128)S(1)}, u32[]{:S(2)}, u32[]{:S(2)}) collective-permute-start(f32[128,256]{1,0:T(8,128)S(1)} %add_add_fusion.1), channel_id=1, source_target_pairs={{0,96},{8,104},{16,112},{24,120},{32,128},{40,136},{48,144},{56,15... | collective-permute-start | bytes 393224 | tf_op jit(solution)/shard_map/ppermute | solution.py:119
  108.7 11.3 %collective-permute-start.13 = (f32[128,256]{1,0:T(8,128)S(1)}, f32[128,256]{1,0:T(8,128)S(1)}, u32[]{:S(2)}, u32[]{:S(2)}) collective-permute-start(f32[128,256]{1,0:T(8,128)S(1)} %add_add_fusion.1), channel_id=1, source_target_pairs={{0,224},{8,232},{16,240},{24,248},{32,0},{40,8},{48,16},{56,24},{6... | collective-permute-start | bytes 393224 | tf_op jit(solution)/shard_map/ppermute | solution.py:119
  110.4 13.4 %collective-permute-start.10 = (f32[128,256]{1,0:T(8,128)S(1)}, f32[128,256]{1,0:T(8,128)S(1)}, u32[]{:S(2)}, u32[]{:S(2)}) collective-permute-start(f32[128,256]{1,0:T(8,128)S(1)} %add_add_fusion.1), channel_id=1, source_target_pairs={{0,32},{8,40},{16,48},{24,56},{32,64},{40,72},{48,80},{56,88},{64,... | collective-permute-start | bytes 393224 | tf_op jit(solution)/shard_map/ppermute | solution.py:119
  111.5 15.0 %collective-permute-start.11 = (f32[128,256]{1,0:T(8,128)S(1)}, f32[128,256]{1,0:T(8,128)S(1)}, u32[]{:S(2)}, u32[]{:S(2)}) collective-permute-start(f32[128,256]{1,0:T(8,128)S(1)} %add_add_fusion.1), channel_id=1, source_target_pairs={{0,160},{8,168},{16,176},{24,184},{32,192},{40,200},{48,208},{56,2... | collective-permute-start | bytes 393224 | tf_op jit(solution)/shard_map/ppermute | solution.py:119
  112.3 14.4 %collective-permute-start.8 = (f32[128,256]{1,0:T(8,128)S(1)}, f32[128,256]{1,0:T(8,128)S(1)}, u32[]{:S(2)}, u32[]{:S(2)}) collective-permute-start(f32[128,256]{1,0:T(8,128)S(1)} %add_add_fusion.1), channel_id=1, source_target_pairs={{0,64},{8,72},{16,80},{24,88},{32,96},{40,104},{48,112},{56,120},{... | collective-permute-start | bytes 393224 | tf_op jit(solution)/shard_map/ppermute | solution.py:119
  116.8 12.1 %collective-permute-start.9 = (f32[128,256]{1,0:T(8,128)S(1)}, f32[128,256]{1,0:T(8,128)S(1)}, u32[]{:S(2)}, u32[]{:S(2)}) collective-permute-start(f32[128,256]{1,0:T(8,128)S(1)} %add_add_fusion.1), channel_id=1, source_target_pairs={{0,192},{8,200},{16,208},{24,216},{32,224},{40,232},{48,240},{56,2... | collective-permute-start | bytes 393224 | tf_op jit(solution)/shard_map/ppermute | solution.py:119
  120.0 10.2 %collective-permute-start.7 = (f32[128,256]{1,0:T(8,128)S(1)}, f32[128,256]{1,0:T(8,128)S(1)}, u32[]{:S(2)}, u32[]{:S(2)}) collective-permute-start(f32[128,256]{1,0:T(8,128)S(1)} %add_add_fusion.1), channel_id=1, source_target_pairs={{0,128},{8,136},{16,144},{24,152},{32,160},{40,168},{48,176},{56,1... | collective-permute-start | bytes 393224 | tf_op jit(solution)/shard_map/ppermute | solution.py:119
  130.2 1.7 collective-permute-start.14
  144.7 8.4 %copy-start.2 = (f32[256,256]{1,0:T(8,128)S(1)}, f32[256,256]{1,0:T(8,128)}, u32[]{:S(2)}) copy-start(f32[256,256]{1,0:T(8,128)} %get-tuple-element.4) | copy-start | bytes 786436
  144.7 19.8 %copy-start.1 = (f32[256,256]{1,0:T(8,128)S(1)}, f32[256,256]{1,0:T(8,128)}, u32[]{:S(2)}) copy-start(f32[256,256]{1,0:T(8,128)} %get-tuple-element.5) | copy-start | bytes 786436
  154.8 30.2 %all-to-all-start = ((f32[32,8,640]{2,1,0:T(8,128)}), f32[32,8,640]{2,1,0:T(8,128)S(1)}, u32[]{:S(2)}, u32[]{:S(2)}) async-start(f32[32,8,640]{2,1,0:T(8,128)} %convolution_bitcast_fusion), calls=%async_computation.1 | async-start | bytes 1310720 | tf_op jit(solution)/shard_map/all_to_all | solution.py:161
Sparse Core Ops, SparseCore 0:
  19.0 55.7 reduce-scatter.1
  77.0 35.0 all-gather.1

commit v2 on v1

--- a/solution.py
+++ b/solution.py
@@ -7,6 +7,7 @@
 from jax.sharding import PartitionSpec as P
 
 f32 = jnp.float32
+f16 = jnp.float16
 HI = lax.Precision.HIGHEST
 
 
@@ -59,22 +60,47 @@
     return jnp.concatenate(done, axis=0)[:, b : 2 * b]
 
 
-def factor_kernel(b, n, g_ref, r_ref, inv_ref, m_ref):
+def factor_kernel(
+    b, n, g_ref, sketch_ref, slab_ref, t_ref, p_ref, m_ref, y_ref, s_ref, x_ref, sems
+):
+    count, _, rows = sketch_ref.shape
+    copies = []
+    for i in range(count):
+        held = pl.ds(i * rows, rows)
+        copies.append(
+            (
+                pltpu.make_async_copy(sketch_ref.at[i], s_ref.at[i], sems.at[0, i]),
+                pltpu.make_async_copy(slab_ref.at[held], x_ref.at[held], sems.at[1, i]),
+            )
+        )
+        for copy in copies[-1]:
+            copy.start()
     m_ref[:, 0:n] = g_ref[...]
     ri = lax.broadcasted_iota(jnp.int32, (n, n), 0)
     ci = lax.broadcasted_iota(jnp.int32, (n, n), 1)
     m_ref[:, n : 2 * n] = jnp.where(ri == ci, 1.0, 0.0)
+    steps = n // b
     for s in range(0, n, b):
+        mine = range(s // b * count // steps, (s // b + 1) * count // steps)
+        for i in mine:
+            for copy in copies[i]:
+                copy.wait()
+        value = None if s == 0 else y_ref[...]
+        for i in mine:
+            term = jnp.dot(
+                s_ref[i], x_ref[i * rows : (i + 1) * rows, :], preferred_element_type=f32
+            )
+            value = term if value is None else value + term
+        y_ref[...] = value
         inverse = factor_diagonal(m_ref[s : s + b, s : s + b], b)
-        rows = jnp.dot(
+        rows_now = jnp.dot(
             inverse, m_ref[s : s + b, :], precision=HI, preferred_element_type=f32
         )
         rr = lax.broadcasted_iota(jnp.int32, (b, n), 0)
         cc = lax.broadcasted_iota(jnp.int32, (b, n), 1)
-        left = jnp.where(cc >= rr + s, rows[:, 0:n], 0.0)
-        right = rows[:, n : 2 * n]
-        r_ref[s : s + b, :] = left
-        inv_ref[s : s + b, :] = right
+        left = jnp.where(cc >= rr + s, rows_now[:, 0:n], 0.0)
+        right = rows_now[:, n : 2 * n]
+        t_ref[s : s + b, :] = left
         if s + b < n:
             update = lax.dot_general(
                 left,
@@ -84,21 +110,231 @@
                 preferred_element_type=f32,
             )
             m_ref[s + b : n, :] = m_ref[s + b : n, :] - update[s + b : n, :]
-
-
-def factor_and_inverse(gram, b=64):
+        m_ref[s : s + b, n : 2 * n] = right
+    value = jnp.dot(
+        m_ref[:, n : 2 * n], y_ref[...], precision=HI, preferred_element_type=f32
+    )
+    d = value.shape[1]
+    value, e = coded(value)
+    p_ref[:, 0:d] = value
+    p_ref[:, d : d + 128] = jnp.broadcast_to(e, (n, 128))
+
+
+def factor_and_project(gram, sketch, slab, b=64):
     n = gram.shape[0]
+    rows, d = slab.shape
+    vmem = pl.BlockSpec(memory_space=pltpu.VMEM)
+    far = pl.BlockSpec(memory_space=pl.ANY)
+    return pl.pallas_call(
+        functools.partial(factor_kernel, b, n),
+        out_shape=(
+            jax.ShapeDtypeStruct((n, n), f32),
+            jax.ShapeDtypeStruct((n, d + 128), f32),
+        ),
+        in_specs=[vmem, far, far],
+        out_specs=(vmem, vmem),
+        scratch_shapes=[
+            pltpu.VMEM((n, 2 * n), f32),
+            pltpu.VMEM((n, d), f32),
+            pltpu.VMEM(sketch.shape, sketch.dtype),
+            pltpu.VMEM((rows, d), slab.dtype),
+            pltpu.SemaphoreType.DMA((2, sketch.shape[0])),
+        ],
+        compiler_params=pltpu.CompilerParams(vmem_limit_bytes=40 << 20),
+        cost_estimate=pl.CostEstimate(
+            flops=12 * n**3 + 2 * rows * n * d,
+            bytes_accessed=12 * n * n + 2 * rows * (n + d),
+            transcendentals=n,
+        ),
+    )(
+        gram,
+        pltpu.with_memory_space_constraint(sketch, pltpu.HBM),
+        pltpu.with_memory_space_constraint(slab, pltpu.HBM),
+    )
+
+
+ROWS_AT_ONCE = 512
+VMEM_LIMIT = 24 << 20
+
+
+def coded(x):
+    e = jnp.ceil(jnp.log2(jnp.maximum(jnp.max(jnp.abs(x), keepdims=True), 1e-30)))
+    return x * jnp.exp2(14.0 - e), e
+
+
+def write_coded(out_ref, x):
+    n = x.shape[0]
+    y, e = coded(x)
+    out_ref[0:n, :] = y
+    out_ref[n : n + 16, :] = jnp.broadcast_to(e, (16, x.shape[1]))
+
+
+def read_coded(ref):
+    n = ref.shape[0] - 16
+    return ref[0:n, :] * jnp.exp2(ref[n : n + 1, :] - 14.0)
+
+
+FAR = ((2, 0), (2, 1))
+NEAR = ((1, 1), (3, 0), (1, 0), (3, 1))
+HERE = ((0, 0), (0, 1))
+
+
+def piece(ring, core, s, h):
+    start = (((ring + s) % 4 * 2 + core) * 2 + h) * ROWS_AT_ONCE
+    return pl.ds(pl.multiple_of(start, ROWS_AT_ONCE), ROWS_AT_ONCE)
+
+
+def load_kernel(
+    place_ref, slab_ref, basis_ref, held_ref, held_basis_ref, first_ref, here_ref, sems
+):
+    ring, core = place_ref[0], place_ref[1]
+    pieces = [(c, s, h) for c in (1 - core, core) for s, h in FAR + NEAR + HERE]
+    copies = [pltpu.make_async_copy(basis_ref, held_basis_ref, sems.at[len(pieces)])]
+    copies[0].start()
+    for i, (c, s, h) in enumerate(pieces):
+        rows = piece(ring, c, s, h)
+        copies.append(pltpu.make_async_copy(slab_ref.at[rows], held_ref.at[rows], sems.at[i]))
+        copies[-1].start()
+    copies.pop(0).wait()
+    size = ROWS_AT_ONCE + 16
+    outs = [first_ref.at[i * size : (i + 1) * size] for i in range(len(FAR + NEAR))]
+    outs += [here_ref.at[i * size : (i + 1) * size] for i in range(len(HERE))]
+    for i in range(0, len(outs), 2):
+        for copy in copies[i : i + 2]:
+            copy.wait()
+        for out, (c, s, h) in zip(outs[i : i + 2], pieces[i : i + 2]):
+            x = jnp.dot(
+                held_ref[piece(ring, c, s, h), :],
+                held_basis_ref[...],
+                preferred_element_type=f32,
+            )
+            write_coded(out, x)
+    for copy in copies[len(outs) :]:
+        copy.wait()
+
+
+def load_and_sketch(slab, basis, place):
+    rows, d = slab.shape
+    k, size = basis.shape[1], ROWS_AT_ONCE + 16
+    vmem = pl.BlockSpec(memory_space=pltpu.VMEM)
+    far = pl.BlockSpec(memory_space=pl.ANY)
+    return pl.pallas_call(
+        load_kernel,
+        out_shape=(
+            pltpu.VMEM((rows, d), slab.dtype),
+            pltpu.VMEM((d, k), basis.dtype),
+            jax.ShapeDtypeStruct((len(FAR + NEAR) * size, k), f32),
+            jax.ShapeDtypeStruct((len(HERE) * size, k), f32),
+        ),
+        in_specs=[pl.BlockSpec(memory_space=pltpu.SMEM), far, far],
+        out_specs=(vmem,) * 4,
+        scratch_shapes=[pltpu.SemaphoreType.DMA((17,))],
+        compiler_params=pltpu.CompilerParams(vmem_limit_bytes=VMEM_LIMIT),
+        cost_estimate=pl.CostEstimate(
+            flops=rows * d * k, bytes_accessed=2 * rows * (d + 2 * k), transcendentals=0
+        ),
+    )(
+        place,
+        pltpu.with_memory_space_constraint(slab, pltpu.HBM),
+        pltpu.with_memory_space_constraint(basis, pltpu.HBM),
+    )
+
+
+def sketch_kernel(pieces, place_ref, slab_ref, basis_ref, other_ref, *outs):
+    ring, core = place_ref[0], place_ref[1]
+    b = ROWS_AT_ONCE
+    for i, ((s, h), out) in enumerate(zip(pieces, outs)):
+        x = jnp.dot(
+            slab_ref[piece(ring, core, s, h), :], basis_ref[...], preferred_element_type=f32
+        )
+        x = x + read_coded(other_ref.at[i * (b + 16) : (i + 1) * (b + 16)])
+        if out.shape[0] == b:
+            out[...] = x
+        else:
+            write_coded(out, x)
+
+
+def sketch_rows(held, basis, place, other, pieces, plain):
+    b, (d, k) = ROWS_AT_ONCE, basis.shape
+    count = len(pieces)
     vmem = pl.BlockSpec(memory_space=pltpu.VMEM)
     return pl.pallas_call(
-        functools.partial(factor_kernel, b, n),
-        out_shape=(jax.ShapeDtypeStruct((n, n), f32),) * 2,
-        in_specs=[vmem],
+        functools.partial(sketch_kernel, pieces),
+        out_shape=[
+            jax.ShapeDtypeStruct((b + 16 if i < count - plain else b, k), f32)
+            for i in range(count)
+        ],
+        in_specs=[pl.BlockSpec(memory_space=pltpu.SMEM), vmem, vmem, vmem],
+        out_specs=[vmem] * count,
+        compiler_params=pltpu.CompilerParams(vmem_limit_bytes=VMEM_LIMIT),
+        cost_estimate=pl.CostEstimate(
+            flops=2 * count * b * d * k,
+            bytes_accessed=count * b * (2 * d + 8 * k),
+            transcendentals=0,
+        ),
+    )(
+        place,
+        pltpu.with_memory_space_constraint(held, pltpu.VMEM),
+        pltpu.with_memory_space_constraint(basis, pltpu.VMEM),
+        other,
+    )
+
+
+def add_kernel(a_ref, b_ref, c_ref, d_ref, up_ref, down_ref):
+    write_coded(up_ref, a_ref[...] + read_coded(b_ref))
+    write_coded(down_ref, c_ref[...] + read_coded(d_ref))
+
+
+def add_received(a, b, c, d):
+    vmem = pl.BlockSpec(memory_space=pltpu.VMEM)
+    return pl.pallas_call(
+        add_kernel,
+        out_shape=(jax.ShapeDtypeStruct(b.shape, f32),) * 2,
+        in_specs=[vmem] * 4,
         out_specs=(vmem, vmem),
-        scratch_shapes=[pltpu.VMEM((n, 2 * n), f32)],
+        compiler_params=pltpu.CompilerParams(vmem_limit_bytes=VMEM_LIMIT),
         cost_estimate=pl.CostEstimate(
-            flops=12 * n**3, bytes_accessed=12 * n * n, transcendentals=n
-        ),
-    )(gram)
+            flops=4 * a.size, bytes_accessed=24 * a.size, transcendentals=0
+        ),
+    )(a, b, c, d)
+
+
+def gram_kernel(a_ref, b_ref, c_ref, d_ref, e_ref, f_ref, gram_ref, half_ref):
+    n = gram_ref.shape[0]
+    total = None
+    b = a_ref.shape[0]
+    for i, (own, first, second) in enumerate(
+        ((a_ref, b_ref, c_ref), (d_ref, e_ref, f_ref))
+    ):
+        s = (own[...] + read_coded(first) + read_coded(second)).T
+        top = s.astype(jnp.bfloat16)
+        rest = (s - top.astype(f32)).astype(jnp.bfloat16)
+        half_ref[:, i * b : (i + 1) * b] = top
+        both = jnp.concatenate([top, rest], axis=0)
+        g = lax.dot_general(
+            both, both, (((1,), (1,)), ((), ())), preferred_element_type=f32
+        )
+        g = (g[0:n, 0:n] + g[n:, n:]) + (g[0:n, n:] + g[n:, 0:n])
+        total = g if total is None else total + g
+    gram_ref[...] = total
+
+
+def gram_and_half(low, high):
+    rows, k = low[0].shape
+    vmem = pl.BlockSpec(memory_space=pltpu.VMEM)
+    return pl.pallas_call(
+        gram_kernel,
+        out_shape=(
+            jax.ShapeDtypeStruct((k, k), f32),
+            jax.ShapeDtypeStruct((k, 2 * rows), jnp.bfloat16),
+        ),
+        in_specs=[vmem] * 6,
+        out_specs=(vmem, vmem),
+        compiler_params=pltpu.CompilerParams(vmem_limit_bytes=VMEM_LIMIT),
+        cost_estimate=pl.CostEstimate(
+            flops=16 * rows * k * k, bytes_accessed=28 * rows * k, transcendentals=0
+        ),
+    )(*low, *high)
 
 
 def shift_core(x):
@@ -119,25 +355,30 @@
     return lax.ppermute(x, "rows", [(i, (i + 4 * k) % 32) for i in range(32)])
 
 
-def sum_of_four(x, shift):
-    return (x + shift(x, 2)) + (shift(x, 1) + shift(x, -1))
-
-
-def sum_of_eight(x, shift):
-    even = (x + shift(x, 4)) + (shift(x, 2) + shift(x, -2))
-    odd = (shift(x, 1) + shift(x, -3)) + (shift(x, 3) + shift(x, -1))
-    return even + odd
+def sum_of_four(x, shift, step=1):
+    return (x + shift(x, 2 * step)) + (shift(x, step) + shift(x, -step))
+
+
+def block_of(x, index, size):
+    return lax.dynamic_slice_in_dim(x, index * size, size, 0)
 
 
 def sum_everywhere(x):
     core = lax.axis_index("width") % 2
-    half = x.shape[0] // 2
-    own = lax.dynamic_slice_in_dim(x, core * half, half, 0)
-    other = lax.dynamic_slice_in_dim(x, (1 - core) * half, half, 0)
-    own = own + shift_core(other)
+    col = lax.axis_index("rows") % 4
+    plane = lax.axis_index("rows") // 4
+    half, piece = x.shape[0] // 2, x.shape[0] // 8
+    own = block_of(x, core, half) + shift_core(block_of(x, 1 - core, half))
+    parts = [block_of(own, (col + k) % 4, piece) for k in range(4)]
+    own = (parts[0] + shift_x(parts[2], 2)) + (
+        shift_x(parts[1], 1) + shift_x(parts[3], -1)
+    )
+    own = sum_of_four(own, shift_z, 2)
+    own = own + lax.ppermute(own, "rows", [(i, i ^ 4) for i in range(32)])
     own = sum_of_four(own, shift_y)
-    own = sum_of_four(own, shift_x)
-    own = sum_of_eight(own, shift_z)
+    ring = [own, shift_x(own, -1), shift_x(own, 2), shift_x(own, 1)]
+    ring = jnp.concatenate(ring + ring, axis=0)
+    own = lax.dynamic_slice_in_dim(ring, (4 - col) % 4 * piece, half, 0)
     other = shift_core(own)
     first = jnp.where(core == 0, own, other)
     second = jnp.where(core == 0, other, own)
@@ -145,21 +386,34 @@
 
 
 def shards(slab, basis):
+    width = lax.axis_index("width")
     total_rows = slab.shape[0] * lax.axis_size("rows")
-    partial_sketch = jnp.dot(slab, basis, preferred_element_type=f32)
-    sketch = lax.psum_scatter(partial_sketch, "width", scatter_dimension=0, tiled=True)
-    whole = lax.all_gather(sketch.astype(jnp.bfloat16), "width", axis=0, tiled=True)
-    gram = lax.dot_general(
-        sketch, sketch, (((0,), (0,)), ((), ())), precision=HI, preferred_element_type=f32
-    )
-    gram = sum_everywhere(gram)
-    factor, inverse = factor_and_inverse(gram)
-    value = lax.dot_general(
-        whole, slab, (((0,), (0,)), ((), ())), preferred_element_type=f32
-    )
-    value = jnp.dot(inverse, value, precision=HI, preferred_element_type=f32)
-    pieces = lax.all_to_all(value, "rows", 0, 0, tiled=True)
-    projected = jnp.sum(pieces.reshape(32, 8, -1), axis=0).T
+    place = jnp.stack([width // 2, width % 2]).astype(jnp.int32)
+
+    held, held_basis, first, here = load_and_sketch(slab, basis, place)
+    first = shift_core(first.astype(f16))
+    first, here = lax.optimization_barrier((first, here))
+    here = shift_core(here.astype(f16))
+    first = sketch_rows(held, held_basis, place, first.astype(f32), FAR + NEAR, 2)
+    far_up, far_down, near_up, near_down, up, down = first
+    far_up, far_down = shift_y(far_up.astype(f16), 1), shift_y(far_down.astype(f16), -1)
+    near_up = shift_y(near_up.astype(f16), 1)
+    near_down = shift_y(near_down.astype(f16), -1)
+    low, high = sketch_rows(held, held_basis, place, here.astype(f32), HERE, 2)
+
+    up, down = add_received(up, far_up.astype(f32), down, far_down.astype(f32))
+    up, down = shift_y(up.astype(f16), 1), shift_y(down.astype(f16), -1)
+    gram, sketch = gram_and_half(
+        (low, up.astype(f32), near_down.astype(f32)),
+        (high, near_up.astype(f32), down.astype(f32)),
+    )
+
+    sketch = lax.all_gather(sketch, "width", axis=0)
+    factor, value = factor_and_project(sum_everywhere(gram), sketch, slab)
+    pieces = lax.all_to_all(value.astype(f16), "rows", 0, 0, tiled=True).reshape(32, 8, -1)
+    n = slab.shape[1]
+    scale = jnp.exp2(pieces[:, :, n : n + 1].astype(f32) - 14.0)
+    projected = jnp.sum(pieces[:, :, :n].astype(f32) * scale, axis=0).T
     triangle = factor / jnp.sqrt(f32(total_rows))
     return (projected, triangle)
 

time: 193 us -> 136 us (0.70)
  waiting for transfers between devices: 99.3 us -> 53.6 us
  matrix products: 24.3 us -> 0 us
  Pallas kernels: 12.1 us -> 23.9 us
    reduce_scatter x1 -> x0, waiting for transfers between devices: 55.9 us -> none  [shards(): lax.psum_scatter(partial_sketch, 'width', scatter_dimension=0, tiled=True)]
    dot_general x4 -> x0, matrix products: 24.3 us -> none  [the longest x1 10.7 us: shards(): partial_sketch = jnp.dot(slab, basis, preferred_element_type=f32)]
    pallas_call x1 -> x6, Pallas kernels: 12.1 us -> 23.9 us  [the longest x1 14 us: factor_and_project(): pl.pallas_call(functools.partial(factor_kernel, b, n), out_shape=(jax.Sha...]
    ppermute x7 -> x3, starting transfers between devices: 17.9 us -> 9.76 us  [shift_z(): return lax.ppermute(x, 'rows', [(i, (i + 4 * k) % 32) for i in range(32)])]
    ppermute x3 -> x9, waiting for transfers between devices: 9.28 us -> 17.3 us  [shift_y(): return lax.ppermute(x, 'width', [(i, (i + 2 * k) % 8) for i in range(8)])]
    ppermute x3 -> x9, starting transfers between devices: 4.06 us -> 11.1 us  [shift_y(): return lax.ppermute(x, 'width', [(i, (i + 2 * k) % 8) for i in range(8)])]
    all_to_all x1, waiting for transfers between devices: 19.8 us -> 14.9 us  [shards(): lax.all_to_all(value.astype(f16), 'rows', 0, 0, tiled=True)]
    ppermute x3 -> x6, waiting for transfers between devices: 4.65 us -> 9.49 us  [shift_x(): lax.ppermute(x, 'rows', [(i, i // 4 * 4 + (i % 4 + k) % 4) for i in range...]
  transfers between devices with their start and end apart: 18 -> 25, of which waited for: 13 -> 18; matrix products, arithmetic and copies ran while one was open for 3% -> 1% of each run, Pallas kernels for 6% -> 1%
where the time goes in v2:
time: 136 us; the launch traced here: 134 us
  waiting for transfers between devices  53.6 us (39%)
  starting transfers between devices  38 us (28%)
  Pallas kernels  23.9 us (18%)
  between operations  14.4 us (11%)
  other arithmetic  3.59 us (3%)
    ppermute x9, waiting for transfers between devices, shift_y(): return lax.ppermute(x, 'width', [(i, (i + 2 * k) % 8) for i in range(8)])  17.3 us
    all_to_all x1, waiting for transfers between devices, shards(): lax.all_to_all(value.astype(f16), 'rows', 0, 0, tiled=True)  14.9 us
    pallas_call x1, Pallas kernels, factor_and_project(): pl.pallas_call(functools.partial(factor_kernel, b, n), out_shape=(jax.Sha...  14 us
    ppermute x9, starting transfers between devices, shift_y(): return lax.ppermute(x, 'width', [(i, (i + 2 * k) % 8) for i in range(8)])  11.1 us
    ppermute x3, starting transfers between devices, shift_z(): return lax.ppermute(x, 'rows', [(i, (i + 4 * k) % 32) for i in range(32)])  9.76 us
    ppermute x6, waiting for transfers between devices, shift_x(): lax.ppermute(x, 'rows', [(i, i // 4 * 4 + (i % 4 + k) % 4) for i in range...  9.49 us
    all_to_all x1, starting transfers between devices, shards(): lax.all_to_all(value.astype(f16), 'rows', 0, 0, tiled=True)  7.85 us
    ppermute x6, starting transfers between devices, shift_x(): lax.ppermute(x, 'rows', [(i, i // 4 * 4 + (i % 4 + k) % 4) for i in range...  7.63 us
  transfers between devices with their start and end apart: 25, of which 18 were waited for; matrix products, arithmetic and copies ran while one was open for 1% of the time, Pallas kernels for 1%

profile of v2, /device:TPU:24, one launch (start us, length us, event | category | flops | bytes accessed | tf_op | source)
XLA Modules:
  0.0 133.9 jit_solution(996151145514963927)
XLA Ops:
  7.3 5.2 %shard_map.41 = (bf16[8192,640]{1,0:T(8,128)(2,1)S(1)}, bf16[640,256]{1,0:T(8,128)(2,1)S(1)}, f32[3168,256]{1,0:T(8,128)S(1)}, f32[1056,256]{1,0:T(8,128)S(1)}) custom-call(s32[2]{0:T(128)S(1)} %pad_add_fusion.place_ref, bf16[8192,640]{1,0:T(8,128)(2,1)} %slab_ref.3, bf16[640,256]{1,0:T(8,128)(2,1)} %basis_ref.1), custom_call_target="tpu_custom_call" | custom-call | flops 1342177280 | bytes 18874368 | tf_op jit(solution)/shard_map/pallas_call | solution.py:221
  12.9 3.5 %collective-permute-done = f16[3168,256]{1,0:T(8,128)(2,1)S(1)} collective-permute-done((f16[3168,256]{1,0:T(8,128)(2,1)S(1)}, f16[3168,256]{1,0:T(8,128)(2,1)S(1)}, u32[]{:S(2)}, u32[]{:S(2)}) %collective-permute-start) | collective-permute-done | bytes 1622048 | tf_op jit(solution)/shard_map/ppermute | solution.py:341
  16.6 2.1 %shard_map.43 = (f32[528,256]{1,0:T(8,128)S(1)}, f32[528,256]{1,0:T(8,128)S(1)}, f32[528,256]{1,0:T(8,128)S(1)}, f32[528,256]{1,0:T(8,128)S(1)}, f32[512,256]{1,0:T(8,128)S(1)}, /*index=5*/f32[512,256]{1,0:T(8,128)S(1)}) custom-call(s32[2]{0:T(128)S(1)} %pad_add_fusion.place_ref, bf16[8192,640]{1,0:T(8,128)(2,1)S(1)} %get-tuple-element.22.slab_ref, ...), custom_call_target="tpu_custom_call" | custom-call | flops 1006632960 | bytes 10223616 | tf_op jit(solution)/shard_map/pallas_call | solution.py:261
  18.8 2.0 %collective-permute-start.2 = (f16[528,256]{1,0:T(8,128)(2,1)S(1)}, f16[528,256]{1,0:T(8,128)(2,1)S(1)}, u32[]{:S(2)}, u32[]{:S(2)}) collective-permute-start(f16[528,256]{1,0:T(8,128)(2,1)S(1)} %convert_element_type.61), channel_id=1, source_target_pairs={{0,2},{1,3},{2,4},{3,5},{4,6},{5,7},{6,0},{7,1},{8,10},{9,11},{10,... | collective-permute-start | bytes 811016 | tf_op jit(solution)/shard_map/ppermute | solution.py:345
  22.1 2.6 %collective-permute-start.6 = (f16[528,256]{1,0:T(8,128)(2,1)S(1)}, f16[528,256]{1,0:T(8,128)(2,1)S(1)}, u32[]{:S(2)}, u32[]{:S(2)}) collective-permute-start(f16[528,256]{1,0:T(8,128)(2,1)S(1)} %convert_element_type.69), channel_id=1, source_target_pairs={{0,2},{1,3},{2,4},{3,5},{4,6},{5,7},{6,0},{7,1},{8,10},{9,11},{10,... | collective-permute-start | bytes 811016 | tf_op jit(solution)/shard_map/ppermute | solution.py:345
  24.7 3.5 %collective-permute-done.2 = f16[528,256]{1,0:T(8,128)(2,1)S(1)} collective-permute-done((f16[528,256]{1,0:T(8,128)(2,1)S(1)}, f16[528,256]{1,0:T(8,128)(2,1)S(1)}, u32[]{:S(2)}, u32[]{:S(2)}) %collective-permute-start.2) | collective-permute-done | bytes 270368 | tf_op jit(solution)/shard_map/ppermute | solution.py:345
  28.2 3.3 %collective-permute-done.3 = f16[528,256]{1,0:T(8,128)(2,1)S(1)} collective-permute-done((f16[528,256]{1,0:T(8,128)(2,1)S(1)}, f16[528,256]{1,0:T(8,128)(2,1)S(1)}, u32[]{:S(2)}, u32[]{:S(2)}) %collective-permute-start.3) | collective-permute-done | bytes 270368 | tf_op jit(solution)/shard_map/ppermute | solution.py:345
  32.1 2.1 %collective-permute-start.7 = (f16[528,256]{1,0:T(8,128)(2,1)S(1)}, f16[528,256]{1,0:T(8,128)(2,1)S(1)}, u32[]{:S(2)}, u32[]{:S(2)}) collective-permute-start(f16[528,256]{1,0:T(8,128)(2,1)S(1)} %convert_element_type.71), channel_id=1, source_target_pairs={{0,6},{1,7},{2,0},{3,1},{4,2},{5,3},{6,4},{7,5},{8,14},{9,15},{10,... | collective-permute-start | bytes 811016 | tf_op jit(solution)/shard_map/ppermute | solution.py:345
  34.2 3.1 %collective-permute-done.5 = f16[528,256]{1,0:T(8,128)(2,1)S(1)} collective-permute-done((f16[528,256]{1,0:T(8,128)(2,1)S(1)}, f16[528,256]{1,0:T(8,128)(2,1)S(1)}, u32[]{:S(2)}, u32[]{:S(2)}) %collective-permute-start.5) | collective-permute-done | bytes 270368 | tf_op jit(solution)/shard_map/ppermute | solution.py:345
  40.1 1.9 %collective-permute-done.7 = f16[528,256]{1,0:T(8,128)(2,1)S(1)} collective-permute-done((f16[528,256]{1,0:T(8,128)(2,1)S(1)}, f16[528,256]{1,0:T(8,128)(2,1)S(1)}, u32[]{:S(2)}, u32[]{:S(2)}) %collective-permute-start.7) | collective-permute-done | bytes 270368 | tf_op jit(solution)/shard_map/ppermute | solution.py:345
  45.0 3.2 %collective-permute-start.11 = (f32[32,256]{1,0:T(8,128)S(1)}, f32[32,256]{1,0:T(8,128)S(1)}, u32[]{:S(2)}, u32[]{:S(2)}) collective-permute-start(f32[32,256]{1,0:T(8,128)S(1)} %get-tuple-element.49), channel_id=1, source_target_pairs={{0,24},{8,0},{16,8},{24,16},{32,56},{40,32},{48,40},{56,48},{64,88... | collective-permute-start | bytes 98312 | tf_op jit(solution)/shard_map/ppermute | solution.py:349
  48.4 1.7 %collective-permute-done.10 = f32[32,256]{1,0:T(8,128)S(1)} collective-permute-done((f32[32,256]{1,0:T(8,128)S(1)}, f32[32,256]{1,0:T(8,128)S(1)}, u32[]{:S(2)}, u32[]{:S(2)}) %collective-permute-start.10) | collective-permute-done | bytes 32800 | tf_op jit(solution)/shard_map/ppermute | solution.py:349
  50.1 3.5 %collective-permute-done.9 = f32[32,256]{1,0:T(8,128)S(1)} collective-permute-done((f32[32,256]{1,0:T(8,128)S(1)}, f32[32,256]{1,0:T(8,128)S(1)}, u32[]{:S(2)}, u32[]{:S(2)}) %collective-permute-start.9) | collective-permute-done | bytes 32800 | tf_op jit(solution)/shard_map/ppermute | solution.py:349
  53.7 1.7 %collective-permute-start.13 = (f32[32,256]{1,0:T(8,128)S(1)}, f32[32,256]{1,0:T(8,128)S(1)}, u32[]{:S(2)}, u32[]{:S(2)}) collective-permute-start(f32[32,256]{1,0:T(8,128)S(1)} %add_add_fusion.2), channel_id=1, source_target_pairs={{0,64},{8,72},{16,80},{24,88},{32,96},{40,104},{48,112},{56,120},{... | collective-permute-start | bytes 98312 | tf_op jit(solution)/shard_map/ppermute | solution.py:355
  55.4 3.1 %collective-permute-start.14 = (f32[32,256]{1,0:T(8,128)S(1)}, f32[32,256]{1,0:T(8,128)S(1)}, u32[]{:S(2)}, u32[]{:S(2)}) collective-permute-start(f32[32,256]{1,0:T(8,128)S(1)} %add_add_fusion.2), channel_id=1, source_target_pairs={{0,192},{8,200},{16,208},{24,216},{32,224},{40,232},{48,240},{56,2... | collective-permute-start | bytes 98312 | tf_op jit(solution)/shard_map/ppermute | solution.py:355
  58.5 5.0 %collective-permute-start.12 = (f32[32,256]{1,0:T(8,128)S(1)}, f32[32,256]{1,0:T(8,128)S(1)}, u32[]{:S(2)}, u32[]{:S(2)}) collective-permute-start(f32[32,256]{1,0:T(8,128)S(1)} %add_add_fusion.2), channel_id=1, source_target_pairs={{0,128},{8,136},{16,144},{24,152},{32,160},{40,168},{48,176},{56,1... | collective-permute-start | bytes 98312 | tf_op jit(solution)/shard_map/ppermute | solution.py:355
  63.4 2.9 %collective-permute-done.12 = f32[32,256]{1,0:T(8,128)S(1)} collective-permute-done((f32[32,256]{1,0:T(8,128)S(1)}, f32[32,256]{1,0:T(8,128)S(1)}, u32[]{:S(2)}, u32[]{:S(2)}) %collective-permute-start.12) | collective-permute-done | bytes 32800 | tf_op jit(solution)/shard_map/ppermute | solution.py:355
  67.4 2.9 %collective-permute-done.15 = f32[32,256]{1,0:T(8,128)S(1)} collective-permute-done((f32[32,256]{1,0:T(8,128)S(1)}, f32[32,256]{1,0:T(8,128)S(1)}, u32[]{:S(2)}, u32[]{:S(2)}) %collective-permute-start.15) | collective-permute-done | bytes 32800 | tf_op jit(solution)/shard_map/ppermute | solution.py:377
  74.9 1.9 %collective-permute-done.18 = f32[32,256]{1,0:T(8,128)S(1)} collective-permute-done((f32[32,256]{1,0:T(8,128)S(1)}, f32[32,256]{1,0:T(8,128)S(1)}, u32[]{:S(2)}, u32[]{:S(2)}) %collective-permute-start.18) | collective-permute-done | bytes 32800 | tf_op jit(solution)/shard_map/ppermute | solution.py:345
  77.8 2.3 %collective-permute-start.19 = (f32[32,256]{1,0:T(8,128)S(1)}, f32[32,256]{1,0:T(8,128)S(1)}, u32[]{:S(2)}, u32[]{:S(2)}) collective-permute-start(f32[32,256]{1,0:T(8,128)S(1)} %get-tuple-element.45), channel_id=1, source_target_pairs={{0,24},{8,0},{16,8},{24,16},{32,56},{40,32},{48,40},{56,48},{64,88... | collective-permute-start | bytes 98312 | tf_op jit(solution)/shard_map/ppermute | solution.py:349
  81.8 3.7 %collective-permute-done.20 = f32[32,256]{1,0:T(8,128)S(1)} collective-permute-done((f32[32,256]{1,0:T(8,128)S(1)}, f32[32,256]{1,0:T(8,128)S(1)}, u32[]{:S(2)}, u32[]{:S(2)}) %collective-permute-start.20) | collective-permute-done | bytes 32800 | tf_op jit(solution)/shard_map/ppermute | solution.py:349
  87.8 14.0 %shard_map.46 = (f32[256,256]{1,0:T(8,128)S(1)}, f32[256,768]{1,0:T(8,128)S(1)}) custom-call(f32[256,256]{1,0:T(8,128)S(1)} %pad_maximum_fusion.g_ref, bf16[8,256,1024]{2,1,0:T(8,128)(2,1)} %bitcast.9, bf16[8192,640]{1,0:T(8,128)(2,1)} %slab_ref.3), custom_call_target="tpu_custom_call" | custom-call | flops 2885681152 | bytes 15466496 | tf_op jit(solution)/shard_map/pallas_call | solution.py:128
  102.6 7.9 %all-to-all-start = ((f16[32,8,768]{2,1,0:T(8,128)(2,1)}), f16[32,8,768]{2,1,0:T(8,128)(2,1)S(1)}, u32[]{:S(2)}, u32[]{:S(2)}) async-start(f16[32,8,768]{2,1,0:T(8,128)(2,1)} %convert_bitcast_fusion), calls=%async_computation | async-start | bytes 786432 | tf_op jit(solution)/shard_map/all_to_all | solution.py:413
  111.2 14.9 %all-to-all-done = f16[32,8,768]{2,1,0:T(8,128)(2,1)S(1)} async-done(((f16[32,8,768]{2,1,0:T(8,128)(2,1)}), f16[32,8,768]{2,1,0:T(8,128)(2,1)S(1)}, u32[]{:S(2)}, u32[]{:S(2)}) %all-to-all-start) | async-done | bytes 393248 | tf_op jit(solution)/shard_map/all_to_all | solution.py:413
  (74 shorter events, 21.7 us)
Async XLA Ops:
  7.2 80.7 %all-gather.3.cloned.1.call-start = ((), (), s32[]{:S(2)}) async-start(), calls=%async_computation.1 | async-start | bytes 4718592 | tf_op jit(solution)/shard_map/all_gather | solution.py:411
  12.8 3.6 %collective-permute-start = (f16[3168,256]{1,0:T(8,128)(2,1)S(1)}, f16[3168,256]{1,0:T(8,128)(2,1)S(1)}, u32[]{:S(2)}, u32[]{:S(2)}) collective-permute-start(f16[3168,256]{1,0:T(8,128)(2,1)S(1)} %convert_element_type.57), channel_id=1, source_target_pairs={{0,1},{1,0},{2,3},{3,2},{4,5},{5,4},{6,7},{7,6},{8,9},{9,8},{10,11... | collective-permute-start | bytes 4866056 | tf_op jit(solution)/shard_map/ppermute | solution.py:341
  18.8 9.4 %collective-permute-start.2 = (f16[528,256]{1,0:T(8,128)(2,1)S(1)}, f16[528,256]{1,0:T(8,128)(2,1)S(1)}, u32[]{:S(2)}, u32[]{:S(2)}) collective-permute-start(f16[528,256]{1,0:T(8,128)(2,1)S(1)} %convert_element_type.61), channel_id=1, source_target_pairs={{0,2},{1,3},{2,4},{3,5},{4,6},{5,7},{6,0},{7,1},{8,10},{9,11},{10,... | collective-permute-start | bytes 811016 | tf_op jit(solution)/shard_map/ppermute | solution.py:345
  20.8 10.7 %collective-permute-start.3 = (f16[528,256]{1,0:T(8,128)(2,1)S(1)}, f16[528,256]{1,0:T(8,128)(2,1)S(1)}, u32[]{:S(2)}, u32[]{:S(2)}) collective-permute-start(f16[528,256]{1,0:T(8,128)(2,1)S(1)} %convert_element_type.63), channel_id=1, source_target_pairs={{0,6},{1,7},{2,0},{3,1},{4,2},{5,3},{6,4},{7,5},{8,14},{9,15},{10,... | collective-permute-start | bytes 811016 | tf_op jit(solution)/shard_map/ppermute | solution.py:345
  21.1 16.3 %collective-permute-start.1 = (f16[1056,256]{1,0:T(8,128)(2,1)S(1)}, f16[1056,256]{1,0:T(8,128)(2,1)S(1)}, u32[]{:S(2)}, u32[]{:S(2)}) collective-permute-start(f16[1056,256]{1,0:T(8,128)(2,1)S(1)} %convert_element_type.58), channel_id=1, source_target_pairs={{0,1},{1,0},{2,3},{3,2},{4,5},{5,4},{6,7},{7,6},{8,9},{9,8},{10,11... | collective-permute-start | bytes 1622024 | tf_op jit(solution)/shard_map/ppermute | solution.py:341
  21.2 16.0 %collective-permute-start.5 = (f16[528,256]{1,0:T(8,128)(2,1)S(1)}, f16[528,256]{1,0:T(8,128)(2,1)S(1)}, u32[]{:S(2)}, u32[]{:S(2)}) collective-permute-start(f16[528,256]{1,0:T(8,128)(2,1)S(1)} %convert_element_type.67), channel_id=1, source_target_pairs={{0,6},{1,7},{2,0},{3,1},{4,2},{5,3},{6,4},{7,5},{8,14},{9,15},{10,... | collective-permute-start | bytes 811016 | tf_op jit(solution)/shard_map/ppermute | solution.py:345
  22.1 15.2 %collective-permute-start.6 = (f16[528,256]{1,0:T(8,128)(2,1)S(1)}, f16[528,256]{1,0:T(8,128)(2,1)S(1)}, u32[]{:S(2)}, u32[]{:S(2)}) collective-permute-start(f16[528,256]{1,0:T(8,128)(2,1)S(1)} %convert_element_type.69), channel_id=1, source_target_pairs={{0,2},{1,3},{2,4},{3,5},{4,6},{5,7},{6,0},{7,1},{8,10},{9,11},{10,... | collective-permute-start | bytes 811016 | tf_op jit(solution)/shard_map/ppermute | solution.py:345
  31.9 7.0 %collective-permute-start.4 = (f16[528,256]{1,0:T(8,128)(2,1)S(1)}, f16[528,256]{1,0:T(8,128)(2,1)S(1)}, u32[]{:S(2)}, u32[]{:S(2)}) collective-permute-start(f16[528,256]{1,0:T(8,128)(2,1)S(1)} %convert_element_type.65), channel_id=1, source_target_pairs={{0,2},{1,3},{2,4},{3,5},{4,6},{5,7},{6,0},{7,1},{8,10},{9,11},{10,... | collective-permute-start | bytes 811016 | tf_op jit(solution)/shard_map/ppermute | solution.py:345
  32.1 9.9 %collective-permute-start.7 = (f16[528,256]{1,0:T(8,128)(2,1)S(1)}, f16[528,256]{1,0:T(8,128)(2,1)S(1)}, u32[]{:S(2)}, u32[]{:S(2)}) collective-permute-start(f16[528,256]{1,0:T(8,128)(2,1)S(1)} %convert_element_type.71), channel_id=1, source_target_pairs={{0,6},{1,7},{2,0},{3,1},{4,2},{5,3},{6,4},{7,5},{8,14},{9,15},{10,... | collective-permute-start | bytes 811016 | tf_op jit(solution)/shard_map/ppermute | solution.py:345
  44.7 5.4 %collective-permute-start.10 = (f32[32,256]{1,0:T(8,128)S(1)}, f32[32,256]{1,0:T(8,128)S(1)}, u32[]{:S(2)}, u32[]{:S(2)}) collective-permute-start(f32[32,256]{1,0:T(8,128)S(1)} %get-tuple-element.50), channel_id=1, source_target_pairs={{0,8},{8,16},{16,24},{24,0},{32,40},{40,48},{48,56},{56,32},{64,72... | collective-permute-start | bytes 98312 | tf_op jit(solution)/shard_map/ppermute | solution.py:349
  45.0 5.1 %collective-permute-start.11 = (f32[32,256]{1,0:T(8,128)S(1)}, f32[32,256]{1,0:T(8,128)S(1)}, u32[]{:S(2)}, u32[]{:S(2)}) collective-permute-start(f32[32,256]{1,0:T(8,128)S(1)} %get-tuple-element.49), channel_id=1, source_target_pairs={{0,24},{8,0},{16,8},{24,16},{32,56},{40,32},{48,40},{56,48},{64,88... | collective-permute-start | bytes 98312 | tf_op jit(solution)/shard_map/ppermute | solution.py:349
  48.2 5.4 %collective-permute-start.9 = (f32[32,256]{1,0:T(8,128)S(1)}, f32[32,256]{1,0:T(8,128)S(1)}, u32[]{:S(2)}, u32[]{:S(2)}) collective-permute-start(f32[32,256]{1,0:T(8,128)S(1)} %get-tuple-element.48), channel_id=1, source_target_pairs={{0,16},{8,24},{16,0},{24,8},{32,48},{40,56},{48,32},{56,40},{64,80... | collective-permute-start | bytes 98312 | tf_op jit(solution)/shard_map/ppermute | solution.py:349
  53.7 9.8 %collective-permute-start.13 = (f32[32,256]{1,0:T(8,128)S(1)}, f32[32,256]{1,0:T(8,128)S(1)}, u32[]{:S(2)}, u32[]{:S(2)}) collective-permute-start(f32[32,256]{1,0:T(8,128)S(1)} %add_add_fusion.2), channel_id=1, source_target_pairs={{0,64},{8,72},{16,80},{24,88},{32,96},{40,104},{48,112},{56,120},{... | collective-permute-start | bytes 98312 | tf_op jit(solution)/shard_map/ppermute | solution.py:355
  55.4 8.1 %collective-permute-start.14 = (f32[32,256]{1,0:T(8,128)S(1)}, f32[32,256]{1,0:T(8,128)S(1)}, u32[]{:S(2)}, u32[]{:S(2)}) collective-permute-start(f32[32,256]{1,0:T(8,128)S(1)} %add_add_fusion.2), channel_id=1, source_target_pairs={{0,192},{8,200},{16,208},{24,216},{32,224},{40,232},{48,240},{56,2... | collective-permute-start | bytes 98312 | tf_op jit(solution)/shard_map/ppermute | solution.py:355
  58.5 7.8 %collective-permute-start.12 = (f32[32,256]{1,0:T(8,128)S(1)}, f32[32,256]{1,0:T(8,128)S(1)}, u32[]{:S(2)}, u32[]{:S(2)}) collective-permute-start(f32[32,256]{1,0:T(8,128)S(1)} %add_add_fusion.2), channel_id=1, source_target_pairs={{0,128},{8,136},{16,144},{24,152},{32,160},{40,168},{48,176},{56,1... | collective-permute-start | bytes 98312 | tf_op jit(solution)/shard_map/ppermute | solution.py:355
  66.3 4.0 %collective-permute-start.15 = (f32[32,256]{1,0:T(8,128)S(1)}, f32[32,256]{1,0:T(8,128)S(1)}, u32[]{:S(2)}, u32[]{:S(2)}) collective-permute-start(f32[32,256]{1,0:T(8,128)S(1)} %add_add_fusion.1), channel_id=1, source_target_pairs={{0,32},{8,40},{16,48},{24,56},{32,0},{40,8},{48,16},{56,24},{64,96... | collective-permute-start | bytes 98312 | tf_op jit(solution)/shard_map/ppermute | solution.py:377
  70.3 4.6 %collective-permute-start.17 = (f32[32,256]{1,0:T(8,128)S(1)}, f32[32,256]{1,0:T(8,128)S(1)}, u32[]{:S(2)}, u32[]{:S(2)}) collective-permute-start(f32[32,256]{1,0:T(8,128)S(1)} %add.110), channel_id=1, source_target_pairs={{0,2},{1,3},{2,4},{3,5},{4,6},{5,7},{6,0},{7,1},{8,10},{9,11},{10,... | collective-permute-start | bytes 98312 | tf_op jit(solution)/shard_map/ppermute | solution.py:345
  71.6 5.1 %collective-permute-start.18 = (f32[32,256]{1,0:T(8,128)S(1)}, f32[32,256]{1,0:T(8,128)S(1)}, u32[]{:S(2)}, u32[]{:S(2)}) collective-permute-start(f32[32,256]{1,0:T(8,128)S(1)} %add.110), channel_id=1, source_target_pairs={{0,6},{1,7},{2,0},{3,1},{4,2},{5,3},{6,4},{7,5},{8,14},{9,15},{10,... | collective-permute-start | bytes 98312 | tf_op jit(solution)/shard_map/ppermute | solution.py:345
  72.4 5.4 %collective-permute-start.16 = (f32[32,256]{1,0:T(8,128)S(1)}, f32[32,256]{1,0:T(8,128)S(1)}, u32[]{:S(2)}, u32[]{:S(2)}) collective-permute-start(f32[32,256]{1,0:T(8,128)S(1)} %add.110), channel_id=1, source_target_pairs={{0,4},{1,5},{2,6},{3,7},{4,0},{5,1},{6,2},{7,3},{8,12},{9,13},{10,... | collective-permute-start | bytes 98312 | tf_op jit(solution)/shard_map/ppermute | solution.py:345
  77.8 4.0 %collective-permute-start.19 = (f32[32,256]{1,0:T(8,128)S(1)}, f32[32,256]{1,0:T(8,128)S(1)}, u32[]{:S(2)}, u32[]{:S(2)}) collective-permute-start(f32[32,256]{1,0:T(8,128)S(1)} %get-tuple-element.45), channel_id=1, source_target_pairs={{0,24},{8,0},{16,8},{24,16},{32,56},{40,32},{48,40},{56,48},{64,88... | collective-permute-start | bytes 98312 | tf_op jit(solution)/shard_map/ppermute | solution.py:349
  80.1 5.4 %collective-permute-start.20 = (f32[32,256]{1,0:T(8,128)S(1)}, f32[32,256]{1,0:T(8,128)S(1)}, u32[]{:S(2)}, u32[]{:S(2)}) collective-permute-start(f32[32,256]{1,0:T(8,128)S(1)} %get-tuple-element.45), channel_id=1, source_target_pairs={{0,16},{8,24},{16,0},{24,8},{32,48},{40,56},{48,32},{56,40},{64,80... | collective-permute-start | bytes 98312 | tf_op jit(solution)/shard_map/ppermute | solution.py:349
  80.9 5.1 %collective-permute-start.21 = (f32[32,256]{1,0:T(8,128)S(1)}, f32[32,256]{1,0:T(8,128)S(1)}, u32[]{:S(2)}, u32[]{:S(2)}) collective-permute-start(f32[32,256]{1,0:T(8,128)S(1)} %get-tuple-element.45), channel_id=1, source_target_pairs={{0,8},{8,16},{16,24},{24,0},{32,40},{40,48},{48,56},{56,32},{64,72... | collective-permute-start | bytes 98312 | tf_op jit(solution)/shard_map/ppermute | solution.py:349
  86.1 1.7 %collective-permute-start.22 = (f32[128,256]{1,0:T(8,128)S(1)}, f32[128,256]{1,0:T(8,128)S(1)}, u32[]{:S(2)}, u32[]{:S(2)}) collective-permute-start(f32[128,256]{1,0:T(8,128)S(1)} %constant_dynamic-slice_fusion), channel_id=1, source_target_pairs={{0,1},{1,0},{2,3},{3,2},{4,5},{5,4},{6,7},{7,6},{8,9},{9,8},{10,11... | collective-permute-start | bytes 393224 | tf_op jit(solution)/shard_map/ppermute | solution.py:341
  102.6 23.5 %all-to-all-start = ((f16[32,8,768]{2,1,0:T(8,128)(2,1)}), f16[32,8,768]{2,1,0:T(8,128)(2,1)S(1)}, u32[]{:S(2)}, u32[]{:S(2)}) async-start(f16[32,8,768]{2,1,0:T(8,128)(2,1)} %convert_bitcast_fusion), calls=%async_computation | async-start | bytes 786432 | tf_op jit(solution)/shard_map/all_to_all | solution.py:413
  (1 other events, 1.4 us)
Sparse Core Ops, SparseCore 0:
  43.4 34.6 all-gather.2

commit v3 on v2

--- a/solution.py
+++ b/solution.py
@@ -60,99 +60,6 @@
     return jnp.concatenate(done, axis=0)[:, b : 2 * b]
 
 
-def factor_kernel(
-    b, n, g_ref, sketch_ref, slab_ref, t_ref, p_ref, m_ref, y_ref, s_ref, x_ref, sems
-):
-    count, _, rows = sketch_ref.shape
-    copies = []
-    for i in range(count):
-        held = pl.ds(i * rows, rows)
-        copies.append(
-            (
-                pltpu.make_async_copy(sketch_ref.at[i], s_ref.at[i], sems.at[0, i]),
-                pltpu.make_async_copy(slab_ref.at[held], x_ref.at[held], sems.at[1, i]),
-            )
-        )
-        for copy in copies[-1]:
-            copy.start()
-    m_ref[:, 0:n] = g_ref[...]
-    ri = lax.broadcasted_iota(jnp.int32, (n, n), 0)
-    ci = lax.broadcasted_iota(jnp.int32, (n, n), 1)
-    m_ref[:, n : 2 * n] = jnp.where(ri == ci, 1.0, 0.0)
-    steps = n // b
-    for s in range(0, n, b):
-        mine = range(s // b * count // steps, (s // b + 1) * count // steps)
-        for i in mine:
-            for copy in copies[i]:
-                copy.wait()
-        value = None if s == 0 else y_ref[...]
-        for i in mine:
-            term = jnp.dot(
-                s_ref[i], x_ref[i * rows : (i + 1) * rows, :], preferred_element_type=f32
-            )
-            value = term if value is None else value + term
-        y_ref[...] = value
-        inverse = factor_diagonal(m_ref[s : s + b, s : s + b], b)
-        rows_now = jnp.dot(
-            inverse, m_ref[s : s + b, :], precision=HI, preferred_element_type=f32
-        )
-        rr = lax.broadcasted_iota(jnp.int32, (b, n), 0)
-        cc = lax.broadcasted_iota(jnp.int32, (b, n), 1)
-        left = jnp.where(cc >= rr + s, rows_now[:, 0:n], 0.0)
-        right = rows_now[:, n : 2 * n]
-        t_ref[s : s + b, :] = left
-        if s + b < n:
-            update = lax.dot_general(
-                left,
-                jnp.concatenate([left, right], axis=1),
-                (((0,), (0,)), ((), ())),
-                precision=HI,
-                preferred_element_type=f32,
-            )
-            m_ref[s + b : n, :] = m_ref[s + b : n, :] - update[s + b : n, :]
-        m_ref[s : s + b, n : 2 * n] = right
-    value = jnp.dot(
-        m_ref[:, n : 2 * n], y_ref[...], precision=HI, preferred_element_type=f32
-    )
-    d = value.shape[1]
-    value, e = coded(value)
-    p_ref[:, 0:d] = value
-    p_ref[:, d : d + 128] = jnp.broadcast_to(e, (n, 128))
-
-
-def factor_and_project(gram, sketch, slab, b=64):
-    n = gram.shape[0]
-    rows, d = slab.shape
-    vmem = pl.BlockSpec(memory_space=pltpu.VMEM)
-    far = pl.BlockSpec(memory_space=pl.ANY)
-    return pl.pallas_call(
-        functools.partial(factor_kernel, b, n),
-        out_shape=(
-            jax.ShapeDtypeStruct((n, n), f32),
-            jax.ShapeDtypeStruct((n, d + 128), f32),
-        ),
-        in_specs=[vmem, far, far],
-        out_specs=(vmem, vmem),
-        scratch_shapes=[
-            pltpu.VMEM((n, 2 * n), f32),
-            pltpu.VMEM((n, d), f32),
-            pltpu.VMEM(sketch.shape, sketch.dtype),
-            pltpu.VMEM((rows, d), slab.dtype),
-            pltpu.SemaphoreType.DMA((2, sketch.shape[0])),
-        ],
-        compiler_params=pltpu.CompilerParams(vmem_limit_bytes=40 << 20),
-        cost_estimate=pl.CostEstimate(
-            flops=12 * n**3 + 2 * rows * n * d,
-            bytes_accessed=12 * n * n + 2 * rows * (n + d),
-            transcendentals=n,
-        ),
-    )(
-        gram,
-        pltpu.with_memory_space_constraint(sketch, pltpu.HBM),
-        pltpu.with_memory_space_constraint(slab, pltpu.HBM),
-    )
-
-
 ROWS_AT_ONCE = 512
 VMEM_LIMIT = 24 << 20
 
@@ -174,9 +81,8 @@
     return ref[0:n, :] * jnp.exp2(ref[n : n + 1, :] - 14.0)
 
 
-FAR = ((2, 0), (2, 1))
-NEAR = ((1, 1), (3, 0), (1, 0), (3, 1))
-HERE = ((0, 0), (0, 1))
+FIRST = ((2, 0), (2, 1), (1, 1), (3, 0))
+SECOND = ((1, 0), (3, 1), (0, 0), (0, 1))
 
 
 def piece(ring, core, s, h):
@@ -185,10 +91,10 @@
 
 
 def load_kernel(
-    place_ref, slab_ref, basis_ref, held_ref, held_basis_ref, first_ref, here_ref, sems
+    place_ref, slab_ref, basis_ref, held_ref, held_basis_ref, first_ref, second_ref, sems
 ):
     ring, core = place_ref[0], place_ref[1]
-    pieces = [(c, s, h) for c in (1 - core, core) for s, h in FAR + NEAR + HERE]
+    pieces = [(c, s, h) for c in (1 - core, core) for s, h in FIRST + SECOND]
     copies = [pltpu.make_async_copy(basis_ref, held_basis_ref, sems.at[len(pieces)])]
     copies[0].start()
     for i, (c, s, h) in enumerate(pieces):
@@ -197,8 +103,8 @@
         copies[-1].start()
     copies.pop(0).wait()
     size = ROWS_AT_ONCE + 16
-    outs = [first_ref.at[i * size : (i + 1) * size] for i in range(len(FAR + NEAR))]
-    outs += [here_ref.at[i * size : (i + 1) * size] for i in range(len(HERE))]
+    outs = [first_ref.at[i * size : (i + 1) * size] for i in range(len(FIRST))]
+    outs += [second_ref.at[i * size : (i + 1) * size] for i in range(len(SECOND))]
     for i in range(0, len(outs), 2):
         for copy in copies[i : i + 2]:
             copy.wait()
@@ -223,8 +129,8 @@
         out_shape=(
             pltpu.VMEM((rows, d), slab.dtype),
             pltpu.VMEM((d, k), basis.dtype),
-            jax.ShapeDtypeStruct((len(FAR + NEAR) * size, k), f32),
-            jax.ShapeDtypeStruct((len(HERE) * size, k), f32),
+            jax.ShapeDtypeStruct((len(FIRST) * size, k), f32),
+            jax.ShapeDtypeStruct((len(SECOND) * size, k), f32),
         ),
         in_specs=[pl.BlockSpec(memory_space=pltpu.SMEM), far, far],
         out_specs=(vmem,) * 4,
@@ -302,14 +208,13 @@
 def gram_kernel(a_ref, b_ref, c_ref, d_ref, e_ref, f_ref, gram_ref, half_ref):
     n = gram_ref.shape[0]
     total = None
-    b = a_ref.shape[0]
     for i, (own, first, second) in enumerate(
         ((a_ref, b_ref, c_ref), (d_ref, e_ref, f_ref))
     ):
         s = (own[...] + read_coded(first) + read_coded(second)).T
         top = s.astype(jnp.bfloat16)
         rest = (s - top.astype(f32)).astype(jnp.bfloat16)
-        half_ref[:, i * b : (i + 1) * b] = top
+        half_ref[i] = top
         both = jnp.concatenate([top, rest], axis=0)
         g = lax.dot_general(
             both, both, (((1,), (1,)), ((), ())), preferred_element_type=f32
@@ -326,7 +231,7 @@
         gram_kernel,
         out_shape=(
             jax.ShapeDtypeStruct((k, k), f32),
-            jax.ShapeDtypeStruct((k, 2 * rows), jnp.bfloat16),
+            jax.ShapeDtypeStruct((2, k, rows), jnp.bfloat16),
         ),
         in_specs=[vmem] * 6,
         out_specs=(vmem, vmem),
@@ -337,6 +242,102 @@
     )(*low, *high)
 
 
+def factor_kernel(b, n, total_rows, place_ref, slab_ref, *refs):
+    parts, halves, refs = refs[:2], refs[2:12], refs[12:]
+    t_ref, p_ref, m_ref, y_ref, x_ref, sems = refs
+    ring, core = place_ref[0], place_ref[1]
+    sketch = []
+    for c, (own, up, down, low, high) in ((core, halves[:5]), (1 - core, halves[5:])):
+        for s, ref in ((0, own), (3, up), (1, down)):
+            sketch += [(s, c, 0, ref.at[0]), (s, c, 1, ref.at[1])]
+        sketch += [(2, c, 0, low), (2, c, 1, high)]
+    count, rows = len(sketch), ROWS_AT_ONCE
+    copies = []
+    for i, (s, c, h, _) in enumerate(sketch):
+        copies.append(
+            pltpu.make_async_copy(slab_ref.at[piece(ring, c, s, h)], x_ref.at[i], sems.at[i])
+        )
+        copies[-1].start()
+    size = n // 8
+    for c, ref in zip((core, 1 - core), parts):
+        for i in range(4):
+            start = (c * 4 + (place_ref[2] + i) % 4) * size
+            m_ref[pl.ds(pl.multiple_of(start, size), size), 0:n] = ref[
+                i * size : (i + 1) * size, :
+            ]
+    ri = lax.broadcasted_iota(jnp.int32, (n, n), 0)
+    ci = lax.broadcasted_iota(jnp.int32, (n, n), 1)
+    m_ref[:, n : 2 * n] = jnp.where(ri == ci, 1.0, 0.0)
+    steps = n // b
+    for s in range(0, n, b):
+        mine = range(s // b * count // steps, (s // b + 1) * count // steps)
+        for i in mine:
+            copies[i].wait()
+        value = None if s == 0 else y_ref[...]
+        for i in mine:
+            term = jnp.dot(sketch[i][3][...], x_ref[i], preferred_element_type=f32)
+            value = term if value is None else value + term
+        y_ref[...] = value
+        inverse = factor_diagonal(m_ref[s : s + b, s : s + b], b)
+        rows_now = jnp.dot(
+            inverse, m_ref[s : s + b, :], precision=HI, preferred_element_type=f32
+        )
+        rr = lax.broadcasted_iota(jnp.int32, (b, n), 0)
+        cc = lax.broadcasted_iota(jnp.int32, (b, n), 1)
+        left = jnp.where(cc >= rr + s, rows_now[:, 0:n], 0.0)
+        right = rows_now[:, n : 2 * n]
+        t_ref[s : s + b, :] = left / jnp.sqrt(f32(total_rows))
+        if s + b < n:
+            update = lax.dot_general(
+                left,
+                jnp.concatenate([left, right], axis=1),
+                (((0,), (0,)), ((), ())),
+                precision=HI,
+                preferred_element_type=f32,
+            )
+            m_ref[s + b : n, :] = m_ref[s + b : n, :] - update[s + b : n, :]
+        m_ref[s : s + b, n : 2 * n] = right
+    value = jnp.dot(
+        m_ref[:, n : 2 * n], y_ref[...], precision=HI, preferred_element_type=f32
+    )
+    d = value.shape[1]
+    value, e = coded(value)
+    p_ref[:, 0:d] = value
+    p_ref[:, d : d + 128] = jnp.broadcast_to(e, (n, 128))
+
+
+def factor_and_project(gram, halves, slab, place, total_rows, b=64):
+    n = gram[0].shape[1]
+    rows, d = slab.shape
+    count = rows // ROWS_AT_ONCE
+    vmem = pl.BlockSpec(memory_space=pltpu.VMEM)
+    return pl.pallas_call(
+        functools.partial(factor_kernel, b, n, total_rows),
+        out_shape=(
+            jax.ShapeDtypeStruct((n, n), f32),
+            jax.ShapeDtypeStruct((n, d + 128), f32),
+        ),
+        in_specs=[
+            pl.BlockSpec(memory_space=pltpu.SMEM),
+            pl.BlockSpec(memory_space=pl.ANY),
+            *[vmem] * (len(gram) + len(halves)),
+        ],
+        out_specs=(vmem, vmem),
+        scratch_shapes=[
+            pltpu.VMEM((n, 2 * n), f32),
+            pltpu.VMEM((n, d), f32),
+            pltpu.VMEM((count, ROWS_AT_ONCE, d), slab.dtype),
+            pltpu.SemaphoreType.DMA((count,)),
+        ],
+        compiler_params=pltpu.CompilerParams(vmem_limit_bytes=VMEM_LIMIT),
+        cost_estimate=pl.CostEstimate(
+            flops=12 * n**3 + 2 * rows * n * d,
+            bytes_accessed=12 * n * n + 2 * rows * (n + d),
+            transcendentals=n,
+        ),
+    )(place, pltpu.with_memory_space_constraint(slab, pltpu.HBM), *gram, *halves)
+
+
 def shift_core(x):
     return lax.ppermute(x, "width", [(i, i ^ 1) for i in range(8)])
 
@@ -363,10 +364,9 @@
     return lax.dynamic_slice_in_dim(x, index * size, size, 0)
 
 
-def sum_everywhere(x):
+def sum_everywhere(x, beside):
     core = lax.axis_index("width") % 2
     col = lax.axis_index("rows") % 4
-    plane = lax.axis_index("rows") // 4
     half, piece = x.shape[0] // 2, x.shape[0] // 8
     own = block_of(x, core, half) + shift_core(block_of(x, 1 - core, half))
     parts = [block_of(own, (col + k) % 4, piece) for k in range(4)]
@@ -374,32 +374,33 @@
         shift_x(parts[1], 1) + shift_x(parts[3], -1)
     )
     own = sum_of_four(own, shift_z, 2)
+    own, first = lax.optimization_barrier((own, beside(0, None)))
     own = own + lax.ppermute(own, "rows", [(i, i ^ 4) for i in range(32)])
     own = sum_of_four(own, shift_y)
+    own, second = lax.optimization_barrier((own, beside(1, first)))
     ring = [own, shift_x(own, -1), shift_x(own, 2), shift_x(own, 1)]
-    ring = jnp.concatenate(ring + ring, axis=0)
-    own = lax.dynamic_slice_in_dim(ring, (4 - col) % 4 * piece, half, 0)
-    other = shift_core(own)
-    first = jnp.where(core == 0, own, other)
-    second = jnp.where(core == 0, other, own)
-    return jnp.concatenate([first, second], axis=0)
+    own = jnp.concatenate(ring, axis=0)
+    return (own, shift_core(own)), first + second
 
 
 def shards(slab, basis):
     width = lax.axis_index("width")
     total_rows = slab.shape[0] * lax.axis_size("rows")
-    place = jnp.stack([width // 2, width % 2]).astype(jnp.int32)
-
-    held, held_basis, first, here = load_and_sketch(slab, basis, place)
+    place = jnp.stack([width // 2, width % 2, lax.axis_index("rows") % 4]).astype(jnp.int32)
+
+    held, held_basis, first, second = load_and_sketch(slab, basis, place)
     first = shift_core(first.astype(f16))
-    first, here = lax.optimization_barrier((first, here))
-    here = shift_core(here.astype(f16))
-    first = sketch_rows(held, held_basis, place, first.astype(f32), FAR + NEAR, 2)
-    far_up, far_down, near_up, near_down, up, down = first
+    first, second = lax.optimization_barrier((first, second))
+    second = shift_core(second.astype(f16))
+    far_up, far_down, near_up, near_down = sketch_rows(
+        held, held_basis, place, first.astype(f32), FIRST, 0
+    )
     far_up, far_down = shift_y(far_up.astype(f16), 1), shift_y(far_down.astype(f16), -1)
     near_up = shift_y(near_up.astype(f16), 1)
     near_down = shift_y(near_down.astype(f16), -1)
-    low, high = sketch_rows(held, held_basis, place, here.astype(f32), HERE, 2)
+    up, down, low, high = sketch_rows(
+        held, held_basis, place, second.astype(f32), SECOND, 4
+    )
 
     up, down = add_received(up, far_up.astype(f32), down, far_down.astype(f32))
     up, down = shift_y(up.astype(f16), 1), shift_y(down.astype(f16), -1)
@@ -408,13 +409,19 @@
         (high, near_up.astype(f32), down.astype(f32)),
     )
 
-    sketch = lax.all_gather(sketch, "width", axis=0)
-    factor, value = factor_and_project(sum_everywhere(gram), sketch, slab)
+    def gather(step, got):
+        if step == 0:
+            return (shift_y(sketch, 1), shift_y(sketch, -1))
+        return (shift_y(got[0][0], 1), shift_y(got[1][1], -1))
+
+    gram, others = sum_everywhere(gram, gather)
+    halves = (sketch, *others)
+    halves += tuple(shift_core(x) for x in halves)
+    triangle, value = factor_and_project(gram, halves, slab, place, total_rows)
     pieces = lax.all_to_all(value.astype(f16), "rows", 0, 0, tiled=True).reshape(32, 8, -1)
     n = slab.shape[1]
     scale = jnp.exp2(pieces[:, :, n : n + 1].astype(f32) - 14.0)
     projected = jnp.sum(pieces[:, :, :n].astype(f32) * scale, axis=0).T
-    triangle = factor / jnp.sqrt(f32(total_rows))
     return (projected, triangle)
 
 

time: 136 us -> 123 us (0.904)
  blocking collectives: 0 us -> 23.9 us
  waiting for transfers between devices: 53.6 us -> 36.2 us
  between operations: 14.4 us -> 1.04 us
  starting transfers between devices: 38 us -> 34 us
  other arithmetic: 3.59 us -> 2.14 us
    all_to_all x0 -> x1, blocking collectives: none -> 23.9 us  [shards(): lax.all_to_all(value.astype(f16), 'rows', 0, 0, tiled=True)]
    all_to_all x1 -> x0, waiting for transfers between devices: 14.9 us -> none  [shards(): lax.all_to_all(value.astype(f16), 'rows', 0, 0, tiled=True)]
    all_to_all x1 -> x0, starting transfers between devices: 7.85 us -> none  [shards(): lax.all_to_all(value.astype(f16), 'rows', 0, 0, tiled=True)]
    ppermute x9 -> x13, starting transfers between devices: 11.1 us -> 15.9 us  [shift_y(): return lax.ppermute(x, 'width', [(i, (i + 2 * k) % 8) for i in range(8)])]
    ppermute x6, waiting for transfers between devices: 9.49 us -> 11.8 us  [shift_x(): lax.ppermute(x, 'rows', [(i, i // 4 * 4 + (i % 4 + k) % 4) for i in range...]
    ppermute x4 -> x9, waiting for transfers between devices: 6.06 us -> 3.82 us  [shift_core(): return lax.ppermute(x, 'width', [(i, i ^ 1) for i in range(8)])]
    ppermute x1, waiting for transfers between devices: 2.9 us -> 0.68 us  [sum_everywhere(): own = own + lax.ppermute(own, 'rows', [(i, i ^ 4) for i in range(32)])]
    ppermute x6, starting transfers between devices: 7.63 us -> 6.11 us  [shift_x(): lax.ppermute(x, 'rows', [(i, i // 4 * 4 + (i % 4 + k) % 4) for i in range...]
  transfers between devices with their start and end apart: 25 -> 32, of which waited for: 18 -> 17; matrix products, arithmetic and copies ran while one was open for 1% -> 1% of each run, Pallas kernels for 1% -> 3%
where the time goes in v3:
time: 123 us; the launch traced here: 122 us
  waiting for transfers between devices  36.2 us (29%)
  starting transfers between devices  34 us (28%)
  Pallas kernels  24 us (20%)
  blocking collectives  23.9 us (19%)
  other arithmetic  2.14 us (2%)
    all_to_all x1, blocking collectives, shards(): lax.all_to_all(value.astype(f16), 'rows', 0, 0, tiled=True)  23.9 us
    ppermute x13, waiting for transfers between devices, shift_y(): return lax.ppermute(x, 'width', [(i, (i + 2 * k) % 8) for i in range(8)])  17.1 us
    ppermute x13, starting transfers between devices, shift_y(): return lax.ppermute(x, 'width', [(i, (i + 2 * k) % 8) for i in range(8)])  15.9 us
    pallas_call x1, Pallas kernels, factor_and_project(): pl.pallas_call(functools.partial(factor_kernel, b, n, total_rows), out_sh...  14.3 us
    ppermute x6, waiting for transfers between devices, shift_x(): lax.ppermute(x, 'rows', [(i, i // 4 * 4 + (i % 4 + k) % 4) for i in range...  11.8 us
    ppermute x3, starting transfers between devices, shift_z(): return lax.ppermute(x, 'rows', [(i, (i + 4 * k) % 32) for i in range(32)])  9.74 us
    ppermute x6, starting transfers between devices, shift_x(): lax.ppermute(x, 'rows', [(i, i // 4 * 4 + (i % 4 + k) % 4) for i in range...  6.11 us
    pallas_call x1, Pallas kernels, load_and_sketch(): pl.pallas_call(load_kernel, out_shape=(pltpu.VMEM((rows, d), slab.dtype),...  5.21 us
  transfers between devices with their start and end apart: 32, of which 17 were waited for; matrix products, arithmetic and copies ran while one was open for 1% of the time, Pallas kernels for 3%

profile of v3, /device:TPU:24, one launch (start us, length us, event | category | flops | bytes accessed | tf_op | source)
XLA Modules:
  0.0 121.6 jit_solution(1911224693804638214)
XLA Ops:
  0.7 5.2 %shard_map.41 = (bf16[8192,640]{1,0:T(8,128)(2,1)S(1)}, bf16[640,256]{1,0:T(8,128)(2,1)S(1)}, f32[2112,256]{1,0:T(8,128)S(1)}, f32[2112,256]{1,0:T(8,128)S(1)}) custom-call(s32[3]{0:T(128)S(1)} %pad_add_fusion.place_ref, bf16[8192,640]{1,0:T(8,128)(2,1)} %slab_ref.3, bf16[640,256]{1,0:T(8,128)(2,1)} %basis_ref.1), custom_call_target="tpu_custom_call" | custom-call | flops 1342177280 | bytes 18874368 | tf_op jit(solution)/shard_map/pallas_call | solution.py:127
  6.3 2.7 %collective-permute-done = f16[2112,256]{1,0:T(8,128)(2,1)S(1)} collective-permute-done((f16[2112,256]{1,0:T(8,128)(2,1)S(1)}, f16[2112,256]{1,0:T(8,128)(2,1)S(1)}, u32[]{:S(2)}, u32[]{:S(2)}) %collective-permute-start) | collective-permute-done | bytes 1081376 | tf_op jit(solution)/shard_map/ppermute | solution.py:342
  9.6 1.8 %shard_map.43 = (f32[528,256]{1,0:T(8,128)S(1)}, f32[528,256]{1,0:T(8,128)S(1)}, f32[528,256]{1,0:T(8,128)S(1)}, f32[528,256]{1,0:T(8,128)S(1)}) custom-call(s32[3]{0:T(128)S(1)} %pad_add_fusion.place_ref, bf16[8192,640]{1,0:T(8,128)(2,1)S(1)} %get-tuple-element.28.slab_ref, bf16[640,256]{1,0:T(8,128)(2,1)S(1)} %get-tuple-element.29.basis_ref, ...), custom_call_target="tpu_custom_call" | custom-call | flops 671088640 | bytes 6815744 | tf_op jit(solution)/shard_map/pallas_call | solution.py:167
  11.4 2.0 %collective-permute-start.2 = (f16[528,256]{1,0:T(8,128)(2,1)S(1)}, f16[528,256]{1,0:T(8,128)(2,1)S(1)}, u32[]{:S(2)}, u32[]{:S(2)}) collective-permute-start(f16[528,256]{1,0:T(8,128)(2,1)S(1)} %convert_element_type.61), channel_id=1, source_target_pairs={{0,2},{1,3},{2,4},{3,5},{4,6},{5,7},{6,0},{7,1},{8,10},{9,11},{10,... | collective-permute-start | bytes 811016 | tf_op jit(solution)/shard_map/ppermute | solution.py:346
  14.5 2.6 %collective-permute-start.6 = (f16[528,256]{1,0:T(8,128)(2,1)S(1)}, f16[528,256]{1,0:T(8,128)(2,1)S(1)}, u32[]{:S(2)}, u32[]{:S(2)}) collective-permute-start(f16[528,256]{1,0:T(8,128)(2,1)S(1)} %convert_element_type.69), channel_id=1, source_target_pairs={{0,2},{1,3},{2,4},{3,5},{4,6},{5,7},{6,0},{7,1},{8,10},{9,11},{10,... | collective-permute-start | bytes 811016 | tf_op jit(solution)/shard_map/ppermute | solution.py:346
  17.1 3.7 %collective-permute-done.2 = f16[528,256]{1,0:T(8,128)(2,1)S(1)} collective-permute-done((f16[528,256]{1,0:T(8,128)(2,1)S(1)}, f16[528,256]{1,0:T(8,128)(2,1)S(1)}, u32[]{:S(2)}, u32[]{:S(2)}) %collective-permute-start.2) | collective-permute-done | bytes 270368 | tf_op jit(solution)/shard_map/ppermute | solution.py:346
  20.8 3.3 %collective-permute-done.3 = f16[528,256]{1,0:T(8,128)(2,1)S(1)} collective-permute-done((f16[528,256]{1,0:T(8,128)(2,1)S(1)}, f16[528,256]{1,0:T(8,128)(2,1)S(1)}, u32[]{:S(2)}, u32[]{:S(2)}) %collective-permute-start.3) | collective-permute-done | bytes 270368 | tf_op jit(solution)/shard_map/ppermute | solution.py:346
  26.4 2.1 %collective-permute-start.7 = (f16[528,256]{1,0:T(8,128)(2,1)S(1)}, f16[528,256]{1,0:T(8,128)(2,1)S(1)}, u32[]{:S(2)}, u32[]{:S(2)}) collective-permute-start(f16[528,256]{1,0:T(8,128)(2,1)S(1)} %convert_element_type.71), channel_id=1, source_target_pairs={{0,6},{1,7},{2,0},{3,1},{4,2},{5,3},{6,4},{7,5},{8,14},{9,15},{10,... | collective-permute-start | bytes 811016 | tf_op jit(solution)/shard_map/ppermute | solution.py:346
  29.2 3.9 %collective-permute-done.4 = f16[528,256]{1,0:T(8,128)(2,1)S(1)} collective-permute-done((f16[528,256]{1,0:T(8,128)(2,1)S(1)}, f16[528,256]{1,0:T(8,128)(2,1)S(1)}, u32[]{:S(2)}, u32[]{:S(2)}) %collective-permute-start.4) | collective-permute-done | bytes 270368 | tf_op jit(solution)/shard_map/ppermute | solution.py:346
  33.1 1.7 %collective-permute-done.7 = f16[528,256]{1,0:T(8,128)(2,1)S(1)} collective-permute-done((f16[528,256]{1,0:T(8,128)(2,1)S(1)}, f16[528,256]{1,0:T(8,128)(2,1)S(1)}, u32[]{:S(2)}, u32[]{:S(2)}) %collective-permute-start.7) | collective-permute-done | bytes 270368 | tf_op jit(solution)/shard_map/ppermute | solution.py:346
  36.4 1.8 %collective-permute-start.16 = (bf16[2,256,512]{2,1,0:T(8,128)(2,1)S(1)}, bf16[2,256,512]{2,1,0:T(8,128)(2,1)S(1)}, u32[]{:S(2)}, u32[]{:S(2)}) collective-permute-start(bf16[2,256,512]{2,1,0:T(8,128)(2,1)S(1)} %get-tuple-element.45.refs_2_), channel_id=1, source_target_pairs={{0,6},{1,7},{2,0},{3,1},{4,2},{5,3},{6,4},{7,5},{8,14},{9,15},{10,... | collective-permute-start | bytes 1572872 | tf_op jit(solution)/shard_map/ppermute | solution.py:346
  38.4 3.2 %collective-permute-start.11 = (f32[32,256]{1,0:T(8,128)S(1)}, f32[32,256]{1,0:T(8,128)S(1)}, u32[]{:S(2)}, u32[]{:S(2)}) collective-permute-start(f32[32,256]{1,0:T(8,128)S(1)} %get-tuple-element.57), channel_id=1, source_target_pairs={{0,24},{8,0},{16,8},{24,16},{32,56},{40,32},{48,40},{56,48},{64,88... | collective-permute-start | bytes 98312 | tf_op jit(solution)/shard_map/ppermute | solution.py:350
  41.8 1.7 %collective-permute-done.10 = f32[32,256]{1,0:T(8,128)S(1)} collective-permute-done((f32[32,256]{1,0:T(8,128)S(1)}, f32[32,256]{1,0:T(8,128)S(1)}, u32[]{:S(2)}, u32[]{:S(2)}) %collective-permute-start.10) | collective-permute-done | bytes 32800 | tf_op jit(solution)/shard_map/ppermute | solution.py:350
  43.5 3.5 %collective-permute-done.9 = f32[32,256]{1,0:T(8,128)S(1)} collective-permute-done((f32[32,256]{1,0:T(8,128)S(1)}, f32[32,256]{1,0:T(8,128)S(1)}, u32[]{:S(2)}, u32[]{:S(2)}) %collective-permute-start.9) | collective-permute-done | bytes 32800 | tf_op jit(solution)/shard_map/ppermute | solution.py:350
  47.0 1.7 %collective-permute-start.13 = (f32[32,256]{1,0:T(8,128)S(1)}, f32[32,256]{1,0:T(8,128)S(1)}, u32[]{:S(2)}, u32[]{:S(2)}) collective-permute-start(f32[32,256]{1,0:T(8,128)S(1)} %add_add_fusion.2), channel_id=1, source_target_pairs={{0,64},{8,72},{16,80},{24,88},{32,96},{40,104},{48,112},{56,120},{... | collective-permute-start | bytes 98312 | tf_op jit(solution)/shard_map/ppermute | solution.py:356
  48.7 3.1 %collective-permute-start.14 = (f32[32,256]{1,0:T(8,128)S(1)}, f32[32,256]{1,0:T(8,128)S(1)}, u32[]{:S(2)}, u32[]{:S(2)}) collective-permute-start(f32[32,256]{1,0:T(8,128)S(1)} %add_add_fusion.2), channel_id=1, source_target_pairs={{0,192},{8,200},{16,208},{24,216},{32,224},{40,232},{48,240},{56,2... | collective-permute-start | bytes 98312 | tf_op jit(solution)/shard_map/ppermute | solution.py:356
  51.9 4.9 %collective-permute-start.12 = (f32[32,256]{1,0:T(8,128)S(1)}, f32[32,256]{1,0:T(8,128)S(1)}, u32[]{:S(2)}, u32[]{:S(2)}) collective-permute-start(f32[32,256]{1,0:T(8,128)S(1)} %add_add_fusion.2), channel_id=1, source_target_pairs={{0,128},{8,136},{16,144},{24,152},{32,160},{40,168},{48,176},{56,1... | collective-permute-start | bytes 98312 | tf_op jit(solution)/shard_map/ppermute | solution.py:356
  56.8 2.9 %collective-permute-done.12 = f32[32,256]{1,0:T(8,128)S(1)} collective-permute-done((f32[32,256]{1,0:T(8,128)S(1)}, f32[32,256]{1,0:T(8,128)S(1)}, u32[]{:S(2)}, u32[]{:S(2)}) %collective-permute-start.12) | collective-permute-done | bytes 32800 | tf_op jit(solution)/shard_map/ppermute | solution.py:356
  63.7 2.1 %collective-permute-start.19 = (f32[32,256]{1,0:T(8,128)S(1)}, f32[32,256]{1,0:T(8,128)S(1)}, u32[]{:S(2)}, u32[]{:S(2)}) collective-permute-start(f32[32,256]{1,0:T(8,128)S(1)} %add.105), channel_id=1, source_target_pairs={{0,2},{1,3},{2,4},{3,5},{4,6},{5,7},{6,0},{7,1},{8,10},{9,11},{10,... | collective-permute-start | bytes 98312 | tf_op jit(solution)/shard_map/ppermute | solution.py:346
  68.0 3.0 %collective-permute-done.20 = f32[32,256]{1,0:T(8,128)S(1)} collective-permute-done((f32[32,256]{1,0:T(8,128)S(1)}, f32[32,256]{1,0:T(8,128)S(1)}, u32[]{:S(2)}, u32[]{:S(2)}) %collective-permute-start.20) | collective-permute-done | bytes 32800 | tf_op jit(solution)/shard_map/ppermute | solution.py:346
  75.8 2.8 %collective-permute-done.24 = f32[32,256]{1,0:T(8,128)S(1)} collective-permute-done((f32[32,256]{1,0:T(8,128)S(1)}, f32[32,256]{1,0:T(8,128)S(1)}, u32[]{:S(2)}, u32[]{:S(2)}) %collective-permute-start.24) | collective-permute-done | bytes 32800 | tf_op jit(solution)/shard_map/ppermute | solution.py:350
  78.6 2.1 %collective-permute-done.25 = f32[32,256]{1,0:T(8,128)S(1)} collective-permute-done((f32[32,256]{1,0:T(8,128)S(1)}, f32[32,256]{1,0:T(8,128)S(1)}, u32[]{:S(2)}, u32[]{:S(2)}) %collective-permute-start.25) | collective-permute-done | bytes 32800 | tf_op jit(solution)/shard_map/ppermute | solution.py:350
  82.4 14.3 %shard_map.46 = (f32[256,256]{1,0:T(8,128)}, f32[256,768]{1,0:T(8,128)S(1)}) custom-call(s32[3]{0:T(128)S(1)} %pad_add_fusion.place_ref, bf16[8192,640]{1,0:T(8,128)(2,1)} %slab_ref.3, f32[128,256]{1,0:T(8,128)S(1)} %constant_dynamic-update-slice_fusion.refs_0_, f32[128,256]{1,0:T(8,128)S(1)} %collective-permute-done.26.refs_1_, ...), custom_call_target="tpu_custom_call" | custom-call | flops 2885681152 | bytes 15466496 | tf_op jit(solution)/shard_map/pallas_call | solution.py:314
  96.8 23.9 %all_to_all.9 = f16[32,8,768]{2,1,0:T(8,128)(2,1)S(1)} all-to-all(f16[32,8,768]{2,1,0:T(8,128)(2,1)S(1)} %convert_bitcast_fusion), channel_id=1, replica_groups=mesh['rows'=32,'width'=8] {'rows'}, dimensions={0} | all-to-all | bytes 786432 | tf_op jit(solution)/shard_map/all_to_all | solution.py:421
  (83 shorter events, 20.6 us)
Async XLA Ops:
  9.2 15.0 %collective-permute-start.1 = (f16[2112,256]{1,0:T(8,128)(2,1)S(1)}, f16[2112,256]{1,0:T(8,128)(2,1)S(1)}, u32[]{:S(2)}, u32[]{:S(2)}) collective-permute-start(f16[2112,256]{1,0:T(8,128)(2,1)S(1)} %convert_element_type.58), channel_id=1, source_target_pairs={{0,1},{1,0},{2,3},{3,2},{4,5},{5,4},{6,7},{7,6},{8,9},{9,8},{10,11... | collective-permute-start | bytes 3244040 | tf_op jit(solution)/shard_map/ppermute | solution.py:342
  11.4 9.4 %collective-permute-start.2 = (f16[528,256]{1,0:T(8,128)(2,1)S(1)}, f16[528,256]{1,0:T(8,128)(2,1)S(1)}, u32[]{:S(2)}, u32[]{:S(2)}) collective-permute-start(f16[528,256]{1,0:T(8,128)(2,1)S(1)} %convert_element_type.61), channel_id=1, source_target_pairs={{0,2},{1,3},{2,4},{3,5},{4,6},{5,7},{6,0},{7,1},{8,10},{9,11},{10,... | collective-permute-start | bytes 811016 | tf_op jit(solution)/shard_map/ppermute | solution.py:346
  13.5 10.6 %collective-permute-start.3 = (f16[528,256]{1,0:T(8,128)(2,1)S(1)}, f16[528,256]{1,0:T(8,128)(2,1)S(1)}, u32[]{:S(2)}, u32[]{:S(2)}) collective-permute-start(f16[528,256]{1,0:T(8,128)(2,1)S(1)} %convert_element_type.63), channel_id=1, source_target_pairs={{0,6},{1,7},{2,0},{3,1},{4,2},{5,3},{6,4},{7,5},{8,14},{9,15},{10,... | collective-permute-start | bytes 811016 | tf_op jit(solution)/shard_map/ppermute | solution.py:346
  13.7 15.4 %collective-permute-start.5 = (f16[528,256]{1,0:T(8,128)(2,1)S(1)}, f16[528,256]{1,0:T(8,128)(2,1)S(1)}, u32[]{:S(2)}, u32[]{:S(2)}) collective-permute-start(f16[528,256]{1,0:T(8,128)(2,1)S(1)} %convert_element_type.67), channel_id=1, source_target_pairs={{0,6},{1,7},{2,0},{3,1},{4,2},{5,3},{6,4},{7,5},{8,14},{9,15},{10,... | collective-permute-start | bytes 811016 | tf_op jit(solution)/shard_map/ppermute | solution.py:346
  14.5 14.6 %collective-permute-start.6 = (f16[528,256]{1,0:T(8,128)(2,1)S(1)}, f16[528,256]{1,0:T(8,128)(2,1)S(1)}, u32[]{:S(2)}, u32[]{:S(2)}) collective-permute-start(f16[528,256]{1,0:T(8,128)(2,1)S(1)} %convert_element_type.69), channel_id=1, source_target_pairs={{0,2},{1,3},{2,4},{3,5},{4,6},{5,7},{6,0},{7,1},{8,10},{9,11},{10,... | collective-permute-start | bytes 811016 | tf_op jit(solution)/shard_map/ppermute | solution.py:346
  26.3 6.8 %collective-permute-start.4 = (f16[528,256]{1,0:T(8,128)(2,1)S(1)}, f16[528,256]{1,0:T(8,128)(2,1)S(1)}, u32[]{:S(2)}, u32[]{:S(2)}) collective-permute-start(f16[528,256]{1,0:T(8,128)(2,1)S(1)} %convert_element_type.65), channel_id=1, source_target_pairs={{0,2},{1,3},{2,4},{3,5},{4,6},{5,7},{6,0},{7,1},{8,10},{9,11},{10,... | collective-permute-start | bytes 811016 | tf_op jit(solution)/shard_map/ppermute | solution.py:346
  26.4 8.4 %collective-permute-start.7 = (f16[528,256]{1,0:T(8,128)(2,1)S(1)}, f16[528,256]{1,0:T(8,128)(2,1)S(1)}, u32[]{:S(2)}, u32[]{:S(2)}) collective-permute-start(f16[528,256]{1,0:T(8,128)(2,1)S(1)} %convert_element_type.71), channel_id=1, source_target_pairs={{0,6},{1,7},{2,0},{3,1},{4,2},{5,3},{6,4},{7,5},{8,14},{9,15},{10,... | collective-permute-start | bytes 811016 | tf_op jit(solution)/shard_map/ppermute | solution.py:346
  36.0 23.7 %collective-permute-start.15 = (bf16[2,256,512]{2,1,0:T(8,128)(2,1)S(1)}, bf16[2,256,512]{2,1,0:T(8,128)(2,1)S(1)}, u32[]{:S(2)}, u32[]{:S(2)}) collective-permute-start(bf16[2,256,512]{2,1,0:T(8,128)(2,1)S(1)} %get-tuple-element.45.refs_2_), channel_id=1, source_target_pairs={{0,2},{1,3},{2,4},{3,5},{4,6},{5,7},{6,0},{7,1},{8,10},{9,11},{10,... | collective-permute-start | bytes 1572872 | tf_op jit(solution)/shard_map/ppermute | solution.py:346
  36.4 23.3 %collective-permute-start.16 = (bf16[2,256,512]{2,1,0:T(8,128)(2,1)S(1)}, bf16[2,256,512]{2,1,0:T(8,128)(2,1)S(1)}, u32[]{:S(2)}, u32[]{:S(2)}) collective-permute-start(bf16[2,256,512]{2,1,0:T(8,128)(2,1)S(1)} %get-tuple-element.45.refs_2_), channel_id=1, source_target_pairs={{0,6},{1,7},{2,0},{3,1},{4,2},{5,3},{6,4},{7,5},{8,14},{9,15},{10,... | collective-permute-start | bytes 1572872 | tf_op jit(solution)/shard_map/ppermute | solution.py:346
  38.3 5.2 %collective-permute-start.10 = (f32[32,256]{1,0:T(8,128)S(1)}, f32[32,256]{1,0:T(8,128)S(1)}, u32[]{:S(2)}, u32[]{:S(2)}) collective-permute-start(f32[32,256]{1,0:T(8,128)S(1)} %get-tuple-element.58), channel_id=1, source_target_pairs={{0,8},{8,16},{16,24},{24,0},{32,40},{40,48},{48,56},{56,32},{64,72... | collective-permute-start | bytes 98312 | tf_op jit(solution)/shard_map/ppermute | solution.py:350
  38.4 5.1 %collective-permute-start.11 = (f32[32,256]{1,0:T(8,128)S(1)}, f32[32,256]{1,0:T(8,128)S(1)}, u32[]{:S(2)}, u32[]{:S(2)}) collective-permute-start(f32[32,256]{1,0:T(8,128)S(1)} %get-tuple-element.57), channel_id=1, source_target_pairs={{0,24},{8,0},{16,8},{24,16},{32,56},{40,32},{48,40},{56,48},{64,88... | collective-permute-start | bytes 98312 | tf_op jit(solution)/shard_map/ppermute | solution.py:350
  41.6 5.4 %collective-permute-start.9 = (f32[32,256]{1,0:T(8,128)S(1)}, f32[32,256]{1,0:T(8,128)S(1)}, u32[]{:S(2)}, u32[]{:S(2)}) collective-permute-start(f32[32,256]{1,0:T(8,128)S(1)} %get-tuple-element.56), channel_id=1, source_target_pairs={{0,16},{8,24},{16,0},{24,8},{32,48},{40,56},{48,32},{56,40},{64,80... | collective-permute-start | bytes 98312 | tf_op jit(solution)/shard_map/ppermute | solution.py:350
  47.0 9.7 %collective-permute-start.13 = (f32[32,256]{1,0:T(8,128)S(1)}, f32[32,256]{1,0:T(8,128)S(1)}, u32[]{:S(2)}, u32[]{:S(2)}) collective-permute-start(f32[32,256]{1,0:T(8,128)S(1)} %add_add_fusion.2), channel_id=1, source_target_pairs={{0,64},{8,72},{16,80},{24,88},{32,96},{40,104},{48,112},{56,120},{... | collective-permute-start | bytes 98312 | tf_op jit(solution)/shard_map/ppermute | solution.py:356
  48.7 8.1 %collective-permute-start.14 = (f32[32,256]{1,0:T(8,128)S(1)}, f32[32,256]{1,0:T(8,128)S(1)}, u32[]{:S(2)}, u32[]{:S(2)}) collective-permute-start(f32[32,256]{1,0:T(8,128)S(1)} %add_add_fusion.2), channel_id=1, source_target_pairs={{0,192},{8,200},{16,208},{24,216},{32,224},{40,232},{48,240},{56,2... | collective-permute-start | bytes 98312 | tf_op jit(solution)/shard_map/ppermute | solution.py:356
  51.9 7.8 %collective-permute-start.12 = (f32[32,256]{1,0:T(8,128)S(1)}, f32[32,256]{1,0:T(8,128)S(1)}, u32[]{:S(2)}, u32[]{:S(2)}) collective-permute-start(f32[32,256]{1,0:T(8,128)S(1)} %add_add_fusion.2), channel_id=1, source_target_pairs={{0,128},{8,136},{16,144},{24,152},{32,160},{40,168},{48,176},{56,1... | collective-permute-start | bytes 98312 | tf_op jit(solution)/shard_map/ppermute | solution.py:356
  60.8 10.7 %collective-permute-start.21 = (bf16[256,512]{1,0:T(8,128)(2,1)S(1)}, bf16[256,512]{1,0:T(8,128)(2,1)S(1)}, u32[]{:S(2)}, u32[]{:S(2)}) collective-permute-start(bf16[256,512]{1,0:T(8,128)(2,1)S(1)} %slice_bitcast_fusion.1), channel_id=1, source_target_pairs={{0,2},{1,3},{2,4},{3,5},{4,6},{5,7},{6,0},{7,1},{8,10},{9,11},{10,... | collective-permute-start | bytes 786440 | tf_op jit(solution)/shard_map/ppermute | solution.py:346
  62.4 9.1 %collective-permute-start.22 = (bf16[256,512]{1,0:T(8,128)(2,1)S(1)}, bf16[256,512]{1,0:T(8,128)(2,1)S(1)}, u32[]{:S(2)}, u32[]{:S(2)}) collective-permute-start(bf16[256,512]{1,0:T(8,128)(2,1)S(1)} %slice_bitcast_fusion), channel_id=1, source_target_pairs={{0,6},{1,7},{2,0},{3,1},{4,2},{5,3},{6,4},{7,5},{8,14},{9,15},{10,... | collective-permute-start | bytes 786440 | tf_op jit(solution)/shard_map/ppermute | solution.py:346
  65.8 5.1 %collective-permute-start.20 = (f32[32,256]{1,0:T(8,128)S(1)}, f32[32,256]{1,0:T(8,128)S(1)}, u32[]{:S(2)}, u32[]{:S(2)}) collective-permute-start(f32[32,256]{1,0:T(8,128)S(1)} %add.105), channel_id=1, source_target_pairs={{0,6},{1,7},{2,0},{3,1},{4,2},{5,3},{6,4},{7,5},{8,14},{9,15},{10,... | collective-permute-start | bytes 98312 | tf_op jit(solution)/shard_map/ppermute | solution.py:346
  65.8 5.5 %collective-permute-start.18 = (f32[32,256]{1,0:T(8,128)S(1)}, f32[32,256]{1,0:T(8,128)S(1)}, u32[]{:S(2)}, u32[]{:S(2)}) collective-permute-start(f32[32,256]{1,0:T(8,128)S(1)} %add.105), channel_id=1, source_target_pairs={{0,4},{1,5},{2,6},{3,7},{4,0},{5,1},{6,2},{7,3},{8,12},{9,13},{10,... | collective-permute-start | bytes 98312 | tf_op jit(solution)/shard_map/ppermute | solution.py:346
  68.0 12.7 %collective-permute-start.27 = (bf16[2,256,512]{2,1,0:T(8,128)(2,1)S(1)}, bf16[2,256,512]{2,1,0:T(8,128)(2,1)S(1)}, u32[]{:S(2)}, u32[]{:S(2)}) collective-permute-start(bf16[2,256,512]{2,1,0:T(8,128)(2,1)S(1)} %get-tuple-element.45.refs_2_), channel_id=1, source_target_pairs={{0,1},{1,0},{2,3},{3,2},{4,5},{5,4},{6,7},{7,6},{8,9},{9,8},{10,11... | collective-permute-start | bytes 1572872 | tf_op jit(solution)/shard_map/ppermute | solution.py:342
  71.0 11.4 %collective-permute-start.28 = (bf16[2,256,512]{2,1,0:T(8,128)(2,1)S(1)}, bf16[2,256,512]{2,1,0:T(8,128)(2,1)S(1)}, u32[]{:S(2)}, u32[]{:S(2)}) collective-permute-start(bf16[2,256,512]{2,1,0:T(8,128)(2,1)S(1)} %collective-permute-done.15.refs_3_), channel_id=1, source_target_pairs={{0,1},{1,0},{2,3},{3,2},{4,5},{5,4},{6,7},{7,6},{8,9},{9,8},{10,11... | collective-permute-start | bytes 1572872 | tf_op jit(solution)/shard_map/ppermute | solution.py:342
  71.3 11.1 %collective-permute-start.29 = (bf16[2,256,512]{2,1,0:T(8,128)(2,1)S(1)}, bf16[2,256,512]{2,1,0:T(8,128)(2,1)S(1)}, u32[]{:S(2)}, u32[]{:S(2)}) collective-permute-start(bf16[2,256,512]{2,1,0:T(8,128)(2,1)S(1)} %collective-permute-done.16.refs_4_), channel_id=1, source_target_pairs={{0,1},{1,0},{2,3},{3,2},{4,5},{5,4},{6,7},{7,6},{8,9},{9,8},{10,11... | collective-permute-start | bytes 1572872 | tf_op jit(solution)/shard_map/ppermute | solution.py:342
  73.2 5.4 %collective-permute-start.24 = (f32[32,256]{1,0:T(8,128)S(1)}, f32[32,256]{1,0:T(8,128)S(1)}, u32[]{:S(2)}, u32[]{:S(2)}) collective-permute-start(f32[32,256]{1,0:T(8,128)S(1)} %add_add_fusion), channel_id=1, source_target_pairs={{0,16},{8,24},{16,0},{24,8},{32,48},{40,56},{48,32},{56,40},{64,80... | collective-permute-start | bytes 98312 | tf_op jit(solution)/shard_map/ppermute | solution.py:350
  75.6 5.1 %collective-permute-start.25 = (f32[32,256]{1,0:T(8,128)S(1)}, f32[32,256]{1,0:T(8,128)S(1)}, u32[]{:S(2)}, u32[]{:S(2)}) collective-permute-start(f32[32,256]{1,0:T(8,128)S(1)} %add_add_fusion), channel_id=1, source_target_pairs={{0,8},{8,16},{16,24},{24,0},{32,40},{40,48},{48,56},{56,32},{64,72... | collective-permute-start | bytes 98312 | tf_op jit(solution)/shard_map/ppermute | solution.py:350
  (8 other events, 24.8 us)

commit v4 on v3

--- a/solution.py
+++ b/solution.py
@@ -90,87 +90,101 @@
     return pl.ds(pl.multiple_of(start, ROWS_AT_ONCE), ROWS_AT_ONCE)
 
 
-def load_kernel(
-    place_ref, slab_ref, basis_ref, held_ref, held_basis_ref, first_ref, second_ref, sems
-):
+def load_kernel(pieces, place_ref, slab_ref, basis_ref, held_ref, out_ref, *refs):
     ring, core = place_ref[0], place_ref[1]
-    pieces = [(c, s, h) for c in (1 - core, core) for s, h in FIRST + SECOND]
-    copies = [pltpu.make_async_copy(basis_ref, held_basis_ref, sems.at[len(pieces)])]
-    copies[0].start()
-    for i, (c, s, h) in enumerate(pieces):
-        rows = piece(ring, c, s, h)
-        copies.append(pltpu.make_async_copy(slab_ref.at[rows], held_ref.at[rows], sems.at[i]))
-        copies[-1].start()
-    copies.pop(0).wait()
-    size = ROWS_AT_ONCE + 16
-    outs = [first_ref.at[i * size : (i + 1) * size] for i in range(len(FIRST))]
-    outs += [second_ref.at[i * size : (i + 1) * size] for i in range(len(SECOND))]
-    for i in range(0, len(outs), 2):
-        for copy in copies[i : i + 2]:
-            copy.wait()
-        for out, (c, s, h) in zip(outs[i : i + 2], pieces[i : i + 2]):
+    b, size, count = ROWS_AT_ONCE, ROWS_AT_ONCE + 16, len(pieces)
+    sems = refs[-1]
+    if len(refs) > 1:
+        held_basis_ref = refs[0]
+        basis_copy = pltpu.make_async_copy(basis_ref, held_basis_ref, sems.at[2 * count])
+        basis_copy.start()
+    else:
+        held_basis_ref = basis_ref
+    copies = []
+    for c in (1 - core, core):
+        for s, h in pieces:
+            i = len(copies)
+            copies.append(
+                pltpu.make_async_copy(
+                    slab_ref.at[piece(ring, c, s, h)],
+                    held_ref.at[i * b : (i + 1) * b],
+                    sems.at[i],
+                )
+            )
+            copies[-1].start()
+    if len(refs) > 1:
+        basis_copy.wait()
+    for i in range(0, count, 2):
+        for k in (i, i + 1):
+            copies[k].wait()
+        for k in (i, i + 1):
             x = jnp.dot(
-                held_ref[piece(ring, c, s, h), :],
+                held_ref[k * b : (k + 1) * b, :],
                 held_basis_ref[...],
                 preferred_element_type=f32,
             )
-            write_coded(out, x)
-    for copy in copies[len(outs) :]:
+            write_coded(out_ref.at[k * size : (k + 1) * size], x)
+    for copy in copies[count:]:
         copy.wait()
 
 
-def load_and_sketch(slab, basis, place):
-    rows, d = slab.shape
-    k, size = basis.shape[1], ROWS_AT_ONCE + 16
+def load_and_sketch(slab, basis, place, pieces, load_basis):
+    d, k = basis.shape
+    b, count = ROWS_AT_ONCE, len(pieces)
     vmem = pl.BlockSpec(memory_space=pltpu.VMEM)
     far = pl.BlockSpec(memory_space=pl.ANY)
+    out_shape = [
+        pltpu.VMEM((2 * count * b, d), slab.dtype),
+        jax.ShapeDtypeStruct((count * (b + 16), k), f32),
+    ]
+    if load_basis:
+        out_shape.append(pltpu.VMEM((d, k), basis.dtype))
     return pl.pallas_call(
-        load_kernel,
-        out_shape=(
-            pltpu.VMEM((rows, d), slab.dtype),
-            pltpu.VMEM((d, k), basis.dtype),
-            jax.ShapeDtypeStruct((len(FIRST) * size, k), f32),
-            jax.ShapeDtypeStruct((len(SECOND) * size, k), f32),
-        ),
-        in_specs=[pl.BlockSpec(memory_space=pltpu.SMEM), far, far],
-        out_specs=(vmem,) * 4,
-        scratch_shapes=[pltpu.SemaphoreType.DMA((17,))],
+        functools.partial(load_kernel, pieces),
+        out_shape=out_shape,
+        in_specs=[
+            pl.BlockSpec(memory_space=pltpu.SMEM),
+            far,
+            far if load_basis else vmem,
+        ],
+        out_specs=[vmem] * len(out_shape),
+        scratch_shapes=[pltpu.SemaphoreType.DMA((2 * count + 1,))],
         compiler_params=pltpu.CompilerParams(vmem_limit_bytes=VMEM_LIMIT),
         cost_estimate=pl.CostEstimate(
-            flops=rows * d * k, bytes_accessed=2 * rows * (d + 2 * k), transcendentals=0
+            flops=2 * count * b * d * k,
+            bytes_accessed=count * b * (4 * d + 4 * k),
+            transcendentals=0,
         ),
     )(
         place,
         pltpu.with_memory_space_constraint(slab, pltpu.HBM),
-        pltpu.with_memory_space_constraint(basis, pltpu.HBM),
-    )
-
-
-def sketch_kernel(pieces, place_ref, slab_ref, basis_ref, other_ref, *outs):
-    ring, core = place_ref[0], place_ref[1]
-    b = ROWS_AT_ONCE
-    for i, ((s, h), out) in enumerate(zip(pieces, outs)):
+        pltpu.with_memory_space_constraint(basis, pltpu.HBM if load_basis else pltpu.VMEM),
+    )
+
+
+def sketch_kernel(slab_ref, basis_ref, other_ref, *outs):
+    b, size, count = ROWS_AT_ONCE, ROWS_AT_ONCE + 16, len(outs)
+    for i, out in enumerate(outs):
         x = jnp.dot(
-            slab_ref[piece(ring, core, s, h), :], basis_ref[...], preferred_element_type=f32
+            slab_ref[(count + i) * b : (count + i + 1) * b, :],
+            basis_ref[...],
+            preferred_element_type=f32,
         )
-        x = x + read_coded(other_ref.at[i * (b + 16) : (i + 1) * (b + 16)])
+        x = x + read_coded(other_ref.at[i * size : (i + 1) * size])
         if out.shape[0] == b:
             out[...] = x
         else:
             write_coded(out, x)
 
 
-def sketch_rows(held, basis, place, other, pieces, plain):
+def sketch_rows(held, basis, other, code):
     b, (d, k) = ROWS_AT_ONCE, basis.shape
-    count = len(pieces)
+    count = held.shape[0] // (2 * b)
     vmem = pl.BlockSpec(memory_space=pltpu.VMEM)
     return pl.pallas_call(
-        functools.partial(sketch_kernel, pieces),
-        out_shape=[
-            jax.ShapeDtypeStruct((b + 16 if i < count - plain else b, k), f32)
-            for i in range(count)
-        ],
-        in_specs=[pl.BlockSpec(memory_space=pltpu.SMEM), vmem, vmem, vmem],
+        sketch_kernel,
+        out_shape=[jax.ShapeDtypeStruct((b + 16 if code else b, k), f32)] * count,
+        in_specs=[vmem, vmem, vmem],
         out_specs=[vmem] * count,
         compiler_params=pltpu.CompilerParams(vmem_limit_bytes=VMEM_LIMIT),
         cost_estimate=pl.CostEstimate(
@@ -179,7 +193,6 @@
             transcendentals=0,
         ),
     )(
-        place,
         pltpu.with_memory_space_constraint(held, pltpu.VMEM),
         pltpu.with_memory_space_constraint(basis, pltpu.VMEM),
         other,
@@ -279,15 +292,23 @@
             value = term if value is None else value + term
         y_ref[...] = value
         inverse = factor_diagonal(m_ref[s : s + b, s : s + b], b)
+        lo, hi = s // 128 * 128, -(-(s + b) // 128) * 128
         rows_now = jnp.dot(
-            inverse, m_ref[s : s + b, :], precision=HI, preferred_element_type=f32
+            inverse,
+            m_ref[s : s + b, lo : n + hi],
+            precision=HI,
+            preferred_element_type=f32,
         )
-        rr = lax.broadcasted_iota(jnp.int32, (b, n), 0)
-        cc = lax.broadcasted_iota(jnp.int32, (b, n), 1)
-        left = jnp.where(cc >= rr + s, rows_now[:, 0:n], 0.0)
-        right = rows_now[:, n : 2 * n]
-        t_ref[s : s + b, :] = left / jnp.sqrt(f32(total_rows))
+        rr = lax.broadcasted_iota(jnp.int32, (b, n - lo), 0) + s
+        cc = lax.broadcasted_iota(jnp.int32, (b, n - lo), 1) + lo
+        left = jnp.where(cc >= rr, rows_now[:, 0 : n - lo], 0.0)
+        right = rows_now[:, n - lo :]
+        if lo:
+            t_ref[s : s + b, 0:lo] = jnp.zeros((b, lo), f32)
+        t_ref[s : s + b, lo:n] = left / jnp.sqrt(f32(total_rows))
         if s + b < n:
+            start = (s + b) // 128 * 128
+            left = left[:, start - lo :]
             update = lax.dot_general(
                 left,
                 jnp.concatenate([left, right], axis=1),
@@ -295,8 +316,10 @@
                 precision=HI,
                 preferred_element_type=f32,
             )
-            m_ref[s + b : n, :] = m_ref[s + b : n, :] - update[s + b : n, :]
-        m_ref[s : s + b, n : 2 * n] = right
+            m_ref[s + b : n, start : n + hi] = (
+                m_ref[s + b : n, start : n + hi] - update[s + b - start :, :]
+            )
+        m_ref[s : s + b, n : n + hi] = right
     value = jnp.dot(
         m_ref[:, n : 2 * n], y_ref[...], precision=HI, preferred_element_type=f32
     )
@@ -378,8 +401,8 @@
     own = own + lax.ppermute(own, "rows", [(i, i ^ 4) for i in range(32)])
     own = sum_of_four(own, shift_y)
     own, second = lax.optimization_barrier((own, beside(1, first)))
-    ring = [own, shift_x(own, -1), shift_x(own, 2), shift_x(own, 1)]
-    own = jnp.concatenate(ring, axis=0)
+    ring = (own, shift_x(own, -1), shift_x(own, 2), shift_x(own, 1))
+    own = jnp.concatenate(lax.optimization_barrier(ring), axis=0)
     return (own, shift_core(own)), first + second
 
 
@@ -388,18 +411,19 @@
     total_rows = slab.shape[0] * lax.axis_size("rows")
     place = jnp.stack([width // 2, width % 2, lax.axis_index("rows") % 4]).astype(jnp.int32)
 
-    held, held_basis, first, second = load_and_sketch(slab, basis, place)
+    held_first, first, held_basis = load_and_sketch(slab, basis, place, FIRST, True)
     first = shift_core(first.astype(f16))
+    held_second, second = load_and_sketch(slab, held_basis, place, SECOND, False)
     first, second = lax.optimization_barrier((first, second))
     second = shift_core(second.astype(f16))
     far_up, far_down, near_up, near_down = sketch_rows(
-        held, held_basis, place, first.astype(f32), FIRST, 0
+        held_first, held_basis, first.astype(f32), True
     )
     far_up, far_down = shift_y(far_up.astype(f16), 1), shift_y(far_down.astype(f16), -1)
     near_up = shift_y(near_up.astype(f16), 1)
     near_down = shift_y(near_down.astype(f16), -1)
     up, down, low, high = sketch_rows(
-        held, held_basis, place, second.astype(f32), SECOND, 4
+        held_second, held_basis, second.astype(f32), False
     )
 
     up, down = add_received(up, far_up.astype(f32), down, far_down.astype(f32))

time: 123 us -> 120 us (0.976); the launches traced: 122 us -> 120 us
  waiting for transfers between devices: 36.2 us -> 28.1 us
  starting transfers between devices: 34 us -> 40.4 us
    ppermute x6, waiting for transfers between devices: 11.8 us -> 7.2 us  [shift_x(): lax.ppermute(x, 'rows', [(i, i // 4 * 4 + (i % 4 + k) % 4) for i in range...]
    ppermute x13, starting transfers between devices: 15.9 us -> 19.1 us  [shift_y(): return lax.ppermute(x, 'width', [(i, (i + 2 * k) % 8) for i in range(8)])]
    ppermute x9, waiting for transfers between devices: 3.82 us -> 1.11 us  [shift_core(): return lax.ppermute(x, 'width', [(i, i ^ 1) for i in range(8)])]
    ppermute x6, starting transfers between devices: 6.11 us -> 8.44 us  [shift_x(): lax.ppermute(x, 'rows', [(i, i // 4 * 4 + (i % 4 + k) % 4) for i in range...]
    ppermute x13, waiting for transfers between devices: 17.1 us -> 15.8 us  [shift_y(): return lax.ppermute(x, 'width', [(i, (i + 2 * k) % 8) for i in range(8)])]
    pallas_call x3 -> x4, Pallas kernels: 8.5 us -> 9.26 us  [the longest x2 7.05 us: load_and_sketch(): pl.pallas_call(functools.partial(load_kernel, pieces), out_shape=out_shap...]
  transfers between devices with their start and end apart: 32 -> 32, of which waited for: 17 -> 15; matrix products, arithmetic and copies ran while one was open for 1% -> 1% of each run, Pallas kernels for 3% -> 5%
where the time goes in v4:
time: 120 us
  starting transfers between devices  40.4 us (34%)
  waiting for transfers between devices  28.1 us (23%)
  Pallas kernels  24.3 us (20%)
  blocking collectives  23.6 us (20%)
  other arithmetic  2.07 us (2%)
    all_to_all x1, blocking collectives, shards(): lax.all_to_all(value.astype(f16), 'rows', 0, 0, tiled=True)  23.6 us
    ppermute x13, starting transfers between devices, shift_y(): return lax.ppermute(x, 'width', [(i, (i + 2 * k) % 8) for i in range(8)])  19.1 us
    ppermute x13, waiting for transfers between devices, shift_y(): return lax.ppermute(x, 'width', [(i, (i + 2 * k) % 8) for i in range(8)])  15.8 us
    pallas_call x1, Pallas kernels, factor_and_project(): pl.pallas_call(functools.partial(factor_kernel, b, n, total_rows), out_sh...  13.9 us
    ppermute x3, starting transfers between devices, shift_z(): return lax.ppermute(x, 'rows', [(i, (i + 4 * k) % 32) for i in range(32)])  10.2 us
    ppermute x6, starting transfers between devices, shift_x(): lax.ppermute(x, 'rows', [(i, i // 4 * 4 + (i % 4 + k) % 4) for i in range...  8.44 us
    ppermute x6, waiting for transfers between devices, shift_x(): lax.ppermute(x, 'rows', [(i, i // 4 * 4 + (i % 4 + k) % 4) for i in range...  7.2 us
    pallas_call x2, Pallas kernels, load_and_sketch(): pl.pallas_call(functools.partial(load_kernel, pieces), out_shape=out_shap...  7.05 us
  transfers between devices with their start and end apart: 32, of which 15 were waited for; matrix products, arithmetic and copies ran while one was open for 1% of the time, Pallas kernels for 5%

profile of v4, /device:TPU:24, one launch (start us, length us, event | category | flops | bytes accessed | tf_op | source)
XLA Modules:
  0.0 119.9 jit_solution(2922290651396027521)
XLA Ops:
  0.7 3.6 %shard_map.41 = (bf16[4096,640]{1,0:T(8,128)(2,1)S(1)}, f32[2112,256]{1,0:T(8,128)S(1)}, bf16[640,256]{1,0:T(8,128)(2,1)S(1)}) custom-call(s32[3]{0:T(128)S(1)} %pad_add_fusion.place_ref, bf16[8192,640]{1,0:T(8,128)(2,1)} %slab_ref.5, bf16[640,256]{1,0:T(8,128)(2,1)} %basis_ref.1), custom_call_target="tpu_custom_call" | custom-call | flops 671088640 | bytes 7340032 | tf_op jit(solution)/shard_map/pallas_call | solution.py:142
  4.6 3.5 %shard_map.42 = (bf16[4096,640]{1,0:T(8,128)(2,1)S(1)}, f32[2112,256]{1,0:T(8,128)S(1)}) custom-call(s32[3]{0:T(128)S(1)} %pad_add_fusion.place_ref, bf16[8192,640]{1,0:T(8,128)(2,1)} %slab_ref.5, bf16[640,256]{1,0:T(8,128)(2,1)S(1)} %get-tuple-element.33.basis_ref), custom_call_target="tpu_custom_call" | custom-call | flops 671088640 | bytes 7340032 | tf_op jit(solution)/shard_map/pallas_call | solution.py:142
  11.2 2.6 %collective-permute-start.2 = (f16[528,256]{1,0:T(8,128)(2,1)S(1)}, f16[528,256]{1,0:T(8,128)(2,1)S(1)}, u32[]{:S(2)}, u32[]{:S(2)}) collective-permute-start(f16[528,256]{1,0:T(8,128)(2,1)S(1)} %convert_element_type.61), channel_id=1, source_target_pairs={{0,2},{1,3},{2,4},{3,5},{4,6},{5,7},{6,0},{7,1},{8,10},{9,11},{10,... | collective-permute-start | bytes 811016 | tf_op jit(solution)/shard_map/ppermute | solution.py:369
  14.7 1.3 %collective-permute-start.5 = (f16[528,256]{1,0:T(8,128)(2,1)S(1)}, f16[528,256]{1,0:T(8,128)(2,1)S(1)}, u32[]{:S(2)}, u32[]{:S(2)}) collective-permute-start(f16[528,256]{1,0:T(8,128)(2,1)S(1)} %convert_element_type.67), channel_id=1, source_target_pairs={{0,6},{1,7},{2,0},{3,1},{4,2},{5,3},{6,4},{7,5},{8,14},{9,15},{10,... | collective-permute-start | bytes 811016 | tf_op jit(solution)/shard_map/ppermute | solution.py:369
  16.0 5.0 %collective-permute-done.3 = f16[528,256]{1,0:T(8,128)(2,1)S(1)} collective-permute-done((f16[528,256]{1,0:T(8,128)(2,1)S(1)}, f16[528,256]{1,0:T(8,128)(2,1)S(1)}, u32[]{:S(2)}, u32[]{:S(2)}) %collective-permute-start.3) | collective-permute-done | bytes 270368 | tf_op jit(solution)/shard_map/ppermute | solution.py:369
  22.9 3.2 %collective-permute-start.4 = (f16[528,256]{1,0:T(8,128)(2,1)S(1)}, f16[528,256]{1,0:T(8,128)(2,1)S(1)}, u32[]{:S(2)}, u32[]{:S(2)}) collective-permute-start(f16[528,256]{1,0:T(8,128)(2,1)S(1)} %convert_element_type.65), channel_id=1, source_target_pairs={{0,2},{1,3},{2,4},{3,5},{4,6},{5,7},{6,0},{7,1},{8,10},{9,11},{10,... | collective-permute-start | bytes 811016 | tf_op jit(solution)/shard_map/ppermute | solution.py:369
  26.8 4.8 %collective-permute-done.7 = f16[528,256]{1,0:T(8,128)(2,1)S(1)} collective-permute-done((f16[528,256]{1,0:T(8,128)(2,1)S(1)}, f16[528,256]{1,0:T(8,128)(2,1)S(1)}, u32[]{:S(2)}, u32[]{:S(2)}) %collective-permute-start.7) | collective-permute-done | bytes 270368 | tf_op jit(solution)/shard_map/ppermute | solution.py:369
  33.4 2.9 %collective-permute-start.15 = (bf16[2,256,512]{2,1,0:T(8,128)(2,1)S(1)}, bf16[2,256,512]{2,1,0:T(8,128)(2,1)S(1)}, u32[]{:S(2)}, u32[]{:S(2)}) collective-permute-start(bf16[2,256,512]{2,1,0:T(8,128)(2,1)S(1)} %get-tuple-element.51.refs_2_), channel_id=1, source_target_pairs={{0,2},{1,3},{2,4},{3,5},{4,6},{5,7},{6,0},{7,1},{8,10},{9,11},{10,... | collective-permute-start | bytes 1572872 | tf_op jit(solution)/shard_map/ppermute | solution.py:369
  36.3 3.1 %collective-permute-start.9 = (f32[32,256]{1,0:T(8,128)S(1)}, f32[32,256]{1,0:T(8,128)S(1)}, u32[]{:S(2)}, u32[]{:S(2)}) collective-permute-start(f32[32,256]{1,0:T(8,128)S(1)} %get-tuple-element.66), channel_id=1, source_target_pairs={{0,16},{8,24},{16,0},{24,8},{32,48},{40,56},{48,32},{56,40},{64,80... | collective-permute-start | bytes 98312 | tf_op jit(solution)/shard_map/ppermute | solution.py:373
  41.8 1.5 %collective-permute-done.11 = f32[32,256]{1,0:T(8,128)S(1)} collective-permute-done((f32[32,256]{1,0:T(8,128)S(1)}, f32[32,256]{1,0:T(8,128)S(1)}, u32[]{:S(2)}, u32[]{:S(2)}) %collective-permute-start.11) | collective-permute-done | bytes 32800 | tf_op jit(solution)/shard_map/ppermute | solution.py:373
  43.4 2.4 %collective-permute-done.10 = f32[32,256]{1,0:T(8,128)S(1)} collective-permute-done((f32[32,256]{1,0:T(8,128)S(1)}, f32[32,256]{1,0:T(8,128)S(1)}, u32[]{:S(2)}, u32[]{:S(2)}) %collective-permute-start.10) | collective-permute-done | bytes 32800 | tf_op jit(solution)/shard_map/ppermute | solution.py:373
  45.7 6.4 %collective-permute-start.14 = (f32[32,256]{1,0:T(8,128)S(1)}, f32[32,256]{1,0:T(8,128)S(1)}, u32[]{:S(2)}, u32[]{:S(2)}) collective-permute-start(f32[32,256]{1,0:T(8,128)S(1)} %add_add_fusion.2), channel_id=1, source_target_pairs={{0,192},{8,200},{16,208},{24,216},{32,224},{40,232},{48,240},{56,2... | collective-permute-start | bytes 98312 | tf_op jit(solution)/shard_map/ppermute | solution.py:379
  52.1 3.8 %collective-permute-start.12 = (f32[32,256]{1,0:T(8,128)S(1)}, f32[32,256]{1,0:T(8,128)S(1)}, u32[]{:S(2)}, u32[]{:S(2)}) collective-permute-start(f32[32,256]{1,0:T(8,128)S(1)} %add_add_fusion.2), channel_id=1, source_target_pairs={{0,128},{8,136},{16,144},{24,152},{32,160},{40,168},{48,176},{56,1... | collective-permute-start | bytes 98312 | tf_op jit(solution)/shard_map/ppermute | solution.py:379
  55.9 2.2 %collective-permute-done.13 = f32[32,256]{1,0:T(8,128)S(1)} collective-permute-done((f32[32,256]{1,0:T(8,128)S(1)}, f32[32,256]{1,0:T(8,128)S(1)}, u32[]{:S(2)}, u32[]{:S(2)}) %collective-permute-start.13) | collective-permute-done | bytes 32800 | tf_op jit(solution)/shard_map/ppermute | solution.py:379
  58.1 1.8 %collective-permute-done.12 = f32[32,256]{1,0:T(8,128)S(1)} collective-permute-done((f32[32,256]{1,0:T(8,128)S(1)}, f32[32,256]{1,0:T(8,128)S(1)}, u32[]{:S(2)}, u32[]{:S(2)}) %collective-permute-start.12) | collective-permute-done | bytes 32800 | tf_op jit(solution)/shard_map/ppermute | solution.py:379
  61.2 3.2 %collective-permute-start.21 = (bf16[256,512]{1,0:T(8,128)(2,1)S(1)}, bf16[256,512]{1,0:T(8,128)(2,1)S(1)}, u32[]{:S(2)}, u32[]{:S(2)}) collective-permute-start(bf16[256,512]{1,0:T(8,128)(2,1)S(1)} %slice_bitcast_fusion.1), channel_id=1, source_target_pairs={{0,2},{1,3},{2,4},{3,5},{4,6},{5,7},{6,0},{7,1},{8,10},{9,11},{10,... | collective-permute-start | bytes 786440 | tf_op jit(solution)/shard_map/ppermute | solution.py:369
  64.5 3.2 %collective-permute-start.19 = (f32[32,256]{1,0:T(8,128)S(1)}, f32[32,256]{1,0:T(8,128)S(1)}, u32[]{:S(2)}, u32[]{:S(2)}) collective-permute-start(f32[32,256]{1,0:T(8,128)S(1)} %add.105), channel_id=1, source_target_pairs={{0,2},{1,3},{2,4},{3,5},{4,6},{5,7},{6,0},{7,1},{8,10},{9,11},{10,... | collective-permute-start | bytes 98312 | tf_op jit(solution)/shard_map/ppermute | solution.py:369
  67.8 1.9 %collective-permute-done.20 = f32[32,256]{1,0:T(8,128)S(1)} collective-permute-done((f32[32,256]{1,0:T(8,128)S(1)}, f32[32,256]{1,0:T(8,128)S(1)}, u32[]{:S(2)}, u32[]{:S(2)}) %collective-permute-start.20) | collective-permute-done | bytes 32800 | tf_op jit(solution)/shard_map/ppermute | solution.py:369
  69.6 3.5 %collective-permute-done.18 = f32[32,256]{1,0:T(8,128)S(1)} collective-permute-done((f32[32,256]{1,0:T(8,128)S(1)}, f32[32,256]{1,0:T(8,128)S(1)}, u32[]{:S(2)}, u32[]{:S(2)}) %collective-permute-start.18) | collective-permute-done | bytes 32800 | tf_op jit(solution)/shard_map/ppermute | solution.py:369
  73.3 1.5 %collective-permute-start.24 = (f32[32,256]{1,0:T(8,128)S(1)}, f32[32,256]{1,0:T(8,128)S(1)}, u32[]{:S(2)}, u32[]{:S(2)}) collective-permute-start(f32[32,256]{1,0:T(8,128)S(1)} %add_add_fusion), channel_id=1, source_target_pairs={{0,16},{8,24},{16,0},{24,8},{32,48},{40,56},{48,32},{56,40},{64,80... | collective-permute-start | bytes 98312 | tf_op jit(solution)/shard_map/ppermute | solution.py:373
  74.8 1.8 %collective-permute-start.23 = (f32[32,256]{1,0:T(8,128)S(1)}, f32[32,256]{1,0:T(8,128)S(1)}, u32[]{:S(2)}, u32[]{:S(2)}) collective-permute-start(f32[32,256]{1,0:T(8,128)S(1)} %add_add_fusion), channel_id=1, source_target_pairs={{0,24},{8,0},{16,8},{24,16},{32,56},{40,32},{48,40},{56,48},{64,88... | collective-permute-start | bytes 98312 | tf_op jit(solution)/shard_map/ppermute | solution.py:373
  76.5 1.9 %collective-permute-done.25 = f32[32,256]{1,0:T(8,128)S(1)} collective-permute-done((f32[32,256]{1,0:T(8,128)S(1)}, f32[32,256]{1,0:T(8,128)S(1)}, u32[]{:S(2)}, u32[]{:S(2)}) %collective-permute-start.25) | collective-permute-done | bytes 32800 | tf_op jit(solution)/shard_map/ppermute | solution.py:373
  81.4 13.9 %shard_map.47 = (f32[256,256]{1,0:T(8,128)}, f32[256,768]{1,0:T(8,128)S(1)}) custom-call(s32[3]{0:T(128)S(1)} %pad_add_fusion.place_ref, bf16[8192,640]{1,0:T(8,128)(2,1)} %slab_ref.5, f32[128,256]{1,0:T(8,128)S(1)} %constant_dynamic-update-slice_fusion.refs_0_, f32[128,256]{1,0:T(8,128)S(1)} %collective-permute-done.26.refs_1_, ...), custom_call_target="tpu_custom_call" | custom-call | flops 2885681152 | bytes 15466496 | tf_op jit(solution)/shard_map/pallas_call | solution.py:337
  95.3 23.6 %all_to_all.9 = f16[32,8,768]{2,1,0:T(8,128)(2,1)S(1)} all-to-all(f16[32,8,768]{2,1,0:T(8,128)(2,1)S(1)} %convert_bitcast_fusion), channel_id=1, replica_groups=mesh['rows'=32,'width'=8] {'rows'}, dimensions={0} | all-to-all | bytes 786432 | tf_op jit(solution)/shard_map/all_to_all | solution.py:445
  (84 shorter events, 16.3 us)
Async XLA Ops:
  8.3 12.8 %collective-permute-start.1 = (f16[2112,256]{1,0:T(8,128)(2,1)S(1)}, f16[2112,256]{1,0:T(8,128)(2,1)S(1)}, u32[]{:S(2)}, u32[]{:S(2)}) collective-permute-start(f16[2112,256]{1,0:T(8,128)(2,1)S(1)} %convert_element_type.58), channel_id=1, source_target_pairs={{0,1},{1,0},{2,3},{3,2},{4,5},{5,4},{6,7},{7,6},{8,9},{9,8},{10,11... | collective-permute-start | bytes 3244040 | tf_op jit(solution)/shard_map/ppermute | solution.py:365
  10.3 10.6 %collective-permute-start.3 = (f16[528,256]{1,0:T(8,128)(2,1)S(1)}, f16[528,256]{1,0:T(8,128)(2,1)S(1)}, u32[]{:S(2)}, u32[]{:S(2)}) collective-permute-start(f16[528,256]{1,0:T(8,128)(2,1)S(1)} %convert_element_type.63), channel_id=1, source_target_pairs={{0,6},{1,7},{2,0},{3,1},{4,2},{5,3},{6,4},{7,5},{8,14},{9,15},{10,... | collective-permute-start | bytes 811016 | tf_op jit(solution)/shard_map/ppermute | solution.py:369
  11.2 9.8 %collective-permute-start.2 = (f16[528,256]{1,0:T(8,128)(2,1)S(1)}, f16[528,256]{1,0:T(8,128)(2,1)S(1)}, u32[]{:S(2)}, u32[]{:S(2)}) collective-permute-start(f16[528,256]{1,0:T(8,128)(2,1)S(1)} %convert_element_type.61), channel_id=1, source_target_pairs={{0,2},{1,3},{2,4},{3,5},{4,6},{5,7},{6,0},{7,1},{8,10},{9,11},{10,... | collective-permute-start | bytes 811016 | tf_op jit(solution)/shard_map/ppermute | solution.py:369
  13.9 12.6 %collective-permute-start.6 = (f16[528,256]{1,0:T(8,128)(2,1)S(1)}, f16[528,256]{1,0:T(8,128)(2,1)S(1)}, u32[]{:S(2)}, u32[]{:S(2)}) collective-permute-start(f16[528,256]{1,0:T(8,128)(2,1)S(1)} %convert_element_type.69), channel_id=1, source_target_pairs={{0,2},{1,3},{2,4},{3,5},{4,6},{5,7},{6,0},{7,1},{8,10},{9,11},{10,... | collective-permute-start | bytes 811016 | tf_op jit(solution)/shard_map/ppermute | solution.py:369
  14.7 12.1 %collective-permute-start.5 = (f16[528,256]{1,0:T(8,128)(2,1)S(1)}, f16[528,256]{1,0:T(8,128)(2,1)S(1)}, u32[]{:S(2)}, u32[]{:S(2)}) collective-permute-start(f16[528,256]{1,0:T(8,128)(2,1)S(1)} %convert_element_type.67), channel_id=1, source_target_pairs={{0,6},{1,7},{2,0},{3,1},{4,2},{5,3},{6,4},{7,5},{8,14},{9,15},{10,... | collective-permute-start | bytes 811016 | tf_op jit(solution)/shard_map/ppermute | solution.py:369
  22.6 9.0 %collective-permute-start.7 = (f16[528,256]{1,0:T(8,128)(2,1)S(1)}, f16[528,256]{1,0:T(8,128)(2,1)S(1)}, u32[]{:S(2)}, u32[]{:S(2)}) collective-permute-start(f16[528,256]{1,0:T(8,128)(2,1)S(1)} %convert_element_type.71), channel_id=1, source_target_pairs={{0,6},{1,7},{2,0},{3,1},{4,2},{5,3},{6,4},{7,5},{8,14},{9,15},{10,... | collective-permute-start | bytes 811016 | tf_op jit(solution)/shard_map/ppermute | solution.py:369
  22.9 8.7 %collective-permute-start.4 = (f16[528,256]{1,0:T(8,128)(2,1)S(1)}, f16[528,256]{1,0:T(8,128)(2,1)S(1)}, u32[]{:S(2)}, u32[]{:S(2)}) collective-permute-start(f16[528,256]{1,0:T(8,128)(2,1)S(1)} %convert_element_type.65), channel_id=1, source_target_pairs={{0,2},{1,3},{2,4},{3,5},{4,6},{5,7},{6,0},{7,1},{8,10},{9,11},{10,... | collective-permute-start | bytes 811016 | tf_op jit(solution)/shard_map/ppermute | solution.py:369
  32.8 27.2 %collective-permute-start.16 = (bf16[2,256,512]{2,1,0:T(8,128)(2,1)S(1)}, bf16[2,256,512]{2,1,0:T(8,128)(2,1)S(1)}, u32[]{:S(2)}, u32[]{:S(2)}) collective-permute-start(bf16[2,256,512]{2,1,0:T(8,128)(2,1)S(1)} %get-tuple-element.51.refs_2_), channel_id=1, source_target_pairs={{0,6},{1,7},{2,0},{3,1},{4,2},{5,3},{6,4},{7,5},{8,14},{9,15},{10,... | collective-permute-start | bytes 1572872 | tf_op jit(solution)/shard_map/ppermute | solution.py:369
  33.4 26.6 %collective-permute-start.15 = (bf16[2,256,512]{2,1,0:T(8,128)(2,1)S(1)}, bf16[2,256,512]{2,1,0:T(8,128)(2,1)S(1)}, u32[]{:S(2)}, u32[]{:S(2)}) collective-permute-start(bf16[2,256,512]{2,1,0:T(8,128)(2,1)S(1)} %get-tuple-element.51.refs_2_), channel_id=1, source_target_pairs={{0,2},{1,3},{2,4},{3,5},{4,6},{5,7},{6,0},{7,1},{8,10},{9,11},{10,... | collective-permute-start | bytes 1572872 | tf_op jit(solution)/shard_map/ppermute | solution.py:369
  36.3 5.5 %collective-permute-start.9 = (f32[32,256]{1,0:T(8,128)S(1)}, f32[32,256]{1,0:T(8,128)S(1)}, u32[]{:S(2)}, u32[]{:S(2)}) collective-permute-start(f32[32,256]{1,0:T(8,128)S(1)} %get-tuple-element.66), channel_id=1, source_target_pairs={{0,16},{8,24},{16,0},{24,8},{32,48},{40,56},{48,32},{56,40},{64,80... | collective-permute-start | bytes 98312 | tf_op jit(solution)/shard_map/ppermute | solution.py:373
  40.6 5.1 %collective-permute-start.10 = (f32[32,256]{1,0:T(8,128)S(1)}, f32[32,256]{1,0:T(8,128)S(1)}, u32[]{:S(2)}, u32[]{:S(2)}) collective-permute-start(f32[32,256]{1,0:T(8,128)S(1)} %get-tuple-element.68), channel_id=1, source_target_pairs={{0,8},{8,16},{16,24},{24,0},{32,40},{40,48},{48,56},{56,32},{64,72... | collective-permute-start | bytes 98312 | tf_op jit(solution)/shard_map/ppermute | solution.py:373
  45.7 10.2 %collective-permute-start.14 = (f32[32,256]{1,0:T(8,128)S(1)}, f32[32,256]{1,0:T(8,128)S(1)}, u32[]{:S(2)}, u32[]{:S(2)}) collective-permute-start(f32[32,256]{1,0:T(8,128)S(1)} %add_add_fusion.2), channel_id=1, source_target_pairs={{0,192},{8,200},{16,208},{24,216},{32,224},{40,232},{48,240},{56,2... | collective-permute-start | bytes 98312 | tf_op jit(solution)/shard_map/ppermute | solution.py:379
  52.1 6.0 %collective-permute-start.13 = (f32[32,256]{1,0:T(8,128)S(1)}, f32[32,256]{1,0:T(8,128)S(1)}, u32[]{:S(2)}, u32[]{:S(2)}) collective-permute-start(f32[32,256]{1,0:T(8,128)S(1)} %add_add_fusion.2), channel_id=1, source_target_pairs={{0,64},{8,72},{16,80},{24,88},{32,96},{40,104},{48,112},{56,120},{... | collective-permute-start | bytes 98312 | tf_op jit(solution)/shard_map/ppermute | solution.py:379
  52.1 7.8 %collective-permute-start.12 = (f32[32,256]{1,0:T(8,128)S(1)}, f32[32,256]{1,0:T(8,128)S(1)}, u32[]{:S(2)}, u32[]{:S(2)}) collective-permute-start(f32[32,256]{1,0:T(8,128)S(1)} %add_add_fusion.2), channel_id=1, source_target_pairs={{0,128},{8,136},{16,144},{24,152},{32,160},{40,168},{48,176},{56,1... | collective-permute-start | bytes 98312 | tf_op jit(solution)/shard_map/ppermute | solution.py:379
  61.1 12.1 %collective-permute-start.22 = (bf16[256,512]{1,0:T(8,128)(2,1)S(1)}, bf16[256,512]{1,0:T(8,128)(2,1)S(1)}, u32[]{:S(2)}, u32[]{:S(2)}) collective-permute-start(bf16[256,512]{1,0:T(8,128)(2,1)S(1)} %slice_bitcast_fusion), channel_id=1, source_target_pairs={{0,6},{1,7},{2,0},{3,1},{4,2},{5,3},{6,4},{7,5},{8,14},{9,15},{10,... | collective-permute-start | bytes 786440 | tf_op jit(solution)/shard_map/ppermute | solution.py:369
  61.2 12.0 %collective-permute-start.21 = (bf16[256,512]{1,0:T(8,128)(2,1)S(1)}, bf16[256,512]{1,0:T(8,128)(2,1)S(1)}, u32[]{:S(2)}, u32[]{:S(2)}) collective-permute-start(bf16[256,512]{1,0:T(8,128)(2,1)S(1)} %slice_bitcast_fusion.1), channel_id=1, source_target_pairs={{0,2},{1,3},{2,4},{3,5},{4,6},{5,7},{6,0},{7,1},{8,10},{9,11},{10,... | collective-permute-start | bytes 786440 | tf_op jit(solution)/shard_map/ppermute | solution.py:369
  64.4 5.2 %collective-permute-start.20 = (f32[32,256]{1,0:T(8,128)S(1)}, f32[32,256]{1,0:T(8,128)S(1)}, u32[]{:S(2)}, u32[]{:S(2)}) collective-permute-start(f32[32,256]{1,0:T(8,128)S(1)} %add.105), channel_id=1, source_target_pairs={{0,6},{1,7},{2,0},{3,1},{4,2},{5,3},{6,4},{7,5},{8,14},{9,15},{10,... | collective-permute-start | bytes 98312 | tf_op jit(solution)/shard_map/ppermute | solution.py:369
  64.5 5.1 %collective-permute-start.19 = (f32[32,256]{1,0:T(8,128)S(1)}, f32[32,256]{1,0:T(8,128)S(1)}, u32[]{:S(2)}, u32[]{:S(2)}) collective-permute-start(f32[32,256]{1,0:T(8,128)S(1)} %add.105), channel_id=1, source_target_pairs={{0,2},{1,3},{2,4},{3,5},{4,6},{5,7},{6,0},{7,1},{8,10},{9,11},{10,... | collective-permute-start | bytes 98312 | tf_op jit(solution)/shard_map/ppermute | solution.py:369
  67.8 5.4 %collective-permute-start.18 = (f32[32,256]{1,0:T(8,128)S(1)}, f32[32,256]{1,0:T(8,128)S(1)}, u32[]{:S(2)}, u32[]{:S(2)}) collective-permute-start(f32[32,256]{1,0:T(8,128)S(1)} %add.105), channel_id=1, source_target_pairs={{0,4},{1,5},{2,6},{3,7},{4,0},{5,1},{6,2},{7,3},{8,12},{9,13},{10,... | collective-permute-start | bytes 98312 | tf_op jit(solution)/shard_map/ppermute | solution.py:369
  69.6 10.0 %collective-permute-start.27 = (bf16[2,256,512]{2,1,0:T(8,128)(2,1)S(1)}, bf16[2,256,512]{2,1,0:T(8,128)(2,1)S(1)}, u32[]{:S(2)}, u32[]{:S(2)}) collective-permute-start(bf16[2,256,512]{2,1,0:T(8,128)(2,1)S(1)} %get-tuple-element.51.refs_2_), channel_id=1, source_target_pairs={{0,1},{1,0},{2,3},{3,2},{4,5},{5,4},{6,7},{7,6},{8,9},{9,8},{10,11... | collective-permute-start | bytes 1572872 | tf_op jit(solution)/shard_map/ppermute | solution.py:365
  73.2 5.2 %collective-permute-start.25 = (f32[32,256]{1,0:T(8,128)S(1)}, f32[32,256]{1,0:T(8,128)S(1)}, u32[]{:S(2)}, u32[]{:S(2)}) collective-permute-start(f32[32,256]{1,0:T(8,128)S(1)} %add_add_fusion), channel_id=1, source_target_pairs={{0,8},{8,16},{16,24},{24,0},{32,40},{40,48},{48,56},{56,32},{64,72... | collective-permute-start | bytes 98312 | tf_op jit(solution)/shard_map/ppermute | solution.py:373
  73.3 5.5 %collective-permute-start.24 = (f32[32,256]{1,0:T(8,128)S(1)}, f32[32,256]{1,0:T(8,128)S(1)}, u32[]{:S(2)}, u32[]{:S(2)}) collective-permute-start(f32[32,256]{1,0:T(8,128)S(1)} %add_add_fusion), channel_id=1, source_target_pairs={{0,16},{8,24},{16,0},{24,8},{32,48},{40,56},{48,32},{56,40},{64,80... | collective-permute-start | bytes 98312 | tf_op jit(solution)/shard_map/ppermute | solution.py:373
  74.8 4.9 %collective-permute-start.23 = (f32[32,256]{1,0:T(8,128)S(1)}, f32[32,256]{1,0:T(8,128)S(1)}, u32[]{:S(2)}, u32[]{:S(2)}) collective-permute-start(f32[32,256]{1,0:T(8,128)S(1)} %add_add_fusion), channel_id=1, source_target_pairs={{0,24},{8,0},{16,8},{24,16},{32,56},{40,32},{48,40},{56,48},{64,88... | collective-permute-start | bytes 98312 | tf_op jit(solution)/shard_map/ppermute | solution.py:373
  76.5 4.8 %collective-permute-start.28 = (bf16[2,256,512]{2,1,0:T(8,128)(2,1)S(1)}, bf16[2,256,512]{2,1,0:T(8,128)(2,1)S(1)}, u32[]{:S(2)}, u32[]{:S(2)}) collective-permute-start(bf16[2,256,512]{2,1,0:T(8,128)(2,1)S(1)} %collective-permute-done.15.refs_3_), channel_id=1, source_target_pairs={{0,1},{1,0},{2,3},{3,2},{4,5},{5,4},{6,7},{7,6},{8,9},{9,8},{10,11... | collective-permute-start | bytes 1572872 | tf_op jit(solution)/shard_map/ppermute | solution.py:365
  (8 other events, 24.5 us)

commit v5 on v4

--- a/solution.py
+++ b/solution.py
@@ -380,7 +380,10 @@
 
 
 def sum_of_four(x, shift, step=1):
-    return (x + shift(x, 2 * step)) + (shift(x, step) + shift(x, -step))
+    far, up, down = lax.optimization_barrier(
+        (shift(x, 2 * step), shift(x, step), shift(x, -step))
+    )
+    return (x + far) + (up + down)
 
 
 def block_of(x, index, size):

time: 120 us -> 120 us (level)
  no operation moved by 1% of the time
where the time goes in v5:
time: 120 us
  starting transfers between devices  40.4 us (34%)
  waiting for transfers between devices  28.1 us (23%)
  Pallas kernels  24.3 us (20%)
  blocking collectives  23.6 us (20%)
  other arithmetic  2.07 us (2%)
    all_to_all x1, blocking collectives, shards(): lax.all_to_all(value.astype(f16), 'rows', 0, 0, tiled=True)  23.6 us
    ppermute x13, starting transfers between devices, shift_y(): return lax.ppermute(x, 'width', [(i, (i + 2 * k) % 8) for i in range(8)])  19.1 us
    ppermute x13, waiting for transfers between devices, shift_y(): return lax.ppermute(x, 'width', [(i, (i + 2 * k) % 8) for i in range(8)])  15.8 us
    pallas_call x1, Pallas kernels, factor_and_project(): pl.pallas_call(functools.partial(factor_kernel, b, n, total_rows), out_sh...  13.9 us
    ppermute x3, starting transfers between devices, shift_z(): return lax.ppermute(x, 'rows', [(i, (i + 4 * k) % 32) for i in range(32)])  10.2 us
    ppermute x6, starting transfers between devices, shift_x(): lax.ppermute(x, 'rows', [(i, i // 4 * 4 + (i % 4 + k) % 4) for i in range...  8.44 us
    ppermute x6, waiting for transfers between devices, shift_x(): lax.ppermute(x, 'rows', [(i, i // 4 * 4 + (i % 4 + k) % 4) for i in range...  7.2 us
    pallas_call x2, Pallas kernels, load_and_sketch(): pl.pallas_call(functools.partial(load_kernel, pieces), out_shape=out_shap...  7.05 us
  transfers between devices with their start and end apart: 32, of which 15 were waited for; matrix products, arithmetic and copies ran while one was open for 1% of the time, Pallas kernels for 5%

profile of v5, /device:TPU:24, one launch (start us, length us, event | category | flops | bytes accessed | tf_op | source)
XLA Modules:
  0.0 119.9 jit_solution(2922290651396027521)
XLA Ops:
  0.7 3.6 %shard_map.41 = (bf16[4096,640]{1,0:T(8,128)(2,1)S(1)}, f32[2112,256]{1,0:T(8,128)S(1)}, bf16[640,256]{1,0:T(8,128)(2,1)S(1)}) custom-call(s32[3]{0:T(128)S(1)} %pad_add_fusion.place_ref, bf16[8192,640]{1,0:T(8,128)(2,1)} %slab_ref.5, bf16[640,256]{1,0:T(8,128)(2,1)} %basis_ref.1), custom_call_target="tpu_custom_call" | custom-call | flops 671088640 | bytes 7340032 | tf_op jit(solution)/shard_map/pallas_call | solution.py:142
  4.6 3.5 %shard_map.42 = (bf16[4096,640]{1,0:T(8,128)(2,1)S(1)}, f32[2112,256]{1,0:T(8,128)S(1)}) custom-call(s32[3]{0:T(128)S(1)} %pad_add_fusion.place_ref, bf16[8192,640]{1,0:T(8,128)(2,1)} %slab_ref.5, bf16[640,256]{1,0:T(8,128)(2,1)S(1)} %get-tuple-element.39.basis_ref), custom_call_target="tpu_custom_call" | custom-call | flops 671088640 | bytes 7340032 | tf_op jit(solution)/shard_map/pallas_call | solution.py:142
  11.2 2.6 %collective-permute-start.2 = (f16[528,256]{1,0:T(8,128)(2,1)S(1)}, f16[528,256]{1,0:T(8,128)(2,1)S(1)}, u32[]{:S(2)}, u32[]{:S(2)}) collective-permute-start(f16[528,256]{1,0:T(8,128)(2,1)S(1)} %convert_element_type.61), channel_id=1, source_target_pairs={{0,2},{1,3},{2,4},{3,5},{4,6},{5,7},{6,0},{7,1},{8,10},{9,11},{10,... | collective-permute-start | bytes 811016 | tf_op jit(solution)/shard_map/ppermute | solution.py:369
  14.7 1.3 %collective-permute-start.5 = (f16[528,256]{1,0:T(8,128)(2,1)S(1)}, f16[528,256]{1,0:T(8,128)(2,1)S(1)}, u32[]{:S(2)}, u32[]{:S(2)}) collective-permute-start(f16[528,256]{1,0:T(8,128)(2,1)S(1)} %convert_element_type.67), channel_id=1, source_target_pairs={{0,6},{1,7},{2,0},{3,1},{4,2},{5,3},{6,4},{7,5},{8,14},{9,15},{10,... | collective-permute-start | bytes 811016 | tf_op jit(solution)/shard_map/ppermute | solution.py:369
  16.0 5.0 %collective-permute-done.3 = f16[528,256]{1,0:T(8,128)(2,1)S(1)} collective-permute-done((f16[528,256]{1,0:T(8,128)(2,1)S(1)}, f16[528,256]{1,0:T(8,128)(2,1)S(1)}, u32[]{:S(2)}, u32[]{:S(2)}) %collective-permute-start.3) | collective-permute-done | bytes 270368 | tf_op jit(solution)/shard_map/ppermute | solution.py:369
  22.9 3.2 %collective-permute-start.4 = (f16[528,256]{1,0:T(8,128)(2,1)S(1)}, f16[528,256]{1,0:T(8,128)(2,1)S(1)}, u32[]{:S(2)}, u32[]{:S(2)}) collective-permute-start(f16[528,256]{1,0:T(8,128)(2,1)S(1)} %convert_element_type.65), channel_id=1, source_target_pairs={{0,2},{1,3},{2,4},{3,5},{4,6},{5,7},{6,0},{7,1},{8,10},{9,11},{10,... | collective-permute-start | bytes 811016 | tf_op jit(solution)/shard_map/ppermute | solution.py:369
  26.8 4.8 %collective-permute-done.7 = f16[528,256]{1,0:T(8,128)(2,1)S(1)} collective-permute-done((f16[528,256]{1,0:T(8,128)(2,1)S(1)}, f16[528,256]{1,0:T(8,128)(2,1)S(1)}, u32[]{:S(2)}, u32[]{:S(2)}) %collective-permute-start.7) | collective-permute-done | bytes 270368 | tf_op jit(solution)/shard_map/ppermute | solution.py:369
  33.4 2.9 %collective-permute-start.15 = (bf16[2,256,512]{2,1,0:T(8,128)(2,1)S(1)}, bf16[2,256,512]{2,1,0:T(8,128)(2,1)S(1)}, u32[]{:S(2)}, u32[]{:S(2)}) collective-permute-start(bf16[2,256,512]{2,1,0:T(8,128)(2,1)S(1)} %get-tuple-element.60.refs_2_), channel_id=1, source_target_pairs={{0,2},{1,3},{2,4},{3,5},{4,6},{5,7},{6,0},{7,1},{8,10},{9,11},{10,... | collective-permute-start | bytes 1572872 | tf_op jit(solution)/shard_map/ppermute | solution.py:369
  36.3 3.1 %collective-permute-start.9 = (f32[32,256]{1,0:T(8,128)S(1)}, f32[32,256]{1,0:T(8,128)S(1)}, u32[]{:S(2)}, u32[]{:S(2)}) collective-permute-start(f32[32,256]{1,0:T(8,128)S(1)} %get-tuple-element.78), channel_id=1, source_target_pairs={{0,16},{8,24},{16,0},{24,8},{32,48},{40,56},{48,32},{56,40},{64,80... | collective-permute-start | bytes 98312 | tf_op jit(solution)/shard_map/ppermute | solution.py:373
  41.8 1.5 %collective-permute-done.11 = f32[32,256]{1,0:T(8,128)S(1)} collective-permute-done((f32[32,256]{1,0:T(8,128)S(1)}, f32[32,256]{1,0:T(8,128)S(1)}, u32[]{:S(2)}, u32[]{:S(2)}) %collective-permute-start.11) | collective-permute-done | bytes 32800 | tf_op jit(solution)/shard_map/ppermute | solution.py:373
  43.4 2.4 %collective-permute-done.10 = f32[32,256]{1,0:T(8,128)S(1)} collective-permute-done((f32[32,256]{1,0:T(8,128)S(1)}, f32[32,256]{1,0:T(8,128)S(1)}, u32[]{:S(2)}, u32[]{:S(2)}) %collective-permute-start.10) | collective-permute-done | bytes 32800 | tf_op jit(solution)/shard_map/ppermute | solution.py:373
  45.7 6.4 %collective-permute-start.14 = (f32[32,256]{1,0:T(8,128)S(1)}, f32[32,256]{1,0:T(8,128)S(1)}, u32[]{:S(2)}, u32[]{:S(2)}) collective-permute-start(f32[32,256]{1,0:T(8,128)S(1)} %add_add_fusion.2), channel_id=1, source_target_pairs={{0,192},{8,200},{16,208},{24,216},{32,224},{40,232},{48,240},{56,2... | collective-permute-start | bytes 98312 | tf_op jit(solution)/shard_map/ppermute | solution.py:379
  52.1 3.8 %collective-permute-start.12 = (f32[32,256]{1,0:T(8,128)S(1)}, f32[32,256]{1,0:T(8,128)S(1)}, u32[]{:S(2)}, u32[]{:S(2)}) collective-permute-start(f32[32,256]{1,0:T(8,128)S(1)} %add_add_fusion.2), channel_id=1, source_target_pairs={{0,128},{8,136},{16,144},{24,152},{32,160},{40,168},{48,176},{56,1... | collective-permute-start | bytes 98312 | tf_op jit(solution)/shard_map/ppermute | solution.py:379
  55.9 2.2 %collective-permute-done.13 = f32[32,256]{1,0:T(8,128)S(1)} collective-permute-done((f32[32,256]{1,0:T(8,128)S(1)}, f32[32,256]{1,0:T(8,128)S(1)}, u32[]{:S(2)}, u32[]{:S(2)}) %collective-permute-start.13) | collective-permute-done | bytes 32800 | tf_op jit(solution)/shard_map/ppermute | solution.py:379
  58.1 1.8 %collective-permute-done.12 = f32[32,256]{1,0:T(8,128)S(1)} collective-permute-done((f32[32,256]{1,0:T(8,128)S(1)}, f32[32,256]{1,0:T(8,128)S(1)}, u32[]{:S(2)}, u32[]{:S(2)}) %collective-permute-start.12) | collective-permute-done | bytes 32800 | tf_op jit(solution)/shard_map/ppermute | solution.py:379
  61.2 3.2 %collective-permute-start.21 = (bf16[256,512]{1,0:T(8,128)(2,1)S(1)}, bf16[256,512]{1,0:T(8,128)(2,1)S(1)}, u32[]{:S(2)}, u32[]{:S(2)}) collective-permute-start(bf16[256,512]{1,0:T(8,128)(2,1)S(1)} %slice_bitcast_fusion.1), channel_id=1, source_target_pairs={{0,2},{1,3},{2,4},{3,5},{4,6},{5,7},{6,0},{7,1},{8,10},{9,11},{10,... | collective-permute-start | bytes 786440 | tf_op jit(solution)/shard_map/ppermute | solution.py:369
  64.5 3.2 %collective-permute-start.19 = (f32[32,256]{1,0:T(8,128)S(1)}, f32[32,256]{1,0:T(8,128)S(1)}, u32[]{:S(2)}, u32[]{:S(2)}) collective-permute-start(f32[32,256]{1,0:T(8,128)S(1)} %add.105), channel_id=1, source_target_pairs={{0,2},{1,3},{2,4},{3,5},{4,6},{5,7},{6,0},{7,1},{8,10},{9,11},{10,... | collective-permute-start | bytes 98312 | tf_op jit(solution)/shard_map/ppermute | solution.py:369
  67.8 1.9 %collective-permute-done.20 = f32[32,256]{1,0:T(8,128)S(1)} collective-permute-done((f32[32,256]{1,0:T(8,128)S(1)}, f32[32,256]{1,0:T(8,128)S(1)}, u32[]{:S(2)}, u32[]{:S(2)}) %collective-permute-start.20) | collective-permute-done | bytes 32800 | tf_op jit(solution)/shard_map/ppermute | solution.py:369
  69.6 3.5 %collective-permute-done.18 = f32[32,256]{1,0:T(8,128)S(1)} collective-permute-done((f32[32,256]{1,0:T(8,128)S(1)}, f32[32,256]{1,0:T(8,128)S(1)}, u32[]{:S(2)}, u32[]{:S(2)}) %collective-permute-start.18) | collective-permute-done | bytes 32800 | tf_op jit(solution)/shard_map/ppermute | solution.py:369
  73.3 1.5 %collective-permute-start.24 = (f32[32,256]{1,0:T(8,128)S(1)}, f32[32,256]{1,0:T(8,128)S(1)}, u32[]{:S(2)}, u32[]{:S(2)}) collective-permute-start(f32[32,256]{1,0:T(8,128)S(1)} %add_add_fusion), channel_id=1, source_target_pairs={{0,16},{8,24},{16,0},{24,8},{32,48},{40,56},{48,32},{56,40},{64,80... | collective-permute-start | bytes 98312 | tf_op jit(solution)/shard_map/ppermute | solution.py:373
  74.8 1.8 %collective-permute-start.23 = (f32[32,256]{1,0:T(8,128)S(1)}, f32[32,256]{1,0:T(8,128)S(1)}, u32[]{:S(2)}, u32[]{:S(2)}) collective-permute-start(f32[32,256]{1,0:T(8,128)S(1)} %add_add_fusion), channel_id=1, source_target_pairs={{0,24},{8,0},{16,8},{24,16},{32,56},{40,32},{48,40},{56,48},{64,88... | collective-permute-start | bytes 98312 | tf_op jit(solution)/shard_map/ppermute | solution.py:373
  76.5 1.9 %collective-permute-done.25 = f32[32,256]{1,0:T(8,128)S(1)} collective-permute-done((f32[32,256]{1,0:T(8,128)S(1)}, f32[32,256]{1,0:T(8,128)S(1)}, u32[]{:S(2)}, u32[]{:S(2)}) %collective-permute-start.25) | collective-permute-done | bytes 32800 | tf_op jit(solution)/shard_map/ppermute | solution.py:373
  81.4 13.9 %shard_map.47 = (f32[256,256]{1,0:T(8,128)}, f32[256,768]{1,0:T(8,128)S(1)}) custom-call(s32[3]{0:T(128)S(1)} %pad_add_fusion.place_ref, bf16[8192,640]{1,0:T(8,128)(2,1)} %slab_ref.5, f32[128,256]{1,0:T(8,128)S(1)} %constant_dynamic-update-slice_fusion.refs_0_, f32[128,256]{1,0:T(8,128)S(1)} %collective-permute-done.26.refs_1_, ...), custom_call_target="tpu_custom_call" | custom-call | flops 2885681152 | bytes 15466496 | tf_op jit(solution)/shard_map/pallas_call | solution.py:337
  95.3 23.6 %all_to_all.9 = f16[32,8,768]{2,1,0:T(8,128)(2,1)S(1)} all-to-all(f16[32,8,768]{2,1,0:T(8,128)(2,1)S(1)} %convert_bitcast_fusion), channel_id=1, replica_groups=mesh['rows'=32,'width'=8] {'rows'}, dimensions={0} | all-to-all | bytes 786432 | tf_op jit(solution)/shard_map/all_to_all | solution.py:448
  (84 shorter events, 16.3 us)
Async XLA Ops:
  8.3 12.8 %collective-permute-start.1 = (f16[2112,256]{1,0:T(8,128)(2,1)S(1)}, f16[2112,256]{1,0:T(8,128)(2,1)S(1)}, u32[]{:S(2)}, u32[]{:S(2)}) collective-permute-start(f16[2112,256]{1,0:T(8,128)(2,1)S(1)} %convert_element_type.58), channel_id=1, source_target_pairs={{0,1},{1,0},{2,3},{3,2},{4,5},{5,4},{6,7},{7,6},{8,9},{9,8},{10,11... | collective-permute-start | bytes 3244040 | tf_op jit(solution)/shard_map/ppermute | solution.py:365
  10.3 10.6 %collective-permute-start.3 = (f16[528,256]{1,0:T(8,128)(2,1)S(1)}, f16[528,256]{1,0:T(8,128)(2,1)S(1)}, u32[]{:S(2)}, u32[]{:S(2)}) collective-permute-start(f16[528,256]{1,0:T(8,128)(2,1)S(1)} %convert_element_type.63), channel_id=1, source_target_pairs={{0,6},{1,7},{2,0},{3,1},{4,2},{5,3},{6,4},{7,5},{8,14},{9,15},{10,... | collective-permute-start | bytes 811016 | tf_op jit(solution)/shard_map/ppermute | solution.py:369
  11.2 9.8 %collective-permute-start.2 = (f16[528,256]{1,0:T(8,128)(2,1)S(1)}, f16[528,256]{1,0:T(8,128)(2,1)S(1)}, u32[]{:S(2)}, u32[]{:S(2)}) collective-permute-start(f16[528,256]{1,0:T(8,128)(2,1)S(1)} %convert_element_type.61), channel_id=1, source_target_pairs={{0,2},{1,3},{2,4},{3,5},{4,6},{5,7},{6,0},{7,1},{8,10},{9,11},{10,... | collective-permute-start | bytes 811016 | tf_op jit(solution)/shard_map/ppermute | solution.py:369
  13.9 12.6 %collective-permute-start.6 = (f16[528,256]{1,0:T(8,128)(2,1)S(1)}, f16[528,256]{1,0:T(8,128)(2,1)S(1)}, u32[]{:S(2)}, u32[]{:S(2)}) collective-permute-start(f16[528,256]{1,0:T(8,128)(2,1)S(1)} %convert_element_type.69), channel_id=1, source_target_pairs={{0,2},{1,3},{2,4},{3,5},{4,6},{5,7},{6,0},{7,1},{8,10},{9,11},{10,... | collective-permute-start | bytes 811016 | tf_op jit(solution)/shard_map/ppermute | solution.py:369
  14.7 12.1 %collective-permute-start.5 = (f16[528,256]{1,0:T(8,128)(2,1)S(1)}, f16[528,256]{1,0:T(8,128)(2,1)S(1)}, u32[]{:S(2)}, u32[]{:S(2)}) collective-permute-start(f16[528,256]{1,0:T(8,128)(2,1)S(1)} %convert_element_type.67), channel_id=1, source_target_pairs={{0,6},{1,7},{2,0},{3,1},{4,2},{5,3},{6,4},{7,5},{8,14},{9,15},{10,... | collective-permute-start | bytes 811016 | tf_op jit(solution)/shard_map/ppermute | solution.py:369
  22.6 9.0 %collective-permute-start.7 = (f16[528,256]{1,0:T(8,128)(2,1)S(1)}, f16[528,256]{1,0:T(8,128)(2,1)S(1)}, u32[]{:S(2)}, u32[]{:S(2)}) collective-permute-start(f16[528,256]{1,0:T(8,128)(2,1)S(1)} %convert_element_type.71), channel_id=1, source_target_pairs={{0,6},{1,7},{2,0},{3,1},{4,2},{5,3},{6,4},{7,5},{8,14},{9,15},{10,... | collective-permute-start | bytes 811016 | tf_op jit(solution)/shard_map/ppermute | solution.py:369
  22.9 8.7 %collective-permute-start.4 = (f16[528,256]{1,0:T(8,128)(2,1)S(1)}, f16[528,256]{1,0:T(8,128)(2,1)S(1)}, u32[]{:S(2)}, u32[]{:S(2)}) collective-permute-start(f16[528,256]{1,0:T(8,128)(2,1)S(1)} %convert_element_type.65), channel_id=1, source_target_pairs={{0,2},{1,3},{2,4},{3,5},{4,6},{5,7},{6,0},{7,1},{8,10},{9,11},{10,... | collective-permute-start | bytes 811016 | tf_op jit(solution)/shard_map/ppermute | solution.py:369
  32.8 27.2 %collective-permute-start.16 = (bf16[2,256,512]{2,1,0:T(8,128)(2,1)S(1)}, bf16[2,256,512]{2,1,0:T(8,128)(2,1)S(1)}, u32[]{:S(2)}, u32[]{:S(2)}) collective-permute-start(bf16[2,256,512]{2,1,0:T(8,128)(2,1)S(1)} %get-tuple-element.60.refs_2_), channel_id=1, source_target_pairs={{0,6},{1,7},{2,0},{3,1},{4,2},{5,3},{6,4},{7,5},{8,14},{9,15},{10,... | collective-permute-start | bytes 1572872 | tf_op jit(solution)/shard_map/ppermute | solution.py:369
  33.4 26.6 %collective-permute-start.15 = (bf16[2,256,512]{2,1,0:T(8,128)(2,1)S(1)}, bf16[2,256,512]{2,1,0:T(8,128)(2,1)S(1)}, u32[]{:S(2)}, u32[]{:S(2)}) collective-permute-start(bf16[2,256,512]{2,1,0:T(8,128)(2,1)S(1)} %get-tuple-element.60.refs_2_), channel_id=1, source_target_pairs={{0,2},{1,3},{2,4},{3,5},{4,6},{5,7},{6,0},{7,1},{8,10},{9,11},{10,... | collective-permute-start | bytes 1572872 | tf_op jit(solution)/shard_map/ppermute | solution.py:369
  36.3 5.5 %collective-permute-start.9 = (f32[32,256]{1,0:T(8,128)S(1)}, f32[32,256]{1,0:T(8,128)S(1)}, u32[]{:S(2)}, u32[]{:S(2)}) collective-permute-start(f32[32,256]{1,0:T(8,128)S(1)} %get-tuple-element.78), channel_id=1, source_target_pairs={{0,16},{8,24},{16,0},{24,8},{32,48},{40,56},{48,32},{56,40},{64,80... | collective-permute-start | bytes 98312 | tf_op jit(solution)/shard_map/ppermute | solution.py:373
  40.6 5.1 %collective-permute-start.10 = (f32[32,256]{1,0:T(8,128)S(1)}, f32[32,256]{1,0:T(8,128)S(1)}, u32[]{:S(2)}, u32[]{:S(2)}) collective-permute-start(f32[32,256]{1,0:T(8,128)S(1)} %get-tuple-element.80), channel_id=1, source_target_pairs={{0,8},{8,16},{16,24},{24,0},{32,40},{40,48},{48,56},{56,32},{64,72... | collective-permute-start | bytes 98312 | tf_op jit(solution)/shard_map/ppermute | solution.py:373
  45.7 10.2 %collective-permute-start.14 = (f32[32,256]{1,0:T(8,128)S(1)}, f32[32,256]{1,0:T(8,128)S(1)}, u32[]{:S(2)}, u32[]{:S(2)}) collective-permute-start(f32[32,256]{1,0:T(8,128)S(1)} %add_add_fusion.2), channel_id=1, source_target_pairs={{0,192},{8,200},{16,208},{24,216},{32,224},{40,232},{48,240},{56,2... | collective-permute-start | bytes 98312 | tf_op jit(solution)/shard_map/ppermute | solution.py:379
  52.1 6.0 %collective-permute-start.13 = (f32[32,256]{1,0:T(8,128)S(1)}, f32[32,256]{1,0:T(8,128)S(1)}, u32[]{:S(2)}, u32[]{:S(2)}) collective-permute-start(f32[32,256]{1,0:T(8,128)S(1)} %add_add_fusion.2), channel_id=1, source_target_pairs={{0,64},{8,72},{16,80},{24,88},{32,96},{40,104},{48,112},{56,120},{... | collective-permute-start | bytes 98312 | tf_op jit(solution)/shard_map/ppermute | solution.py:379
  52.1 7.8 %collective-permute-start.12 = (f32[32,256]{1,0:T(8,128)S(1)}, f32[32,256]{1,0:T(8,128)S(1)}, u32[]{:S(2)}, u32[]{:S(2)}) collective-permute-start(f32[32,256]{1,0:T(8,128)S(1)} %add_add_fusion.2), channel_id=1, source_target_pairs={{0,128},{8,136},{16,144},{24,152},{32,160},{40,168},{48,176},{56,1... | collective-permute-start | bytes 98312 | tf_op jit(solution)/shard_map/ppermute | solution.py:379
  61.1 12.1 %collective-permute-start.22 = (bf16[256,512]{1,0:T(8,128)(2,1)S(1)}, bf16[256,512]{1,0:T(8,128)(2,1)S(1)}, u32[]{:S(2)}, u32[]{:S(2)}) collective-permute-start(bf16[256,512]{1,0:T(8,128)(2,1)S(1)} %slice_bitcast_fusion), channel_id=1, source_target_pairs={{0,6},{1,7},{2,0},{3,1},{4,2},{5,3},{6,4},{7,5},{8,14},{9,15},{10,... | collective-permute-start | bytes 786440 | tf_op jit(solution)/shard_map/ppermute | solution.py:369
  61.2 12.0 %collective-permute-start.21 = (bf16[256,512]{1,0:T(8,128)(2,1)S(1)}, bf16[256,512]{1,0:T(8,128)(2,1)S(1)}, u32[]{:S(2)}, u32[]{:S(2)}) collective-permute-start(bf16[256,512]{1,0:T(8,128)(2,1)S(1)} %slice_bitcast_fusion.1), channel_id=1, source_target_pairs={{0,2},{1,3},{2,4},{3,5},{4,6},{5,7},{6,0},{7,1},{8,10},{9,11},{10,... | collective-permute-start | bytes 786440 | tf_op jit(solution)/shard_map/ppermute | solution.py:369
  64.4 5.2 %collective-permute-start.20 = (f32[32,256]{1,0:T(8,128)S(1)}, f32[32,256]{1,0:T(8,128)S(1)}, u32[]{:S(2)}, u32[]{:S(2)}) collective-permute-start(f32[32,256]{1,0:T(8,128)S(1)} %add.105), channel_id=1, source_target_pairs={{0,6},{1,7},{2,0},{3,1},{4,2},{5,3},{6,4},{7,5},{8,14},{9,15},{10,... | collective-permute-start | bytes 98312 | tf_op jit(solution)/shard_map/ppermute | solution.py:369
  64.5 5.1 %collective-permute-start.19 = (f32[32,256]{1,0:T(8,128)S(1)}, f32[32,256]{1,0:T(8,128)S(1)}, u32[]{:S(2)}, u32[]{:S(2)}) collective-permute-start(f32[32,256]{1,0:T(8,128)S(1)} %add.105), channel_id=1, source_target_pairs={{0,2},{1,3},{2,4},{3,5},{4,6},{5,7},{6,0},{7,1},{8,10},{9,11},{10,... | collective-permute-start | bytes 98312 | tf_op jit(solution)/shard_map/ppermute | solution.py:369
  67.8 5.4 %collective-permute-start.18 = (f32[32,256]{1,0:T(8,128)S(1)}, f32[32,256]{1,0:T(8,128)S(1)}, u32[]{:S(2)}, u32[]{:S(2)}) collective-permute-start(f32[32,256]{1,0:T(8,128)S(1)} %add.105), channel_id=1, source_target_pairs={{0,4},{1,5},{2,6},{3,7},{4,0},{5,1},{6,2},{7,3},{8,12},{9,13},{10,... | collective-permute-start | bytes 98312 | tf_op jit(solution)/shard_map/ppermute | solution.py:369
  69.6 10.0 %collective-permute-start.27 = (bf16[2,256,512]{2,1,0:T(8,128)(2,1)S(1)}, bf16[2,256,512]{2,1,0:T(8,128)(2,1)S(1)}, u32[]{:S(2)}, u32[]{:S(2)}) collective-permute-start(bf16[2,256,512]{2,1,0:T(8,128)(2,1)S(1)} %get-tuple-element.60.refs_2_), channel_id=1, source_target_pairs={{0,1},{1,0},{2,3},{3,2},{4,5},{5,4},{6,7},{7,6},{8,9},{9,8},{10,11... | collective-permute-start | bytes 1572872 | tf_op jit(solution)/shard_map/ppermute | solution.py:365
  73.2 5.2 %collective-permute-start.25 = (f32[32,256]{1,0:T(8,128)S(1)}, f32[32,256]{1,0:T(8,128)S(1)}, u32[]{:S(2)}, u32[]{:S(2)}) collective-permute-start(f32[32,256]{1,0:T(8,128)S(1)} %add_add_fusion), channel_id=1, source_target_pairs={{0,8},{8,16},{16,24},{24,0},{32,40},{40,48},{48,56},{56,32},{64,72... | collective-permute-start | bytes 98312 | tf_op jit(solution)/shard_map/ppermute | solution.py:373
  73.3 5.5 %collective-permute-start.24 = (f32[32,256]{1,0:T(8,128)S(1)}, f32[32,256]{1,0:T(8,128)S(1)}, u32[]{:S(2)}, u32[]{:S(2)}) collective-permute-start(f32[32,256]{1,0:T(8,128)S(1)} %add_add_fusion), channel_id=1, source_target_pairs={{0,16},{8,24},{16,0},{24,8},{32,48},{40,56},{48,32},{56,40},{64,80... | collective-permute-start | bytes 98312 | tf_op jit(solution)/shard_map/ppermute | solution.py:373
  74.8 4.9 %collective-permute-start.23 = (f32[32,256]{1,0:T(8,128)S(1)}, f32[32,256]{1,0:T(8,128)S(1)}, u32[]{:S(2)}, u32[]{:S(2)}) collective-permute-start(f32[32,256]{1,0:T(8,128)S(1)} %add_add_fusion), channel_id=1, source_target_pairs={{0,24},{8,0},{16,8},{24,16},{32,56},{40,32},{48,40},{56,48},{64,88... | collective-permute-start | bytes 98312 | tf_op jit(solution)/shard_map/ppermute | solution.py:373
  76.5 4.8 %collective-permute-start.28 = (bf16[2,256,512]{2,1,0:T(8,128)(2,1)S(1)}, bf16[2,256,512]{2,1,0:T(8,128)(2,1)S(1)}, u32[]{:S(2)}, u32[]{:S(2)}) collective-permute-start(bf16[2,256,512]{2,1,0:T(8,128)(2,1)S(1)} %collective-permute-done.15.refs_3_), channel_id=1, source_target_pairs={{0,1},{1,0},{2,3},{3,2},{4,5},{5,4},{6,7},{7,6},{8,9},{9,8},{10,11... | collective-permute-start | bytes 1572872 | tf_op jit(solution)/shard_map/ppermute | solution.py:365
  (8 other events, 24.5 us)
